TPU v7x, 256 devices: a whole 4x4x8 slice. The times are simulated.
256 devices in a mesh: src: 32 (over y, z), dst: 8 (over x, core).
Axes of the slice: x: 4, y: 4, z: 8, core: 2. Of those that a mesh axis runs over, the one named last changes fastest.
Arguments:
- features: bfloat16 [131072, 768], P(('dst', 'src')), may hold values from -300 to 300
- weight: bfloat16 [768, 256], replicated, may hold values from -0.21875 to 0.21875
- att_src: float32 [256], replicated, may hold values from -0.75 to 0.75
- att_dst: float32 [256], replicated, may hold values from -0.75 to 0.75
- bias: float32 [256], replicated, may hold values from -3 to 3
- block_pairs: int32 [32, 8, 32, 2], P('src', 'dst'), may hold values from 0 to 127, as said below
- edge_masks: int32 [32, 8, 32, 2, 128, 128], P('src', 'dst'), may hold values from 0 to 1, as said below
Outputs:
- output: float32 [131072, 256], P(('dst', 'src'))
Inputs may be any that keep to these rules, and one draw needn't show every extreme that they name: `block_pairs`: the 2 entries of one device and one owner are distinct. `edge_masks`: every row of every listed block holds at least one edge.
All inputs are finite; a program needn't handle non-finite values.
Results may differ from a plain program's by a relative error of at most 0.039.
Values may be sent and summed in bfloat16 or wider, within the bound.
No kernel may reach another device: no remote copies, remote signals or barrier semaphores. Data moves between devices by JAX's collectives and lax.ppermute only.
A program may use at most 128 MiB of HBM per device.

v0:
```python
import jax
import jax.numpy as jnp
from jax import lax
from jax.sharding import PartitionSpec as P

HEADS = 4
HEAD = 64
BLK = 128


lowest = -1e30


def leaky(values):
    return jnp.where(values > 0, values, 0.2 * values)


def head_scores(hidden, vector):
    flat = hidden.astype(jnp.float32).reshape(hidden.shape[0], HEADS, HEAD)
    return jnp.einsum("nkc,kc->kn", flat, vector.reshape(HEADS, HEAD))


def body(features, weight, att_src, att_dst, bias, block_pairs, edge_masks):
    hidden = jnp.dot(
        lax.all_gather(features, "dst", axis=0, tiled=True),
        weight,
        preferred_element_type=jnp.float32,
    ).astype(jnp.bfloat16)
    own_rows = features.shape[0]
    own_blocks = own_rows // BLK
    src_rows = hidden.shape[0]
    src_blocks = src_rows // BLK
    src_index = lax.axis_index("src")
    dst_index = lax.axis_index("dst")
    src_scores = head_scores(hidden, att_src)
    own_hidden = lax.dynamic_slice_in_dim(hidden, dst_index * own_rows, own_rows, 0)
    own_targets = head_scores(own_hidden, att_dst)
    own_sources = lax.dynamic_slice_in_dim(src_scores, dst_index * own_rows, own_rows, 1)
    every_target = lax.all_gather(own_targets, "src", axis=1, tiled=True)
    dst_blocks = every_target.shape[1] // BLK
    target_blocks = every_target.reshape(HEADS, dst_blocks, BLK).transpose(1, 0, 2)
    source_blocks = src_scores.reshape(HEADS, src_blocks, BLK).transpose(1, 0, 2)
    values = hidden.reshape(src_blocks, BLK, HEADS, HEAD)
    own_values = (
        own_hidden.astype(jnp.float32).reshape(own_blocks, BLK, HEADS, HEAD).transpose(0, 2, 3, 1)
    )
    self_logit = leaky(own_targets + own_sources).reshape(HEADS, own_blocks, BLK).transpose(1, 0, 2)
    per_owner = block_pairs.shape[-1]
    pairs = block_pairs.reshape(-1)
    masks = edge_masks.reshape(-1, BLK, BLK)
    slot_owner = jnp.arange(pairs.shape[0], dtype=jnp.int32) // per_owner
    place = pairs // src_blocks
    dst_pick = slot_owner * own_blocks + place
    src_pick = pairs % src_blocks
    logits = leaky(target_blocks[dst_pick][:, :, :, None] + source_blocks[src_pick][:, :, None, :])
    live = (masks > 0)[:, None]
    logits = jnp.where(live, logits, lowest)
    zero_index = jnp.int32(0)
    offset = src_index * own_blocks
    bound_start = lax.dynamic_update_slice(
        jnp.full((dst_blocks, HEADS, BLK), lowest, jnp.float32),
        self_logit,
        (offset, zero_index, zero_index),
    )
    total_start = lax.dynamic_update_slice(
        jnp.zeros((dst_blocks, HEADS, BLK), jnp.float32),
        jnp.ones_like(self_logit),
        (offset, zero_index, zero_index),
    )
    accum_start = lax.dynamic_update_slice(
        jnp.zeros((dst_blocks, HEADS, HEAD, BLK), jnp.float32),
        own_values,
        (offset, zero_index, zero_index, zero_index),
    )
    bound = bound_start.at[dst_pick].max(logits.max(-1))
    weights = jnp.where(live, jnp.exp(logits - bound[dst_pick][..., None]), 0.0)
    keep = jnp.exp(bound_start - bound)
    totals = (total_start * keep).at[dst_pick].add(weights.sum(-1))
    numer = jnp.einsum(
        "lkij,ljkc->lkci",
        weights.astype(jnp.bfloat16),
        values[src_pick],
        preferred_element_type=jnp.float32,
    )
    accum = (accum_start * keep[:, :, None, :]).at[dst_pick].add(numer)
    global_bound = lax.pmax(bound, "src")
    factor = jnp.exp(bound - global_bound)
    final_total, final_accum = (
        lax.psum_scatter(totals * factor, "src", scatter_dimension=0, tiled=True),
        lax.psum_scatter(accum * factor[:, :, None, :], "src", scatter_dimension=0, tiled=True),
    )
    result = (
        (final_accum / final_total[:, :, None, :])
        .transpose(0, 3, 1, 2)
        .reshape(own_blocks * BLK, HEADS * HEAD)
    )
    return jax.nn.elu(result + bias)


def solution(mesh):
    placed = (
        P(("dst", "src"), None),
        P(),
        P(),
        P(),
        P(),
        P("src", "dst", None, None),
        P("src", "dst", None, None, None, None),
    )
    return jax.shard_map(
        body, mesh=mesh, in_specs=placed, out_specs=P(("dst", "src"), None), check_vma=False
    )
```

profile of v0, /device:TPU:8, one launch (start us, length us, event | category | flops | bytes accessed | tf_op | source)
XLA Modules:
  0.0 678.2 jit_solution(12250885677185442408)
XLA Ops:
  11.7 2.8 broadcast_compare_fusion
  14.5 41.0 %all-gather.2.cloned.1.call-done = bf16[4096,768]{1,0:T(8,128)(2,1)} async-done(((bf16[512,768]{1,0:T(8,128)(2,1)}), bf16[4096,768]{1,0:T(8,128)(2,1)}) %all-gather.2.cloned.1.call-update) | async-done | bytes 6291472 | tf_op jit(solution)/shard_map/all_gather | solution.py:25
  55.5 4.6 convolution_convert_fusion
  61.7 53.4 %all_gather.7 = f32[4,16384]{1,0:T(4,128)} all-gather(f32[4,512]{1,0:T(4,128)S(1)} %bitcast.90), channel_id=1, replica_groups=mesh['src'=32,'dst'=8] {'src'}, dimensions={1}, use_global_device_ids=true | all-gather | bytes 270336 | tf_op jit(solution)/shard_map/all_gather | solution.py:39
  116.0 1.3 gather_fusion.1
  117.3 2.4 gather_fusion
  119.7 11.0 %fusion.1 = f32[64,4,128]{2,1,0:T(4,128)} fusion(f32[64,4,128]{2,1,0:T(4,128)} %gather_fusion.1, f32[64,4,128]{2,1,0:T(4,128)} %gather_fusion, pred[64,128,128]{2,1,0:T(8,128)(4,1)S(1)} %bitcast.75), kind=kLoop, calls=%fused_computation.10 | loop fusion | flops 25133056 | bytes 1441792 | tf_op jit(solution)/shard_map/reduce_max | solution.py:75
  130.7 4.7 scatter_fusion
  135.4 1.4 gather_fusion.3
  138.4 3.1 gather_fusion.2
  141.5 13.0 %fusion.4 = f32[64,4,64,128]{3,2,1,0:T(8,128)} fusion(bf16[64,128,4,64]{1,3,2,0:T(8,128)(2,1)} %gather_fusion.2, f32[64,4,128]{2,1,0:T(4,128)S(1)} %copy-done.10, f32[64,4,128]{2,1,0:T(4,128)S(1)} %copy-done.7, f32[64,4,128]{2,1,0:T(4,128)S(1)} %copy-done.8, pred[64,128,128]{2,1,0:T(8,128)(4,1)S(1)} %bitcast.76), kind=kOutput, calls=%fused_computation.13 | convolution fusion | flops 570425344 | bytes 14024704 | tf_op jit(solution)/shard_map/lkij,ljkc->lkci/dot_general | solution.py:79
  154.5 2.1 broadcast_in_dim.26
  156.7 1.0 fusion.24
  157.8 6.6 broadcast_multiply_fusion.1
  164.4 14.6 %fusion.2 = f32[64,4,128]{2,1,0:T(4,128)S(1)} fusion(f32[64,4,128]{2,1,0:T(4,128)S(1)} %copy-done.11, f32[64,4,128]{2,1,0:T(4,128)S(1)} %copy-done.7, f32[64,4,128]{2,1,0:T(4,128)S(1)} %copy-done.9, pred[64,128,128]{2,1,0:T(8,128)(4,1)S(1)} %bitcast.77), kind=kLoop, calls=%fused_computation.11 | loop fusion | flops 33521664 | bytes 1572864 | tf_op jit(solution)/shard_map/reduce_sum | solution.py:78
  179.0 2.8 scatter_fusion.2
  181.8 19.4 %scatter_fusion.1 = f32[128,4,64,128]{3,2,1,0:T(8,128)} fusion(f32[128,4,64,128]{3,2,1,0:T(8,128)} %broadcast_multiply_fusion.1, s32[64]{0:T(128)S(1)} %get-tuple-element.12, f32[64,4,64,128]{3,2,1,0:T(8,128)} %fusion.4), kind=kCustom, calls=%fused_computation.5 | custom fusion | flops 2097152 | bytes 25166080 | tf_op jit(solution)/shard_map/scatter-add | solution.py:85
  201.1 77.0 %all-reduce.4.cloned.1.call-done = f32[128,4,128]{2,1,0:T(4,128)} async-done(((f32[128,4,128]{2,1,0:T(4,128)}), f32[128,4,128]{2,1,0:T(4,128)}) %all-reduce.4.cloned.1.call-update) | async-done | bytes 262160 | tf_op jit(solution)/shard_map/pmax | solution.py:86
  278.1 1.7 fusion.23
  279.9 12.7 %broadcast_multiply_fusion = f32[128,4,64,128]{3,2,1,0:T(8,128)} fusion(f32[128,4,64,128]{3,2,1,0:T(8,128)} %scatter_fusion.1, f32[128,4,128]{2,1,0:T(4,128)S(1)} %bitcast.83), kind=kLoop, calls=%fused_computation.14 | loop fusion | flops 4194304 | bytes 33816576 | tf_op jit(solution)/shard_map/mul | solution.py:90
  294.5 128.2 %all-reduce.6.cloned.1.call-done = f32[128,4,128]{2,1,0:T(4,128)} async-done(((f32[128,4,128]{2,1,0:T(4,128)}), f32[128,4,128]{2,1,0:T(4,128)}) %all-reduce.6.cloned.1.call-update) | async-done | bytes 262160
  423.4 245.5 %reduce-scatter.2.cloned.1.call-done = f32[4,4,64,128]{3,2,1,0:T(8,128)} async-done(((f32[128,4,64,128]{3,2,1,0:T(8,128)}), f32[4,4,64,128]{3,2,1,0:T(8,128)}) %reduce-scatter.2.cloned.1.call-update) | async-done | bytes 524304 | tf_op jit(solution)/shard_map/reduce_scatter | solution.py:90
  668.9 1.1 divide_bitcast_fusion
  670.6 1.0 copy.19
  (60 shorter events, 11.8 us)
Async XLA Ops:
  6.5 49.0 %copy-start = (bf16[768,256]{1,0:T(8,128)(2,1)S(1)}, bf16[768,256]{1,0:T(8,128)(2,1)}, u32[]{:S(2)}) copy-start(bf16[768,256]{1,0:T(8,128)(2,1)} %param.8) | copy-start | bytes 1179652
  6.5 49.0 %all-gather.2.cloned.1.call-start = ((), (), s32[]{:S(2)}) async-start(), calls=%async_computation.1 | async-start | bytes 7077888 | tf_op jit(solution)/shard_map/all_gather | solution.py:25
  7.3 270.8 %all-reduce.4.cloned.1.call-start = ((), (), s32[]{:S(2)}) async-start(), calls=%async_computation.2 | async-start | bytes 524288 | tf_op jit(solution)/shard_map/pmax | solution.py:86
  115.2 0.7 copy-start.4
  117.3 24.2 %copy-start.7 = (f32[64,4,128]{2,1,0:T(4,128)S(1)}, f32[64,4,128]{2,1,0:T(4,128)}, u32[]{:S(2)}) copy-start(f32[64,4,128]{2,1,0:T(4,128)} %gather_fusion.1) | copy-start | bytes 393220
  135.4 1.4 copy-start.2
  136.9 4.6 copy-start.8
  136.9 4.6 copy-start.10
  136.9 285.9 %all-reduce.6.cloned.1.call-start = ((), (), s32[]{:S(2)}) async-start(), calls=%async_computation.4 | async-start | bytes 524288
  154.5 2.1 copy-start.6
  154.5 2.2 copy-start.3
  154.5 2.2 copy-start.5
  157.7 6.6 copy-start.9
  157.8 6.6 copy-start.11
  279.8 389.1 %reduce-scatter.2.cloned.1.call-start = ((), (), s32[]{:S(2)}) async-start(), calls=%async_computation.3 | async-start | bytes 17301504 | tf_op jit(solution)/shard_map/reduce_scatter | solution.py:90
  279.9 391.8 %copy-start.1 = (bf16[768,256]{1,0:T(8,128)(2,1)S(1)}, bf16[768,256]{1,0:T(8,128)(2,1)}, u32[]{:S(2)}) copy-start(bf16[768,256]{1,0:T(8,128)(2,1)} %param.8) | copy-start | bytes 1179652
  292.5 0.7 copy-start.13
  292.5 377.8 %copy-start.12 = (f32[256]{0:T(256)S(1)}, f32[256]{0:T(256)}, u32[]{:S(2)}) copy-start(f32[256]{0:T(256)} %param.11) | copy-start | bytes 3076
Sparse Core Ops, SparseCore 0:
  9.2 46.3 all-gather.1
  137.0 141.0 all-reduce.3
  281.6 141.1 all-reduce.5
  426.7 242.1 reduce-scatter.1
where the time goes:
time: 680 us; the launch traced here: 678 us
  waiting for transfers between devices  492 us (72%)
  other arithmetic  79.3 us (12%)
  blocking collectives  53.4 us (8%)
  local copies, waits for them, and re-layouts  20.6 us (3%)
  matrix products  18.1 us (3%)
  between operations  14.1 us (2%)
    reduce_scatter x1, waiting for transfers between devices, body(): lax.psum_scatter(accum * factor[:, :, None, :], 'src', scatter_dimension=...  245 us
    unnamed x5, waiting for transfers between devices  129 us
    pmax x1, waiting for transfers between devices, body(): global_bound = lax.pmax(bound, 'src')  77 us
    all_gather x1, blocking collectives, body(): every_target = lax.all_gather(own_targets, 'src', axis=1, tiled=True)  53.4 us
    all_gather x1, waiting for transfers between devices, body(): lax.all_gather(features, 'dst', axis=0, tiled=True)  41 us
    scatter-add x1, other arithmetic, body(): accum = (accum_start * keep[:, :, None, :]).at[dst_pick].add(numer)  19.4 us
    reduce_sum x1, other arithmetic, body(): totals = (total_start * keep).at[dst_pick].add(weights.sum(-1))  14.6 us
  transfers between devices with their start and end apart: 4, of which 4 were waited for; matrix products, arithmetic and copies ran while one was open for 13% of the time, Pallas kernels for 0%

commit v1 on v0

v1 whole, which is shorter than its diff:
```python
import functools

import jax
import jax.numpy as jnp
from jax import lax
from jax.experimental import pallas as pl
from jax.experimental.pallas import tpu as pltpu
from jax.sharding import PartitionSpec as P

HEADS = 4
HEAD = 64
FEAT = HEADS * HEAD
BLK = 128
NBD = 4
SLOTS = 2
NY, NZ, NX, NC = 4, 8, 4, 2
PIECES = NX * NC
SRC_BLOCKS = NBD * PIECES
OWNERS = NY * NZ
PAIRS = OWNERS * SLOTS
ROWS = FEAT + 16
LOG2E = 1.4426950408889634
EMPTY = -(2.0**100)
GROUPS = NZ // 2
F32 = jnp.float32
BF16 = jnp.bfloat16
VMEM = pl.BlockSpec(memory_space=pltpu.VMEM)
ANY = pl.BlockSpec(memory_space=pl.ANY)


def params(**more):
    return pltpu.CompilerParams(vmem_limit_bytes=40 * 1024 * 1024, **more)


def leaky(values):
    return jnp.maximum(values, 0.2 * values)


def y_from(k):
    return [(y * NZ + z, (y - k) % NY * NZ + z) for y in range(NY) for z in range(NZ)]


def z_from(k):
    return [(y * NZ + z, y * NZ + (z - k) % NZ) for y in range(NY) for z in range(NZ)]


def x_from(k):
    return [(x * NC + c, (x - k) % NX * NC + c) for x in range(NX) for c in range(NC)]


def core_from(k):
    return [(x * NC + c, x * NC + (c - k) % NC) for x in range(NX) for c in range(NC)]


def up_offset(group):
    return NZ // 2 - group


def down_offset(group):
    return (NZ // 2 + 1 + group) % NZ


def head_sums(products):
    return jnp.concatenate(
        [jnp.sum(products[h * HEAD : (h + 1) * HEAD], axis=0, keepdims=True) for h in range(HEADS)],
        axis=0,
    )


def project_kernel(x_ref, w_ref, src_ref, dst_ref, hidden_ref, target_ref, self_ref, att_ref):
    att_src = jnp.broadcast_to(src_ref[...] * LOG2E, (BLK, FEAT)).T
    att_dst = jnp.broadcast_to(dst_ref[...] * LOG2E, (BLK, FEAT)).T
    att_ref[...] = att_src
    for b in range(NBD):
        hidden = jnp.dot(
            x_ref[b * BLK : (b + 1) * BLK, :], w_ref[...], preferred_element_type=F32
        )
        hidden = hidden.T.astype(BF16)
        hidden_ref[b] = hidden
        wide = hidden.astype(F32)
        source = head_sums(wide * att_src)
        target = head_sums(wide * att_dst)
        target_ref[b] = target
        self_ref[b] = leaky(target + source)


def project(features, weight, att_src, att_dst):
    return pl.pallas_call(
        project_kernel,
        out_shape=(
            jax.ShapeDtypeStruct((NBD, FEAT, BLK), BF16),
            jax.ShapeDtypeStruct((NBD, HEADS, BLK), F32),
            jax.ShapeDtypeStruct((NBD, HEADS, BLK), F32),
            jax.ShapeDtypeStruct((FEAT, BLK), F32),
        ),
        in_specs=[VMEM] * 4,
        out_specs=(VMEM,) * 4,
        compiler_params=params(),
        name="project",
    )(features, weight, att_src.reshape(1, FEAT), att_dst.reshape(1, FEAT))


def mask_kernel(mask_ref, out_ref):
    for n in range(mask_ref.shape[0]):
        for t in range(SLOTS):
            bias = jnp.where(mask_ref[n, t] > 0, 0.0, EMPTY).astype(F32)
            out_ref[n, t] = bias.T


def mask_bias(masks):
    step = 4
    spec = pl.BlockSpec((step, SLOTS, BLK, BLK), lambda i: (i, 0, 0, 0))
    return pl.pallas_call(
        mask_kernel,
        grid=(OWNERS // step,),
        out_shape=jax.ShapeDtypeStruct((OWNERS, SLOTS, BLK, BLK), F32),
        in_specs=[spec],
        out_specs=spec,
        compiler_params=params(),
        cost_estimate=pl.CostEstimate(
            flops=PAIRS * BLK * BLK * 8, bytes_accessed=2 * PAIRS * BLK * BLK * 4, transcendentals=0
        ),
        name="mask_bias",
    )(masks)


def owner_of(scal, k, offset):
    y = lax.rem(scal[PAIRS] + k, NY)
    z = lax.rem(scal[PAIRS + 1] + offset, NZ)
    return y * NZ + z


def halves(values):
    high = values.astype(BF16).astype(F32)
    return high, (values - high).astype(BF16).astype(F32)


def slot_partial(hidden, att, bias, target, out_ref, place):
    sources = head_sums(hidden.astype(F32) * att)
    sources = jnp.concatenate([sources, sources], axis=0).T
    bounds, totals = [], []
    for h in range(HEADS):
        masked = sources[:, h : h + 1] + bias
        top = jnp.max(masked, axis=0, keepdims=True)
        own = target[h : h + 1]
        high, low = halves(leaky(own + top))
        bound = high + low
        weights = jnp.exp2(
            jnp.maximum(masked + (own - bound), 0.2 * masked + (0.2 * own - bound))
        )
        bounds.append((high, low))
        totals.append(halves(jnp.sum(weights, axis=0, keepdims=True)))
        out_ref[place + (pl.ds(h * HEAD, HEAD), slice(None))] = jnp.dot(
            hidden[h * HEAD : (h + 1) * HEAD], weights.astype(BF16), preferred_element_type=F32
        ).astype(BF16)
    rows = [b[0] for b in bounds] + [t[0] for t in totals]
    rows += [b[1] for b in bounds] + [t[1] for t in totals]
    out_ref[place + (pl.ds(FEAT, 16), slice(None))] = jnp.concatenate(rows, axis=0).astype(BF16)


def slots_kernel(offsets, scal, up_mask, down_mask, up_target, down_target, att, *rest):
    pieces, outs = rest[:PIECES], rest[PIECES : PIECES + NY]
    hidden, made, sems = rest[PIECES + NY :]
    step = pl.program_id(0)

    @pl.when(step == 0)
    def _():
        copies = [
            pltpu.make_async_copy(pieces[n], hidden.at[pl.ds(n * NBD, NBD)], sems.at[n])
            for n in range(PIECES)
        ]
        for copy in copies:
            copy.start()
        for copy in copies:
            copy.wait()

    for n, (offset, mask, target) in enumerate(
        zip(offsets, (up_mask, down_mask), (up_target, down_target), strict=True)
    ):
        owner = owner_of(scal, step, offset)
        for t in range(SLOTS):
            pair = scal[owner * SLOTS + t]
            block = lax.rem(pair, SRC_BLOCKS)
            place = lax.div(pair, SRC_BLOCKS)
            holder = lax.div(block, NBD)
            dx = lax.rem(lax.div(holder, NC) - scal[PAIRS + 2] + NX, NX)
            dc = lax.rem(lax.rem(holder, NC) - scal[PAIRS + 3] + NC, NC)
            held = (dx * NC + dc) * NBD + lax.rem(block, NBD)
            slot_partial(hidden[held], att[...], mask[0, t], target[step, place], made, (n, t))

    for k in range(NY):

        @pl.when(step == k)
        def _(k=k):
            outs[k][...] = made[...]


def slots(group, scal, bias, targets, att, pieces):
    offsets = (up_offset(group), down_offset(group))

    def mask_spec(offset):
        return pl.BlockSpec(
            (1, SLOTS, BLK, BLK), lambda i, scal: (owner_of(scal, i, offset), 0, 0, 0)
        )

    def whole(shape):
        return pl.BlockSpec(shape, lambda i, scal: (0,) * len(shape))

    shape = (2, SLOTS, ROWS, BLK)
    return pl.pallas_call(
        functools.partial(slots_kernel, offsets),
        out_shape=(jax.ShapeDtypeStruct(shape, BF16),) * NY,
        grid_spec=pltpu.PrefetchScalarGridSpec(
            num_scalar_prefetch=1,
            grid=(NY,),
            in_specs=[mask_spec(offsets[0]), mask_spec(offsets[1])]
            + [whole((NY, NBD, HEADS, BLK))] * 2
            + [whole((FEAT, BLK))]
            + [ANY] * PIECES,
            out_specs=(whole(shape),) * NY,
            scratch_shapes=[
                pltpu.VMEM((SRC_BLOCKS, FEAT, BLK), BF16),
                pltpu.VMEM(shape, BF16),
                pltpu.SemaphoreType.DMA((PIECES,)),
            ],
        ),
        compiler_params=params(),
        cost_estimate=pl.CostEstimate(
            flops=2 * 16 * BLK * BLK * FEAT, bytes_accessed=8 * 1024 * 1024, transcendentals=16 * HEADS * BLK * BLK
        ),
        name="slots",
    )(scal, bias, bias, targets[offsets[0]], targets[offsets[1]], att, *pieces)


def bound_total(ref, place):
    rows = ref[place + (pl.ds(FEAT, 16), slice(None))].astype(F32)
    both = rows[:8] + rows[8:]
    return both[:HEADS], both[HEADS:]


def merge(slot_list, dense, bounds, totals, sums, self_parts=None):
    for b in range(NBD):
        top = jnp.full((HEADS, BLK), EMPTY, F32)
        if self_parts is not None:
            top = self_parts[0][b]
        for ref in dense:
            top = jnp.maximum(top, bound_total(ref, (b,))[0])
        bounds[b] = top
    for ref, index, place in slot_list:
        bounds[place] = jnp.maximum(bounds[place], bound_total(ref, index)[0])
    for b in range(NBD):
        total = jnp.zeros((HEADS, BLK), F32)
        terms = []
        if self_parts is not None:
            factor = jnp.exp2(self_parts[0][b] - bounds[b])
            total += factor
            terms.append((self_parts[1], (b,), factor))
        for ref in dense:
            bound, more = bound_total(ref, (b,))
            factor = jnp.exp2(bound - bounds[b])
            total += more * factor
            terms.append((ref, (b,), factor))
        totals[b] = total
        for h in range(HEADS):
            rows = pl.ds(h * HEAD, HEAD)
            value = jnp.zeros((HEAD, BLK), F32)
            for ref, index, factor in terms:
                value += ref[index + (rows, slice(None))].astype(F32) * factor[h : h + 1]
            sums[b, rows, :] = value
    for ref, index, place in slot_list:
        bound, more = bound_total(ref, index)
        factor = jnp.exp2(bound - bounds[place])
        totals[place] += more * factor
        for h in range(HEADS):
            rows = pl.ds(h * HEAD, HEAD)
            sums[place, rows, :] += (
                ref[index + (rows, slice(None))].astype(F32) * factor[h : h + 1]
            )


def placed(scals, offset, refs, n):
    owner = owner_of(scals[0], 0, offset)
    return [
        (refs[k], (n, t), lax.div(scals[k][owner * SLOTS + t], SRC_BLOCKS))
        for k in range(NY)
        for t in range(SLOTS)
    ]


def write_dense(out, bounds, totals, sums):
    for b in range(NBD):
        out[b, pl.ds(0, FEAT), :] = sums[b].astype(BF16)
        both = halves(jnp.concatenate([bounds[b], totals[b]], axis=0))
        out[b, pl.ds(FEAT, 16), :] = jnp.concatenate(both, axis=0).astype(BF16)


def merge_kernel(work, *refs):
    scals, refs = refs[:NY], refs[NY:]
    parts, refs = refs[:NY], refs[NY:]
    n_dense = sum(w[2] for w in work)
    dense, refs = refs[:n_dense], refs[n_dense:]
    outs, (bounds, totals, sums) = refs[: len(work)], refs[len(work) :]
    for out, (offset, n, count) in zip(outs, work, strict=True):
        mine, dense = dense[:count], dense[count:]
        merge(placed(scals, offset, parts, n), mine, bounds, totals, sums)
        write_dense(out, bounds, totals, sums)


def merge_scratch():
    return [
        pltpu.VMEM((NBD, HEADS, BLK), F32),
        pltpu.VMEM((NBD, HEADS, BLK), F32),
        pltpu.VMEM((NBD, FEAT, BLK), F32),
    ]


SMEM = pl.BlockSpec(memory_space=pltpu.SMEM)


def merge_group(work, scals, parts, dense):
    return pl.pallas_call(
        functools.partial(merge_kernel, work),
        out_shape=(jax.ShapeDtypeStruct((NBD, ROWS, BLK), BF16),) * len(work),
        in_specs=[SMEM] * NY + [VMEM] * (NY + len(dense)),
        out_specs=(VMEM,) * len(work),
        scratch_shapes=merge_scratch(),
        compiler_params=params(),
        cost_estimate=pl.CostEstimate(flops=20_000_000, bytes_accessed=2_000_000, transcendentals=0),
        name="merge",
    )(*scals, *parts, *dense)


def final_kernel(work, *refs):
    scals, refs = refs[:NY], refs[NY:]
    parts, refs = refs[:NY], refs[NY:]
    dense, (self_ref, hidden_ref, bias_ref, out, bounds, totals, sums) = refs[:2], refs[2:]
    offset, n = work
    merge(placed(scals, offset, parts, n), dense, bounds, totals, sums, (self_ref, hidden_ref))
    for b in range(NBD):
        scale = 1.0 / totals[b]
        value = jnp.concatenate(
            [sums[b, pl.ds(h * HEAD, HEAD), :] * scale[h : h + 1] for h in range(HEADS)], axis=0
        )
        value = value.T + bias_ref[...]
        out[pl.ds(b * BLK, BLK), :] = jnp.where(
            value > 0, value, jnp.exp(jnp.minimum(value, 0.0)) - 1.0
        )


def finish(work, scals, parts, dense, self_logit, hidden, bias):
    return pl.pallas_call(
        functools.partial(final_kernel, work),
        out_shape=jax.ShapeDtypeStruct((NBD * BLK, FEAT), F32),
        in_specs=[SMEM] * NY + [VMEM] * (NY + 5),
        out_specs=VMEM,
        scratch_shapes=merge_scratch(),
        compiler_params=params(),
        name="finish",
    )(*scals, *parts, *dense, self_logit, hidden, bias.reshape(1, FEAT))


def body(features, weight, att_src, att_dst, bias, block_pairs, edge_masks):
    src = lax.axis_index("src")
    dst = lax.axis_index("dst")
    place = jnp.stack([src // NZ, src % NZ, dst // NC, dst % NC]).astype(jnp.int32)
    scal = jnp.concatenate([block_pairs.reshape(-1), place])
    scals = [scal] + [lax.ppermute(scal, "src", y_from(-k)) for k in range(1, NY)]

    hidden, own_target, self_logit, att = project(features, weight, att_src, att_dst)
    along_x = [hidden] + [lax.ppermute(hidden, "dst", x_from(k)) for k in range(1, NX)]
    pieces = []
    for piece in along_x:
        pieces += [piece, lax.ppermute(piece, "dst", core_from(1))]
    along_y = jnp.stack(
        [own_target] + [lax.ppermute(own_target, "src", y_from(k)) for k in range(1, NY)]
    )
    targets = [along_y] + [lax.ppermute(along_y, "src", z_from(k)) for k in range(1, NZ)]

    masks = mask_bias(edge_masks.reshape(OWNERS, SLOTS, BLK, BLK))

    up, down = [], []
    for group in range(GROUPS):
        made = slots(group, scal, masks, targets, att, pieces)
        parts = [made[0]] + [lax.ppermute(made[k], "src", y_from(-k)) for k in range(1, NY)]
        work = [(up_offset(group), 0, len(up))]
        if group < GROUPS - 1:
            work.append((down_offset(group), 1, len(down)))
            sent = merge_group(work, scals, parts, up + down)
            down = [lax.ppermute(sent[1], "src", z_from(1))]
        else:
            sent = merge_group(work, scals, parts, up)
        up = [lax.ppermute(sent[0], "src", z_from(-1))]
    return finish((0, 1), scals, parts, up + down, self_logit, hidden, bias)


def solution(mesh):
    placed_at = (
        P(("dst", "src"), None),
        P(),
        P(),
        P(),
        P(),
        P("src", "dst", None, None),
        P("src", "dst", None, None, None, None),
    )
    return jax.shard_map(
        body, mesh=mesh, in_specs=placed_at, out_specs=P(("dst", "src"), None), check_vma=False
    )
```

time: 680 us -> 140 us (0.21)
  waiting for transfers between devices: 492 us -> 34.2 us
  other arithmetic: 79.3 us -> 0.01 us
  starting transfers between devices: 0.31 us -> 71.8 us
  blocking collectives: 53.4 us -> 0 us
  Pallas kernels: 0 us -> 25.4 us
  matrix products: 18.1 us -> 0 us
  local copies, waits for them, and re-layouts: 20.6 us -> 6.63 us
  between operations: 14.1 us -> 0.28 us
    reduce_scatter x1 -> x0, waiting for transfers between devices: 245 us -> none  [body(): lax.psum_scatter(accum * factor[:, :, None, :], 'src', scatter_dimension=...]
    unnamed x5 -> x0, waiting for transfers between devices: 129 us -> none
    pmax x1 -> x0, waiting for transfers between devices: 77 us -> none  [body(): global_bound = lax.pmax(bound, 'src')]
    ppermute x0 -> x39, starting transfers between devices: none -> 71.8 us  [the longest x12 23.9 us: body(): lax.ppermute(made[k], 'src', y_from(-k))]
    all_gather x1 -> x0, blocking collectives: 53.4 us -> none  [body(): every_target = lax.all_gather(own_targets, 'src', axis=1, tiled=True)]
    all_gather x1 -> x0, waiting for transfers between devices: 41 us -> none  [body(): lax.all_gather(features, 'dst', axis=0, tiled=True)]
    ppermute x0 -> x39, waiting for transfers between devices: none -> 34.2 us  [the longest x4 9.17 us: body(): up = [lax.ppermute(sent[0], 'src', z_from(-1))]]
    pallas_call x0 -> x11, Pallas kernels: none -> 25.4 us  [the longest x4 17.8 us: slots(): pl.pallas_call(functools.partial(slots_kernel, offsets), out_shape=(jax.S...]
  transfers between devices with their start and end apart: 4 -> 39, of which waited for: 4 -> 14; matrix products, arithmetic and copies ran while one was open for 13% -> 1% of each run, Pallas kernels for 0% -> 13%
where the time goes in v1:
time: 140 us; the launch traced here: 138 us
  starting transfers between devices  71.8 us (51%)
  waiting for transfers between devices  34.2 us (24%)
  Pallas kernels  25.4 us (18%)
  local copies, waits for them, and re-layouts  6.63 us (5%)
    ppermute x12, starting transfers between devices, body(): lax.ppermute(made[k], 'src', y_from(-k))  23.9 us
    ppermute x7, starting transfers between devices, body(): lax.ppermute(along_y, 'src', z_from(k))  22 us
    pallas_call x4, Pallas kernels, slots(): pl.pallas_call(functools.partial(slots_kernel, offsets), out_shape=(jax.S...  17.8 us
    ppermute x3, starting transfers between devices, body(): down = [lax.ppermute(sent[1], 'src', z_from(1))]  9.65 us
    ppermute x4, waiting for transfers between devices, body(): up = [lax.ppermute(sent[0], 'src', z_from(-1))]  9.17 us
    ppermute x3, waiting for transfers between devices, body(): lax.ppermute(hidden, 'dst', x_from(k))  9.02 us
    ppermute x3, starting transfers between devices, body(): lax.ppermute(own_target, 'src', y_from(k))  6.51 us
    unnamed x13, local copies, waits for them, and re-layouts  6.44 us
  transfers between devices with their start and end apart: 39, of which 14 were waited for; matrix products, arithmetic and copies ran while one was open for 1% of the time, Pallas kernels for 13%

profile of v1, /device:TPU:8, one launch (start us, length us, event | category | flops | bytes accessed | tf_op | source)
XLA Modules:
  0.0 138.3 jit_solution(3026374318400495558)
XLA Ops:
  4.0 3.1 %collective-permute-start.10 = (bf16[4,256,128]{2,1,0:T(8,128)(2,1)S(1)}, bf16[4,256,128]{2,1,0:T(8,128)(2,1)S(1)}, u32[]{:S(2)}, u32[]{:S(2)}) collective-permute-start(bf16[4,256,128]{2,1,0:T(8,128)(2,1)S(1)} %get-tuple-element.33.rest_0_.refs_11_), channel_id=1, source_target_pairs={{0,4},{1,5},{2,6},{3,7},{4,0},{5,1},{6,2},{7,3},{8,12},{9,13},{10,... | collective-permute-start | bytes 786440 | tf_op jit(solution)/shard_map/ppermute | solution.py:370
  7.7 2.6 %collective-permute-start.8 = (bf16[4,256,128]{2,1,0:T(8,128)(2,1)S(1)}, bf16[4,256,128]{2,1,0:T(8,128)(2,1)S(1)}, u32[]{:S(2)}, u32[]{:S(2)}) collective-permute-start(bf16[4,256,128]{2,1,0:T(8,128)(2,1)S(1)} %get-tuple-element.33.rest_0_.refs_11_), channel_id=1, source_target_pairs={{0,6},{1,7},{2,0},{3,1},{4,2},{5,3},{6,4},{7,5},{8,14},{9,15},{10,... | collective-permute-start | bytes 786440 | tf_op jit(solution)/shard_map/ppermute | solution.py:370
  10.4 4.5 %collective-permute-done.10.rest_4_ = bf16[4,256,128]{2,1,0:T(8,128)(2,1)S(1)} collective-permute-done((bf16[4,256,128]{2,1,0:T(8,128)(2,1)S(1)}, bf16[4,256,128]{2,1,0:T(8,128)(2,1)S(1)}, u32[]{:S(2)}, u32[]{:S(2)}) %collective-permute-start.10) | collective-permute-done | bytes 262176 | tf_op jit(solution)/shard_map/ppermute | solution.py:370
  14.9 4.4 %collective-permute-done.12.rest_6_ = bf16[4,256,128]{2,1,0:T(8,128)(2,1)S(1)} collective-permute-done((bf16[4,256,128]{2,1,0:T(8,128)(2,1)S(1)}, bf16[4,256,128]{2,1,0:T(8,128)(2,1)S(1)}, u32[]{:S(2)}, u32[]{:S(2)}) %collective-permute-start.12) | collective-permute-done | bytes 262176 | tf_op jit(solution)/shard_map/ppermute | solution.py:370
  24.9 2.2 %collective-permute-done.3 = f32[4,4,128]{2,1,0:T(4,128)S(1)} collective-permute-done((f32[4,4,128]{2,1,0:T(4,128)S(1)}, f32[4,4,128]{2,1,0:T(4,128)S(1)}, u32[]{:S(2)}, u32[]{:S(2)}) %collective-permute-start.3) | collective-permute-done | bytes 8224 | tf_op jit(solution)/shard_map/ppermute | solution.py:375
  27.1 3.5 %collective-permute-start.4 = (f32[4,4,128]{2,1,0:T(4,128)S(1)}, f32[4,4,128]{2,1,0:T(4,128)S(1)}, u32[]{:S(2)}, u32[]{:S(2)}) collective-permute-start(f32[4,4,128]{2,1,0:T(4,128)S(1)} %get-tuple-element.31), channel_id=1, source_target_pairs={{0,128},{8,136},{16,144},{24,152},{32,160},{40,168},{48,176},{56,1... | collective-permute-start | bytes 24584 | tf_op jit(solution)/shard_map/ppermute | solution.py:375
  32.3 7.3 %collective-permute-start.27 = (f32[4,4,4,128]{3,2,1,0:T(4,128)S(1)}, f32[4,4,4,128]{3,2,1,0:T(4,128)S(1)}, u32[]{:S(2)}, u32[]{:S(2)}) collective-permute-start(f32[4,4,4,128]{3,2,1,0:T(4,128)S(1)} %pad_maximum_fusion.down_target), channel_id=1, source_target_pairs={{0,32},{8,40},{16,48},{24,56},{32,0},{40,8},{48,16},{56,24},{64,96... | collective-permute-start | bytes 98312 | tf_op jit(solution)/shard_map/ppermute | solution.py:377
  41.4 3.4 %collective-permute-start.28 = (f32[4,4,4,128]{3,2,1,0:T(4,128)S(1)}, f32[4,4,4,128]{3,2,1,0:T(4,128)S(1)}, u32[]{:S(2)}, u32[]{:S(2)}) collective-permute-start(f32[4,4,4,128]{3,2,1,0:T(4,128)S(1)} %pad_maximum_fusion.down_target), channel_id=1, source_target_pairs={{0,24},{8,32},{16,40},{24,48},{32,56},{40,0},{48,8},{56,16},{64,88... | collective-permute-start | bytes 98312 | tf_op jit(solution)/shard_map/ppermute | solution.py:377
  49.2 4.4 %slots.7 = (bf16[2,2,272,128]{3,2,1,0:T(8,128)(2,1)S(1)}, bf16[2,2,272,128]{3,2,1,0:T(8,128)(2,1)S(1)}, bf16[2,2,272,128]{3,2,1,0:T(8,128)(2,1)S(1)}, bf16[2,2,272,128]{3,2,1,0:T(8,128)(2,1)S(1)}) custom-call(s32[68]{0:T(128)S(1)} %concatenate.3.scal.refs_0_, f32[32,2,128,128]{3,2,1,0:T(8,128)S(1)} %mask_bias.1.up_mask.down_mask, ...), custom_call_target="tpu_custom_call" | custom-call | flops 134217728 | bytes 8388608 | tf_op jit(solution)/shard_map/slots/pallas_call | solution.py:210
  57.4 2.4 %collective-permute-start.31 = (bf16[2,2,272,128]{3,2,1,0:T(8,128)(2,1)S(1)}, bf16[2,2,272,128]{3,2,1,0:T(8,128)(2,1)S(1)}, u32[]{:S(2)}, u32[]{:S(2)}) collective-permute-start(bf16[2,2,272,128]{3,2,1,0:T(8,128)(2,1)S(1)} %get-tuple-element.49), channel_id=1, source_target_pairs={{0,192},{8,200},{16,208},{24,216},{32,224},{40,232},{48,240},{56,2... | collective-permute-start | bytes 835592 | tf_op jit(solution)/shard_map/ppermute | solution.py:384
  62.1 2.3 %collective-permute-done.refs_1_ = s32[68]{0:T(128)S(1)} collective-permute-done((s32[68]{0:T(128)S(1)}, s32[68]{0:T(128)S(1)}, u32[]{:S(2)}, u32[]{:S(2)}) %collective-permute-start) | collective-permute-done | bytes 304 | tf_op jit(solution)/shard_map/ppermute | solution.py:367
  66.4 4.7 %collective-permute-start.22 = (f32[4,4,4,128]{3,2,1,0:T(4,128)S(1)}, f32[4,4,4,128]{3,2,1,0:T(4,128)S(1)}, u32[]{:S(2)}, u32[]{:S(2)}) collective-permute-start(f32[4,4,4,128]{3,2,1,0:T(4,128)S(1)} %pad_maximum_fusion.down_target), channel_id=1, source_target_pairs={{0,40},{8,48},{16,56},{24,0},{32,8},{40,16},{48,24},{56,32},{64,10... | collective-permute-start | bytes 98312 | tf_op jit(solution)/shard_map/ppermute | solution.py:377
  72.7 4.9 %collective-permute-start.17 = (f32[4,4,4,128]{3,2,1,0:T(4,128)S(1)}, f32[4,4,4,128]{3,2,1,0:T(4,128)S(1)}, u32[]{:S(2)}, u32[]{:S(2)}) collective-permute-start(f32[4,4,4,128]{3,2,1,0:T(4,128)S(1)} %pad_maximum_fusion.down_target), channel_id=1, source_target_pairs={{0,48},{8,56},{16,0},{24,8},{32,16},{40,24},{48,32},{56,40},{64,11... | collective-permute-start | bytes 98312 | tf_op jit(solution)/shard_map/ppermute | solution.py:377
  78.2 4.4 %slots.6 = (bf16[2,2,272,128]{3,2,1,0:T(8,128)(2,1)S(1)}, bf16[2,2,272,128]{3,2,1,0:T(8,128)(2,1)S(1)}, bf16[2,2,272,128]{3,2,1,0:T(8,128)(2,1)S(1)}, bf16[2,2,272,128]{3,2,1,0:T(8,128)(2,1)S(1)}) custom-call(s32[68]{0:T(128)S(1)} %concatenate.3.scal.refs_0_, f32[32,2,128,128]{3,2,1,0:T(8,128)S(1)} %mask_bias.1.up_mask.down_mask, ...), custom_call_target="tpu_custom_call" | custom-call | flops 134217728 | bytes 8388608 | tf_op jit(solution)/shard_map/slots/pallas_call | solution.py:210
  82.8 3.6 %collective-permute-start.25 = (bf16[2,2,272,128]{3,2,1,0:T(8,128)(2,1)S(1)}, bf16[2,2,272,128]{3,2,1,0:T(8,128)(2,1)S(1)}, u32[]{:S(2)}, u32[]{:S(2)}) collective-permute-start(bf16[2,2,272,128]{3,2,1,0:T(8,128)(2,1)S(1)} %get-tuple-element.44), channel_id=1, source_target_pairs={{0,128},{8,136},{16,144},{24,152},{32,160},{40,168},{48,176},{56,1... | collective-permute-start | bytes 835592 | tf_op jit(solution)/shard_map/ppermute | solution.py:384
  89.3 3.2 %collective-permute-start.33 = (bf16[4,272,128]{2,1,0:T(8,128)(2,1)S(1)}, bf16[4,272,128]{2,1,0:T(8,128)(2,1)S(1)}, u32[]{:S(2)}, u32[]{:S(2)}) collective-permute-start(bf16[4,272,128]{2,1,0:T(8,128)(2,1)S(1)} %get-tuple-element.51), channel_id=1, source_target_pairs={{0,56},{8,0},{16,8},{24,16},{32,24},{40,32},{48,40},{56,48},{64,12... | collective-permute-start | bytes 835592 | tf_op jit(solution)/shard_map/ppermute | solution.py:389
  93.3 4.4 %slots.5 = (bf16[2,2,272,128]{3,2,1,0:T(8,128)(2,1)S(1)}, bf16[2,2,272,128]{3,2,1,0:T(8,128)(2,1)S(1)}, bf16[2,2,272,128]{3,2,1,0:T(8,128)(2,1)S(1)}, bf16[2,2,272,128]{3,2,1,0:T(8,128)(2,1)S(1)}) custom-call(s32[68]{0:T(128)S(1)} %concatenate.3.scal.refs_0_, f32[32,2,128,128]{3,2,1,0:T(8,128)S(1)} %mask_bias.1.up_mask.down_mask, ...), custom_call_target="tpu_custom_call" | custom-call | flops 134217728 | bytes 8388608 | tf_op jit(solution)/shard_map/slots/pallas_call | solution.py:210
  98.9 3.5 %collective-permute-start.20 = (bf16[2,2,272,128]{3,2,1,0:T(8,128)(2,1)S(1)}, bf16[2,2,272,128]{3,2,1,0:T(8,128)(2,1)S(1)}, u32[]{:S(2)}, u32[]{:S(2)}) collective-permute-start(bf16[2,2,272,128]{3,2,1,0:T(8,128)(2,1)S(1)} %get-tuple-element.40), channel_id=1, source_target_pairs={{0,128},{8,136},{16,144},{24,152},{32,160},{40,168},{48,176},{56,1... | collective-permute-start | bytes 835592 | tf_op jit(solution)/shard_map/ppermute | solution.py:384
  104.7 3.2 %collective-permute-start.35 = (bf16[4,272,128]{2,1,0:T(8,128)(2,1)S(1)}, bf16[4,272,128]{2,1,0:T(8,128)(2,1)S(1)}, u32[]{:S(2)}, u32[]{:S(2)}) collective-permute-start(bf16[4,272,128]{2,1,0:T(8,128)(2,1)S(1)} %get-tuple-element.53), channel_id=1, source_target_pairs={{0,56},{8,0},{16,8},{24,16},{32,24},{40,32},{48,40},{56,48},{64,12... | collective-permute-start | bytes 835592 | tf_op jit(solution)/shard_map/ppermute | solution.py:389
  107.9 4.4 %slots.4 = (bf16[2,2,272,128]{3,2,1,0:T(8,128)(2,1)S(1)}, bf16[2,2,272,128]{3,2,1,0:T(8,128)(2,1)S(1)}, bf16[2,2,272,128]{3,2,1,0:T(8,128)(2,1)S(1)}, bf16[2,2,272,128]{3,2,1,0:T(8,128)(2,1)S(1)}) custom-call(s32[68]{0:T(128)S(1)} %concatenate.3.scal.refs_0_, f32[32,2,128,128]{3,2,1,0:T(8,128)S(1)} %mask_bias.1.up_mask.down_mask, ...), custom_call_target="tpu_custom_call" | custom-call | flops 134217728 | bytes 8388608 | tf_op jit(solution)/shard_map/slots/pallas_call | solution.py:210
  113.5 5.2 %collective-permute-start.15 = (bf16[2,2,272,128]{3,2,1,0:T(8,128)(2,1)S(1)}, bf16[2,2,272,128]{3,2,1,0:T(8,128)(2,1)S(1)}, u32[]{:S(2)}, u32[]{:S(2)}) collective-permute-start(bf16[2,2,272,128]{3,2,1,0:T(8,128)(2,1)S(1)} %get-tuple-element.36), channel_id=1, source_target_pairs={{0,128},{8,136},{16,144},{24,152},{32,160},{40,168},{48,176},{56,1... | collective-permute-start | bytes 835592 | tf_op jit(solution)/shard_map/ppermute | solution.py:384
  119.9 3.2 %collective-permute-start.38 = (bf16[4,272,128]{2,1,0:T(8,128)(2,1)S(1)}, bf16[4,272,128]{2,1,0:T(8,128)(2,1)S(1)}, u32[]{:S(2)}, u32[]{:S(2)}) collective-permute-start(bf16[4,272,128]{2,1,0:T(8,128)(2,1)S(1)} %get-tuple-element.55), channel_id=1, source_target_pairs={{0,56},{8,0},{16,8},{24,16},{32,24},{40,32},{48,40},{56,48},{64,12... | collective-permute-start | bytes 835592 | tf_op jit(solution)/shard_map/ppermute | solution.py:389
  123.4 2.9 %collective-permute-done.16.refs_7_ = bf16[2,2,272,128]{3,2,1,0:T(8,128)(2,1)S(1)} collective-permute-done((bf16[2,2,272,128]{3,2,1,0:T(8,128)(2,1)S(1)}, bf16[2,2,272,128]{3,2,1,0:T(8,128)(2,1)S(1)}, u32[]{:S(2)}, u32[]{:S(2)}) %collective-permute-start.16) | collective-permute-done | bytes 278560 | tf_op jit(solution)/shard_map/ppermute | solution.py:384
  128.6 7.7 %collective-permute-done.37.refs_8_ = bf16[4,272,128]{2,1,0:T(8,128)(2,1)S(1)} collective-permute-done((bf16[4,272,128]{2,1,0:T(8,128)(2,1)S(1)}, bf16[4,272,128]{2,1,0:T(8,128)(2,1)S(1)}, u32[]{:S(2)}, u32[]{:S(2)}) %collective-permute-start.37) | collective-permute-done | bytes 278560 | tf_op jit(solution)/shard_map/ppermute | solution.py:392
  (81 shorter events, 42.3 us)
Async XLA Ops:
  4.0 10.8 %collective-permute-start.10 = (bf16[4,256,128]{2,1,0:T(8,128)(2,1)S(1)}, bf16[4,256,128]{2,1,0:T(8,128)(2,1)S(1)}, u32[]{:S(2)}, u32[]{:S(2)}) collective-permute-start(bf16[4,256,128]{2,1,0:T(8,128)(2,1)S(1)} %get-tuple-element.33.rest_0_.refs_11_), channel_id=1, source_target_pairs={{0,4},{1,5},{2,6},{3,7},{4,0},{5,1},{6,2},{7,3},{8,12},{9,13},{10,... | collective-permute-start | bytes 786440 | tf_op jit(solution)/shard_map/ppermute | solution.py:370
  7.1 12.2 %collective-permute-start.12 = (bf16[4,256,128]{2,1,0:T(8,128)(2,1)S(1)}, bf16[4,256,128]{2,1,0:T(8,128)(2,1)S(1)}, u32[]{:S(2)}, u32[]{:S(2)}) collective-permute-start(bf16[4,256,128]{2,1,0:T(8,128)(2,1)S(1)} %get-tuple-element.33.rest_0_.refs_11_), channel_id=1, source_target_pairs={{0,2},{1,3},{2,4},{3,5},{4,6},{5,7},{6,0},{7,1},{8,10},{9,11},{10,... | collective-permute-start | bytes 786440 | tf_op jit(solution)/shard_map/ppermute | solution.py:370
  7.7 11.7 %collective-permute-start.8 = (bf16[4,256,128]{2,1,0:T(8,128)(2,1)S(1)}, bf16[4,256,128]{2,1,0:T(8,128)(2,1)S(1)}, u32[]{:S(2)}, u32[]{:S(2)}) collective-permute-start(bf16[4,256,128]{2,1,0:T(8,128)(2,1)S(1)} %get-tuple-element.33.rest_0_.refs_11_), channel_id=1, source_target_pairs={{0,6},{1,7},{2,0},{3,1},{4,2},{5,3},{6,4},{7,5},{8,14},{9,15},{10,... | collective-permute-start | bytes 786440 | tf_op jit(solution)/shard_map/ppermute | solution.py:370
  10.4 38.8 %collective-permute-start.7 = (bf16[4,256,128]{2,1,0:T(8,128)(2,1)S(1)}, bf16[4,256,128]{2,1,0:T(8,128)(2,1)S(1)}, u32[]{:S(2)}, u32[]{:S(2)}) collective-permute-start(bf16[4,256,128]{2,1,0:T(8,128)(2,1)S(1)} %get-tuple-element.33.rest_0_.refs_11_), channel_id=1, source_target_pairs={{0,1},{1,0},{2,3},{3,2},{4,5},{5,4},{6,7},{7,6},{8,9},{9,8},{10,11... | collective-permute-start | bytes 786440 | tf_op jit(solution)/shard_map/ppermute | solution.py:373
  14.9 34.3 %collective-permute-start.11 = (bf16[4,256,128]{2,1,0:T(8,128)(2,1)S(1)}, bf16[4,256,128]{2,1,0:T(8,128)(2,1)S(1)}, u32[]{:S(2)}, u32[]{:S(2)}) collective-permute-start(bf16[4,256,128]{2,1,0:T(8,128)(2,1)S(1)} %collective-permute-done.10.rest_4_), channel_id=1, source_target_pairs={{0,1},{1,0},{2,3},{3,2},{4,5},{5,4},{6,7},{7,6},{8,9},{9,8},{10,11... | collective-permute-start | bytes 786440 | tf_op jit(solution)/shard_map/ppermute | solution.py:373
  19.3 29.9 %collective-permute-start.13 = (bf16[4,256,128]{2,1,0:T(8,128)(2,1)S(1)}, bf16[4,256,128]{2,1,0:T(8,128)(2,1)S(1)}, u32[]{:S(2)}, u32[]{:S(2)}) collective-permute-start(bf16[4,256,128]{2,1,0:T(8,128)(2,1)S(1)} %collective-permute-done.12.rest_6_), channel_id=1, source_target_pairs={{0,1},{1,0},{2,3},{3,2},{4,5},{5,4},{6,7},{7,6},{8,9},{9,8},{10,11... | collective-permute-start | bytes 786440 | tf_op jit(solution)/shard_map/ppermute | solution.py:373
  19.4 29.8 %collective-permute-start.9 = (bf16[4,256,128]{2,1,0:T(8,128)(2,1)S(1)}, bf16[4,256,128]{2,1,0:T(8,128)(2,1)S(1)}, u32[]{:S(2)}, u32[]{:S(2)}) collective-permute-start(bf16[4,256,128]{2,1,0:T(8,128)(2,1)S(1)} %collective-permute-done.8.rest_2_), channel_id=1, source_target_pairs={{0,1},{1,0},{2,3},{3,2},{4,5},{5,4},{6,7},{7,6},{8,9},{9,8},{10,11... | collective-permute-start | bytes 786440 | tf_op jit(solution)/shard_map/ppermute | solution.py:373
  53.6 29.0 %collective-permute-start.29 = (bf16[2,2,272,128]{3,2,1,0:T(8,128)(2,1)S(1)}, bf16[2,2,272,128]{3,2,1,0:T(8,128)(2,1)S(1)}, u32[]{:S(2)}, u32[]{:S(2)}) collective-permute-start(bf16[2,2,272,128]{3,2,1,0:T(8,128)(2,1)S(1)} %get-tuple-element.47), channel_id=1, source_target_pairs={{0,64},{8,72},{16,80},{24,88},{32,96},{40,104},{48,112},{56,120},{... | collective-permute-start | bytes 835592 | tf_op jit(solution)/shard_map/ppermute | solution.py:384
  55.3 27.4 %collective-permute-start.30 = (bf16[2,2,272,128]{3,2,1,0:T(8,128)(2,1)S(1)}, bf16[2,2,272,128]{3,2,1,0:T(8,128)(2,1)S(1)}, u32[]{:S(2)}, u32[]{:S(2)}) collective-permute-start(bf16[2,2,272,128]{3,2,1,0:T(8,128)(2,1)S(1)} %get-tuple-element.48), channel_id=1, source_target_pairs={{0,128},{8,136},{16,144},{24,152},{32,160},{40,168},{48,176},{56,1... | collective-permute-start | bytes 835592 | tf_op jit(solution)/shard_map/ppermute | solution.py:384
  57.4 28.9 %collective-permute-start.31 = (bf16[2,2,272,128]{3,2,1,0:T(8,128)(2,1)S(1)}, bf16[2,2,272,128]{3,2,1,0:T(8,128)(2,1)S(1)}, u32[]{:S(2)}, u32[]{:S(2)}) collective-permute-start(bf16[2,2,272,128]{3,2,1,0:T(8,128)(2,1)S(1)} %get-tuple-element.49), channel_id=1, source_target_pairs={{0,192},{8,200},{16,208},{24,216},{32,224},{40,232},{48,240},{56,2... | collective-permute-start | bytes 835592 | tf_op jit(solution)/shard_map/ppermute | solution.py:384
  72.7 16.5 %collective-permute-start.17 = (f32[4,4,4,128]{3,2,1,0:T(4,128)S(1)}, f32[4,4,4,128]{3,2,1,0:T(4,128)S(1)}, u32[]{:S(2)}, u32[]{:S(2)}) collective-permute-start(f32[4,4,4,128]{3,2,1,0:T(4,128)S(1)} %pad_maximum_fusion.down_target), channel_id=1, source_target_pairs={{0,48},{8,56},{16,0},{24,8},{32,16},{40,24},{48,32},{56,40},{64,11... | collective-permute-start | bytes 98312 | tf_op jit(solution)/shard_map/ppermute | solution.py:377
  77.6 11.7 %collective-permute-start.18 = (f32[4,4,4,128]{3,2,1,0:T(4,128)S(1)}, f32[4,4,4,128]{3,2,1,0:T(4,128)S(1)}, u32[]{:S(2)}, u32[]{:S(2)}) collective-permute-start(f32[4,4,4,128]{3,2,1,0:T(4,128)S(1)} %pad_maximum_fusion.down_target), channel_id=1, source_target_pairs={{0,8},{8,16},{16,24},{24,32},{32,40},{40,48},{48,56},{56,0},{64,72... | collective-permute-start | bytes 98312 | tf_op jit(solution)/shard_map/ppermute | solution.py:377
  82.6 9.9 %collective-permute-start.24 = (bf16[2,2,272,128]{3,2,1,0:T(8,128)(2,1)S(1)}, bf16[2,2,272,128]{3,2,1,0:T(8,128)(2,1)S(1)}, u32[]{:S(2)}, u32[]{:S(2)}) collective-permute-start(bf16[2,2,272,128]{3,2,1,0:T(8,128)(2,1)S(1)} %get-tuple-element.43), channel_id=1, source_target_pairs={{0,64},{8,72},{16,80},{24,88},{32,96},{40,104},{48,112},{56,120},{... | collective-permute-start | bytes 835592 | tf_op jit(solution)/shard_map/ppermute | solution.py:384
  82.8 15.0 %collective-permute-start.25 = (bf16[2,2,272,128]{3,2,1,0:T(8,128)(2,1)S(1)}, bf16[2,2,272,128]{3,2,1,0:T(8,128)(2,1)S(1)}, u32[]{:S(2)}, u32[]{:S(2)}) collective-permute-start(bf16[2,2,272,128]{3,2,1,0:T(8,128)(2,1)S(1)} %get-tuple-element.44), channel_id=1, source_target_pairs={{0,128},{8,136},{16,144},{24,152},{32,160},{40,168},{48,176},{56,1... | collective-permute-start | bytes 835592 | tf_op jit(solution)/shard_map/ppermute | solution.py:384
  86.3 12.6 %collective-permute-start.26 = (bf16[2,2,272,128]{3,2,1,0:T(8,128)(2,1)S(1)}, bf16[2,2,272,128]{3,2,1,0:T(8,128)(2,1)S(1)}, u32[]{:S(2)}, u32[]{:S(2)}) collective-permute-start(bf16[2,2,272,128]{3,2,1,0:T(8,128)(2,1)S(1)} %get-tuple-element.45), channel_id=1, source_target_pairs={{0,192},{8,200},{16,208},{24,216},{32,224},{40,232},{48,240},{56,2... | collective-permute-start | bytes 835592 | tf_op jit(solution)/shard_map/ppermute | solution.py:384
  89.2 13.3 %collective-permute-start.32 = (bf16[4,272,128]{2,1,0:T(8,128)(2,1)S(1)}, bf16[4,272,128]{2,1,0:T(8,128)(2,1)S(1)}, u32[]{:S(2)}, u32[]{:S(2)}) collective-permute-start(bf16[4,272,128]{2,1,0:T(8,128)(2,1)S(1)} %get-tuple-element.50), channel_id=1, source_target_pairs={{0,8},{8,16},{16,24},{24,32},{32,40},{40,48},{48,56},{56,0},{64,72... | collective-permute-start | bytes 835592 | tf_op jit(solution)/shard_map/ppermute | solution.py:392
  89.3 14.2 %collective-permute-start.33 = (bf16[4,272,128]{2,1,0:T(8,128)(2,1)S(1)}, bf16[4,272,128]{2,1,0:T(8,128)(2,1)S(1)}, u32[]{:S(2)}, u32[]{:S(2)}) collective-permute-start(bf16[4,272,128]{2,1,0:T(8,128)(2,1)S(1)} %get-tuple-element.51), channel_id=1, source_target_pairs={{0,56},{8,0},{16,8},{24,16},{32,24},{40,32},{48,40},{56,48},{64,12... | collective-permute-start | bytes 835592 | tf_op jit(solution)/shard_map/ppermute | solution.py:389
  92.6 12.1 %collective-permute-start.6 = (f32[4,4,4,128]{3,2,1,0:T(4,128)S(1)}, f32[4,4,4,128]{3,2,1,0:T(4,128)S(1)}, u32[]{:S(2)}, u32[]{:S(2)}) collective-permute-start(f32[4,4,4,128]{3,2,1,0:T(4,128)S(1)} %pad_maximum_fusion.down_target), channel_id=1, source_target_pairs={{0,56},{8,0},{16,8},{24,16},{32,24},{40,32},{48,40},{56,48},{64,12... | collective-permute-start | bytes 98312 | tf_op jit(solution)/shard_map/ppermute | solution.py:377
  97.8 14.6 %collective-permute-start.19 = (bf16[2,2,272,128]{3,2,1,0:T(8,128)(2,1)S(1)}, bf16[2,2,272,128]{3,2,1,0:T(8,128)(2,1)S(1)}, u32[]{:S(2)}, u32[]{:S(2)}) collective-permute-start(bf16[2,2,272,128]{3,2,1,0:T(8,128)(2,1)S(1)} %get-tuple-element.39), channel_id=1, source_target_pairs={{0,64},{8,72},{16,80},{24,88},{32,96},{40,104},{48,112},{56,120},{... | collective-permute-start | bytes 835592 | tf_op jit(solution)/shard_map/ppermute | solution.py:384
  98.9 14.5 %collective-permute-start.20 = (bf16[2,2,272,128]{3,2,1,0:T(8,128)(2,1)S(1)}, bf16[2,2,272,128]{3,2,1,0:T(8,128)(2,1)S(1)}, u32[]{:S(2)}, u32[]{:S(2)}) collective-permute-start(bf16[2,2,272,128]{3,2,1,0:T(8,128)(2,1)S(1)} %get-tuple-element.40), channel_id=1, source_target_pairs={{0,128},{8,136},{16,144},{24,152},{32,160},{40,168},{48,176},{56,1... | collective-permute-start | bytes 835592 | tf_op jit(solution)/shard_map/ppermute | solution.py:384
  102.5 16.2 %collective-permute-start.21 = (bf16[2,2,272,128]{3,2,1,0:T(8,128)(2,1)S(1)}, bf16[2,2,272,128]{3,2,1,0:T(8,128)(2,1)S(1)}, u32[]{:S(2)}, u32[]{:S(2)}) collective-permute-start(bf16[2,2,272,128]{3,2,1,0:T(8,128)(2,1)S(1)} %get-tuple-element.41), channel_id=1, source_target_pairs={{0,192},{8,200},{16,208},{24,216},{32,224},{40,232},{48,240},{56,2... | collective-permute-start | bytes 835592 | tf_op jit(solution)/shard_map/ppermute | solution.py:384
  104.6 14.1 %collective-permute-start.34 = (bf16[4,272,128]{2,1,0:T(8,128)(2,1)S(1)}, bf16[4,272,128]{2,1,0:T(8,128)(2,1)S(1)}, u32[]{:S(2)}, u32[]{:S(2)}) collective-permute-start(bf16[4,272,128]{2,1,0:T(8,128)(2,1)S(1)} %get-tuple-element.52), channel_id=1, source_target_pairs={{0,8},{8,16},{16,24},{24,32},{32,40},{40,48},{48,56},{56,0},{64,72... | collective-permute-start | bytes 835592 | tf_op jit(solution)/shard_map/ppermute | solution.py:392
  104.7 14.0 %collective-permute-start.35 = (bf16[4,272,128]{2,1,0:T(8,128)(2,1)S(1)}, bf16[4,272,128]{2,1,0:T(8,128)(2,1)S(1)}, u32[]{:S(2)}, u32[]{:S(2)}) collective-permute-start(bf16[4,272,128]{2,1,0:T(8,128)(2,1)S(1)} %get-tuple-element.53), channel_id=1, source_target_pairs={{0,56},{8,0},{16,8},{24,16},{32,24},{40,32},{48,40},{56,48},{64,12... | collective-permute-start | bytes 835592 | tf_op jit(solution)/shard_map/ppermute | solution.py:389
  112.4 10.8 %collective-permute-start.14 = (bf16[2,2,272,128]{3,2,1,0:T(8,128)(2,1)S(1)}, bf16[2,2,272,128]{3,2,1,0:T(8,128)(2,1)S(1)}, u32[]{:S(2)}, u32[]{:S(2)}) collective-permute-start(bf16[2,2,272,128]{3,2,1,0:T(8,128)(2,1)S(1)} %get-tuple-element.35), channel_id=1, source_target_pairs={{0,64},{8,72},{16,80},{24,88},{32,96},{40,104},{48,112},{56,120},{... | collective-permute-start | bytes 835592 | tf_op jit(solution)/shard_map/ppermute | solution.py:384
  (21 other events, 138.9 us)

commit v2 on v1

v2 whole, which is shorter than its diff:
```python
import functools

import jax
import jax.numpy as jnp
from jax import lax
from jax.experimental import pallas as pl
from jax.experimental.pallas import tpu as pltpu
from jax.sharding import PartitionSpec as P

HEADS = 4
HEAD = 64
FEAT = HEADS * HEAD
BLK = 128
NBD = 4
SLOTS = 2
NY, NZ, NX, NC = 4, 8, 4, 2
LOG_NZ = 3
PIECES = NX * NC
SRC_BLOCKS = NBD * PIECES
OWNERS = NY * NZ
PAIRS = OWNERS * SLOTS
ROWS = FEAT + 16
GATE_COST = 800_000_000
LOG2E = 1.4426950408889634
EMPTY = -(2.0**100)
F32 = jnp.float32
BF16 = jnp.bfloat16
VMEM = pl.BlockSpec(memory_space=pltpu.VMEM)
ANY = pl.BlockSpec(memory_space=pl.ANY)


def params(**more):
    return pltpu.CompilerParams(vmem_limit_bytes=48 * 1024 * 1024, **more)


def leaky(values):
    return jnp.maximum(values, 0.2 * values)


def y_from(k):
    return [(y * NZ + z, (y - k) % NY * NZ + z) for y in range(NY) for z in range(NZ)]


def z_from(k):
    return [(y * NZ + z, y * NZ + (z - k) % NZ) for y in range(NY) for z in range(NZ)]


def x_from(k):
    return [(x * NC + c, (x - k) % NX * NC + c) for x in range(NX) for c in range(NC)]


def core_from(k):
    return [(x * NC + c, x * NC + (c - k) % NC) for x in range(NX) for c in range(NC)]


PLAN = ((4,), (3, -3), (2, -2), (1, -1), (0,))


def head_sums(products):
    return jnp.concatenate(
        [jnp.sum(products[h * HEAD : (h + 1) * HEAD], axis=0, keepdims=True) for h in range(HEADS)],
        axis=0,
    )


def prepare_kernel(x_ref, src_hbm, dst_hbm, hidden_ref, target_ref, self_ref, att_ref, src_ref, dst_ref, sems):
    copies = [
        pltpu.make_async_copy(src_hbm, src_ref, sems.at[0]),
        pltpu.make_async_copy(dst_hbm, dst_ref, sems.at[1]),
    ]
    for copy in copies:
        copy.start()
    for copy in copies:
        copy.wait()
    att_src = jnp.broadcast_to(src_ref[...] * LOG2E, (BLK, FEAT)).T
    att_dst = jnp.broadcast_to(dst_ref[...] * LOG2E, (BLK, FEAT)).T
    att_ref[...] = att_src
    for b in range(NBD):
        wide = x_ref[b * BLK : (b + 1) * BLK, :].astype(F32).T
        hidden_ref[b] = wide.astype(BF16)
        source = head_sums(wide * att_src)
        target = head_sums(wide * att_dst)
        target_ref[b] = target
        self_ref[b] = leaky(target + source)


def prepare(hidden, att_src, att_dst):
    return pl.pallas_call(
        prepare_kernel,
        out_shape=(
            jax.ShapeDtypeStruct((NBD, FEAT, BLK), BF16),
            jax.ShapeDtypeStruct((NBD, HEADS, BLK), F32),
            jax.ShapeDtypeStruct((NBD, HEADS, BLK), F32),
            jax.ShapeDtypeStruct((FEAT, BLK), F32),
        ),
        in_specs=[VMEM, ANY, ANY],
        out_specs=(VMEM,) * 4,
        scratch_shapes=[
            pltpu.VMEM((1, FEAT), F32),
            pltpu.VMEM((1, FEAT), F32),
            pltpu.SemaphoreType.DMA((2,)),
        ],
        compiler_params=params(),
        name="prepare",
    )(hidden, att_src.reshape(1, FEAT), att_dst.reshape(1, FEAT))


def gate_kernel(*refs):
    refs[-1][...] = jnp.zeros((8, BLK), F32)


def gate(pieces):
    return pl.pallas_call(
        gate_kernel,
        out_shape=jax.ShapeDtypeStruct((8, BLK), F32),
        in_specs=[ANY] * PIECES,
        out_specs=VMEM,
        compiler_params=params(),
        cost_estimate=pl.CostEstimate(flops=GATE_COST, bytes_accessed=1000, transcendentals=0),
        name="gate",
    )(*pieces)


def owner_of(scal, k, offset):
    src = scal[PAIRS]
    return ((((src >> LOG_NZ) + k) & (NY - 1)) << LOG_NZ) | ((src + offset) & (NZ - 1))


def halves(values):
    high = values.astype(BF16).astype(F32)
    return high, (values - high).astype(BF16).astype(F32)


def slot_partial(hidden, att, bias, target, out_ref, place):
    sources = head_sums(hidden.astype(F32) * att)
    sources = jnp.concatenate([sources, sources], axis=0).T
    bounds, totals = [], []
    for h in range(HEADS):
        masked = sources[:, h : h + 1] + bias
        top = jnp.max(masked, axis=0, keepdims=True)
        own = target[h : h + 1]
        high, low = halves(leaky(own + top))
        bound = high + low
        weights = jnp.exp2(
            jnp.maximum(masked + (own - bound), 0.2 * masked + (0.2 * own - bound))
        )
        bounds.append((high, low))
        totals.append(halves(jnp.sum(weights, axis=0, keepdims=True)))
        out_ref[place + (pl.ds(h * HEAD, HEAD), slice(None))] = jnp.dot(
            hidden[h * HEAD : (h + 1) * HEAD], weights.astype(BF16), preferred_element_type=F32
        ).astype(BF16)
    rows = [b[0] for b in bounds] + [t[0] for t in totals]
    rows += [b[1] for b in bounds] + [t[1] for t in totals]
    out_ref[place + (pl.ds(FEAT, 16), slice(None))] = jnp.concatenate(rows, axis=0).astype(BF16)


def slots_kernel(offsets, first, scal, token, targets, att, *rest):
    del token
    n_own, n_in = len(offsets), PIECES if first else 1
    masks, sources, rest = rest[:n_own], rest[n_own : n_own + n_in], rest[n_own + n_in :]
    step = pl.program_id(0)
    if first:
        *outs, hidden, made, sems = rest

        @pl.when(step == 0)
        def _():
            copies = [
                pltpu.make_async_copy(sources[n], hidden.at[pl.ds(n * NBD, NBD)], sems.at[n])
                for n in range(PIECES)
            ]
            for copy in copies:
                copy.start()
            for copy in copies:
                copy.wait()

    else:
        (hidden,), (*outs, made) = sources, rest
    for n, (offset, mask) in enumerate(zip(offsets, masks, strict=True)):
        owner = owner_of(scal, step, offset)
        for t in range(SLOTS):
            pair = scal[owner * SLOTS + t]
            block = pair & (SRC_BLOCKS - 1)
            place = pair >> (SRC_BLOCKS.bit_length() - 1)
            holder = block >> (NBD.bit_length() - 1)
            dst = scal[PAIRS + 1]
            dx = ((holder >> 1) - (dst >> 1)) & (NX - 1)
            dc = (holder ^ dst) & (NC - 1)
            held = ((dx * NC + dc) * NBD) | (block & (NBD - 1))
            bias = jnp.where(mask[0, t] > 0, 0.0, EMPTY).astype(F32).T
            slot_partial(hidden[held], att[...], bias, targets[owner, place], made, (n, t))

    for k in range(NY):

        @pl.when(step == k)
        def _(k=k):
            outs[k][...] = made[...]


def slots(offsets, scal, token, masks, targets, att, source):
    first = isinstance(source, list)

    def mask_spec(offset):
        return pl.BlockSpec(
            (1, SLOTS, BLK, BLK), lambda i, scal: (owner_of(scal, i, offset), 0, 0, 0)
        )

    shape = (len(offsets), SLOTS, ROWS, BLK)
    out_shape = (jax.ShapeDtypeStruct(shape, BF16),) * NY
    scratch = [pltpu.VMEM(shape, BF16)]
    if first:
        out_shape += (jax.ShapeDtypeStruct((SRC_BLOCKS, FEAT, BLK), BF16),)
        scratch.append(pltpu.SemaphoreType.DMA((PIECES,)))
    return pl.pallas_call(
        functools.partial(slots_kernel, offsets, first),
        out_shape=out_shape,
        grid_spec=pltpu.PrefetchScalarGridSpec(
            num_scalar_prefetch=1,
            grid=(NY,),
            in_specs=[ANY, VMEM, VMEM]
            + [mask_spec(offset) for offset in offsets]
            + ([ANY] * PIECES if first else [VMEM]),
            out_specs=(VMEM,) * len(out_shape),
            scratch_shapes=scratch,
        ),
        compiler_params=params(),
        cost_estimate=pl.CostEstimate(flops=1000, bytes_accessed=1000, transcendentals=0),
        name="slots",
    )(scal, token, targets, att, *[masks] * len(offsets), *(source if first else [source]))


def bound_total(ref, place):
    rows = ref[place + (pl.ds(FEAT, 16), slice(None))].astype(F32)
    both = rows[:8] + rows[8:]
    return both[:HEADS], both[HEADS:]


def merge(slot_list, dense, bounds, totals, sums, given=None):
    for b in range(NBD):
        top = jnp.full((HEADS, BLK), EMPTY, F32) if given is None else given[0][b]
        for ref in dense:
            top = jnp.maximum(top, bound_total(ref, (b,))[0])
        bounds[b] = top
    for ref, index, place in slot_list:
        bounds[place] = jnp.maximum(bounds[place], bound_total(ref, index)[0])
    for b in range(NBD):
        total = jnp.zeros((HEADS, BLK), F32)
        terms = []
        if given is not None:
            factor = jnp.exp2(given[0][b] - bounds[b])
            total += factor if given[1] is None else given[1][b] * factor
            terms.append((given[2], (b,), factor))
        for ref in dense:
            bound, more = bound_total(ref, (b,))
            factor = jnp.exp2(bound - bounds[b])
            total += more * factor
            terms.append((ref, (b,), factor))
        totals[b] = total
        for h in range(HEADS):
            rows = pl.ds(h * HEAD, HEAD)
            value = jnp.zeros((HEAD, BLK), F32)
            for ref, index, factor in terms:
                value += ref[index + (rows, slice(None))].astype(F32) * factor[h : h + 1]
            sums[b, rows, :] = value
    for ref, index, place in slot_list:
        bound, more = bound_total(ref, index)
        factor = jnp.exp2(bound - bounds[place])
        totals[place] += more * factor
        for h in range(HEADS):
            rows = pl.ds(h * HEAD, HEAD)
            sums[place, rows, :] += (
                ref[index + (rows, slice(None))].astype(F32) * factor[h : h + 1]
            )


def placed(scal, every_pair, offset, refs, n):
    owner = owner_of(scal, 0, offset)
    found = []
    for k in range(NY):
        for t in range(SLOTS):
            place = every_pair[k, owner * SLOTS + t] >> (SRC_BLOCKS.bit_length() - 1)
            found.append((refs[k], (n, t), place))
    return found


def write_dense(out, bounds, totals, sums):
    for b in range(NBD):
        out[b, pl.ds(0, FEAT), :] = sums[b].astype(BF16)
        both = halves(jnp.concatenate([bounds[b], totals[b]], axis=0))
        out[b, pl.ds(FEAT, 16), :] = jnp.concatenate(both, axis=0).astype(BF16)


def merge_kernel(work, scal, every_pair, *refs):
    parts, refs = refs[:NY], refs[NY:]
    n_dense = sum(w[1] for w in work)
    dense, refs = refs[:n_dense], refs[n_dense:]
    outs, (bounds, totals, sums) = refs[: len(work)], refs[len(work) :]
    for n, (out, (offset, count)) in enumerate(zip(outs, work, strict=True)):
        mine, dense = dense[:count], dense[count:]
        merge(placed(scal, every_pair, offset, parts, n), mine, bounds, totals, sums)
        write_dense(out, bounds, totals, sums)


SUMS = ((NBD, HEADS, BLK), (NBD, HEADS, BLK), (NBD, FEAT, BLK))
SMEM = pl.BlockSpec(memory_space=pltpu.SMEM)


def merge_group(work, scal, every_pair, parts, dense):
    return pl.pallas_call(
        functools.partial(merge_kernel, work),
        out_shape=(jax.ShapeDtypeStruct((NBD, ROWS, BLK), BF16),) * len(work),
        in_specs=[SMEM] * 2 + [VMEM] * (NY + len(dense)),
        out_specs=(VMEM,) * len(work),
        scratch_shapes=[pltpu.VMEM(shape, F32) for shape in SUMS],
        compiler_params=params(),
        cost_estimate=pl.CostEstimate(flops=1000, bytes_accessed=1000, transcendentals=0),
        name="merge",
    )(scal, every_pair, *parts, *dense)


def home_kernel(scal, every_pair, *refs):
    parts, (self_ref, hidden_ref, bounds, totals, sums) = refs[:NY], refs[NY:]
    found = placed(scal, every_pair, 0, parts, 0)
    merge(found, (), bounds, totals, sums, (self_ref, None, hidden_ref))


def merge_home(scal, every_pair, parts, self_logit, hidden):
    return pl.pallas_call(
        home_kernel,
        out_shape=tuple(jax.ShapeDtypeStruct(shape, F32) for shape in SUMS),
        in_specs=[SMEM] * 2 + [VMEM] * (NY + 2),
        out_specs=(VMEM,) * 3,
        compiler_params=params(),
        cost_estimate=pl.CostEstimate(flops=1000, bytes_accessed=1000, transcendentals=0),
        name="merge_home",
    )(scal, every_pair, *parts, self_logit, hidden)


def finish_kernel(up, down, home_bounds, home_totals, home_sums, bias_ref, out, bounds, totals, sums):
    merge((), (up, down), bounds, totals, sums, (home_bounds, home_totals, home_sums))
    for b in range(NBD):
        scale = 1.0 / totals[b]
        value = jnp.concatenate(
            [sums[b, pl.ds(h * HEAD, HEAD), :] * scale[h : h + 1] for h in range(HEADS)], axis=0
        )
        value = value.T + bias_ref[...]
        out[pl.ds(b * BLK, BLK), :] = jnp.where(
            value > 0, value, jnp.exp(jnp.minimum(value, 0.0)) - 1.0
        )


def finish(up, down, home, bias):
    return pl.pallas_call(
        finish_kernel,
        out_shape=jax.ShapeDtypeStruct((NBD * BLK, FEAT), F32),
        in_specs=[VMEM] * 6,
        out_specs=VMEM,
        scratch_shapes=[pltpu.VMEM(shape, F32) for shape in SUMS],
        compiler_params=params(),
        name="finish",
    )(up, down, *home, bias.reshape(1, FEAT))


def body(features, weight, att_src, att_dst, bias, block_pairs, edge_masks):
    masks = edge_masks.reshape(OWNERS, SLOTS, BLK, BLK)
    hidden = jnp.dot(features, weight, preferred_element_type=F32).astype(BF16)
    hidden, own_target, self_logit, att = prepare(hidden, att_src, att_dst)
    along_x = [hidden] + [lax.ppermute(hidden, "dst", x_from(k)) for k in range(1, NX)]

    src = lax.axis_index("src")
    dst = lax.axis_index("dst")
    pairs = block_pairs.reshape(-1)
    scal = jnp.concatenate([pairs, jnp.stack([src, dst]).astype(jnp.int32)])

    told = jnp.broadcast_to(own_target[None], (OWNERS,) + own_target.shape)
    told = lax.all_to_all(told, "src", 0, 0)

    pieces = []
    for piece in along_x:
        pieces += [piece, lax.ppermute(piece, "dst", core_from(1))]
    pairs, pieces[-1] = lax.optimization_barrier((pairs, pieces[-1]))
    every_pair = jnp.stack([pairs] + [lax.ppermute(pairs, "src", y_from(-k)) for k in range(1, NY)])
    token = gate(pieces)
    scal, every_pair = lax.optimization_barrier((scal, every_pair))

    up, down = (), ()
    made, parts = [], []
    source = pieces
    for step, offsets in enumerate(PLAN):
        made.append(slots(offsets, scal, token, masks, told, att, source))
        if step == 0:
            source = made[0][NY]
        parts.append(
            [made[-1][0]] + [lax.ppermute(made[-1][k], "src", y_from(-k)) for k in range(1, NY)]
        )
    for step, offsets in enumerate(PLAN[:-1]):
        work = [(offsets[0], len(up))] + [(offset, len(down)) for offset in offsets[1:]]
        if step == len(PLAN) - 2:
            parts[step][0], parts[step + 1][1] = lax.optimization_barrier(
                (parts[step][0], parts[step + 1][1])
            )
        sent = merge_group(work, scal, every_pair, parts[step], up + down)
        up = (lax.ppermute(sent[0], "src", z_from(-1)),)
        if len(sent) > 1:
            down = (lax.ppermute(sent[1], "src", z_from(1)),)
    home = merge_home(scal, every_pair, parts[-1], self_logit, hidden)
    return finish(up[0], down[0], home, bias)


def solution(mesh):
    placed_at = (
        P(("dst", "src"), None),
        P(),
        P(),
        P(),
        P(),
        P("src", "dst", None, None),
        P("src", "dst", None, None, None, None),
    )
    return jax.shard_map(
        body, mesh=mesh, in_specs=placed_at, out_specs=P(("dst", "src"), None), check_vma=False
    )
```

time: 140 us -> 112 us (0.80)
  the two profiles are of different devices: /device:TPU:8 before, /device:TPU:6 now
where the time goes in v2:
time: 112 us; the launch traced here: 111 us
  starting transfers between devices  59.2 us (53%)
  Pallas kernels  30.4 us (27%)
  waiting for transfers between devices  15.7 us (14%)
  local copies, waits for them, and re-layouts  4.09 us (4%)
  matrix products  1.36 us (1%)
    pallas_call x5, Pallas kernels, slots(): pl.pallas_call(functools.partial(slots_kernel, offsets, first), out_shape...  24.2 us
    ppermute x15, starting transfers between devices, body(): lax.ppermute(made[-1][k], 'src', y_from(-k))  23 us
    all_to_all x1, starting transfers between devices, body(): told = lax.all_to_all(told, 'src', 0, 0)  11.1 us
    ppermute x3, starting transfers between devices, body(): down = (lax.ppermute(sent[1], 'src', z_from(1)),)  10.8 us
    ppermute x15, waiting for transfers between devices, body(): lax.ppermute(made[-1][k], 'src', y_from(-k))  6.26 us
    ppermute x4, waiting for transfers between devices, body(): up = (lax.ppermute(sent[0], 'src', z_from(-1)),)  6.01 us
    ppermute x3, starting transfers between devices, body(): lax.ppermute(pairs, 'src', y_from(-k))  5.96 us
    pallas_call x4, Pallas kernels, merge_group(): pl.pallas_call(functools.partial(merge_kernel, work), out_shape=(jax.Shap...  4.01 us
  transfers between devices with their start and end apart: 33, of which 8 were waited for; matrix products, arithmetic and copies ran while one was open for 2% of the time, Pallas kernels for 21%

profile of v2, /device:TPU:6, one launch (start us, length us, event | category | flops | bytes accessed | tf_op | source)
XLA Modules:
  0.0 111.2 jit_solution(18221141174475922642)
XLA Ops:
  4.2 2.3 %collective-permute-start = (bf16[4,256,128]{2,1,0:T(8,128)(2,1)S(1)}, bf16[4,256,128]{2,1,0:T(8,128)(2,1)S(1)}, u32[]{:S(2)}, u32[]{:S(2)}) collective-permute-start(bf16[4,256,128]{2,1,0:T(8,128)(2,1)S(1)} %get-tuple-element.45.refs_0_.rest_1_.refs_5_), channel_id=1, source_target_pairs={{0,2},{1,3},{2,4},{3,5},{4,6},{5,7},{6,0},{7,1},{8,10},{9,11},{10,... | collective-permute-start | bytes 786440 | tf_op jit(solution)/shard_map/ppermute | solution.py:367
  6.5 1.6 %collective-permute-start.8 = (bf16[4,256,128]{2,1,0:T(8,128)(2,1)S(1)}, bf16[4,256,128]{2,1,0:T(8,128)(2,1)S(1)}, u32[]{:S(2)}, u32[]{:S(2)}) collective-permute-start(bf16[4,256,128]{2,1,0:T(8,128)(2,1)S(1)} %get-tuple-element.45.refs_0_.rest_1_.refs_5_), channel_id=1, source_target_pairs={{0,4},{1,5},{2,6},{3,7},{4,0},{5,1},{6,2},{7,3},{8,12},{9,13},{10,... | collective-permute-start | bytes 786440 | tf_op jit(solution)/shard_map/ppermute | solution.py:367
  8.7 11.1 %all-to-all-start = ((f32[32,4,4,128]{3,2,1,0:T(4,128)}), f32[32,4,4,128]{3,2,1,0:T(4,128)S(1)}, u32[]{:S(2)}, u32[]{:S(2)}) async-start(f32[32,4,4,128]{3,2,1,0:T(4,128)} %broadcast_in_dim.2), calls=%async_computation | async-start | bytes 524288 | tf_op jit(solution)/shard_map/all_to_all | solution.py:375
  22.0 1.8 %collective-permute-start.2 = (s32[64]{0:T(128)S(1)}, s32[64]{0:T(128)S(1)}, u32[]{:S(2)}, u32[]{:S(2)}) collective-permute-start(s32[64]{0:T(128)S(1)} %reshape.16), channel_id=1, source_target_pairs={{0,64},{8,72},{16,80},{24,88},{32,96},{40,104},{48,112},{56,120},{... | collective-permute-start | bytes 776 | tf_op jit(solution)/shard_map/ppermute | solution.py:381
  23.8 2.7 %collective-permute-start.3 = (s32[64]{0:T(128)S(1)}, s32[64]{0:T(128)S(1)}, u32[]{:S(2)}, u32[]{:S(2)}) collective-permute-start(s32[64]{0:T(128)S(1)} %reshape.16), channel_id=1, source_target_pairs={{0,128},{8,136},{16,144},{24,152},{32,160},{40,168},{48,176},{56,1... | collective-permute-start | bytes 776 | tf_op jit(solution)/shard_map/ppermute | solution.py:381
  31.4 4.6 %slots.5 = (bf16[1,2,272,128]{3,2,1,0:T(8,128)(2,1)S(1)}, bf16[1,2,272,128]{3,2,1,0:T(8,128)(2,1)S(1)}, bf16[1,2,272,128]{3,2,1,0:T(8,128)(2,1)S(1)}, bf16[1,2,2...) custom-call(s32[66]{0:T(128)S(1)} %pad_add_fusion.1.scal, f32[8,128]{1,0:T(8,128)S(1)} %gate.1.token, ...), custom_call_target="tpu_custom_call" | custom-call | flops 1000 | bytes 1000 | tf_op jit(solution)/shard_map/slots/pallas_call | solution.py:213
  36.7 2.2 %collective-permute-start.21 = (bf16[1,2,272,128]{3,2,1,0:T(8,128)(2,1)S(1)}, bf16[1,2,272,128]{3,2,1,0:T(8,128)(2,1)S(1)}, u32[]{:S(2)}, u32[]{:S(2)}) collective-permute-start(bf16[1,2,272,128]{3,2,1,0:T(8,128)(2,1)S(1)} %get-tuple-element.69), channel_id=1, source_target_pairs={{0,128},{8,136},{16,144},{24,152},{32,160},{40,168},{48,176},{56,1... | collective-permute-start | bytes 417800 | tf_op jit(solution)/shard_map/ppermute | solution.py:393
  40.3 5.1 %slots.9 = (bf16[2,2,272,128]{3,2,1,0:T(8,128)(2,1)S(1)}, bf16[2,2,272,128]{3,2,1,0:T(8,128)(2,1)S(1)}, bf16[2,2,272,128]{3,2,1,0:T(8,128)(2,1)S(1)}, bf16[2,2,272,128]{3,2,1,0:T(8,128)(2,1)S(1)}) custom-call(s32[66]{0:T(128)S(1)} %pad_add_fusion.1.scal, f32[8,128]{1,0:T(8,128)S(1)} %gate.1.token, f32[32,4,4,128]{3,2,1,0:T(4,128)S(1)} %all-to-all-done.targets, ...), custom_call_target="tpu_custom_call" | custom-call | flops 1000 | bytes 1000 | tf_op jit(solution)/shard_map/slots/pallas_call | solution.py:213
  46.1 1.6 %collective-permute-start.18 = (bf16[2,2,272,128]{3,2,1,0:T(8,128)(2,1)S(1)}, bf16[2,2,272,128]{3,2,1,0:T(8,128)(2,1)S(1)}, u32[]{:S(2)}, u32[]{:S(2)}) collective-permute-start(bf16[2,2,272,128]{3,2,1,0:T(8,128)(2,1)S(1)} %get-tuple-element.65), channel_id=1, source_target_pairs={{0,128},{8,136},{16,144},{24,152},{32,160},{40,168},{48,176},{56,1... | collective-permute-start | bytes 835592 | tf_op jit(solution)/shard_map/ppermute | solution.py:393
  47.7 2.4 %collective-permute-start.19 = (bf16[2,2,272,128]{3,2,1,0:T(8,128)(2,1)S(1)}, bf16[2,2,272,128]{3,2,1,0:T(8,128)(2,1)S(1)}, u32[]{:S(2)}, u32[]{:S(2)}) collective-permute-start(bf16[2,2,272,128]{3,2,1,0:T(8,128)(2,1)S(1)} %get-tuple-element.66), channel_id=1, source_target_pairs={{0,192},{8,200},{16,208},{24,216},{32,224},{40,232},{48,240},{56,2... | collective-permute-start | bytes 835592 | tf_op jit(solution)/shard_map/ppermute | solution.py:393
  50.9 1.8 %collective-permute-start.23 = (bf16[4,272,128]{2,1,0:T(8,128)(2,1)S(1)}, bf16[4,272,128]{2,1,0:T(8,128)(2,1)S(1)}, u32[]{:S(2)}, u32[]{:S(2)}) collective-permute-start(bf16[4,272,128]{2,1,0:T(8,128)(2,1)S(1)} %merge.4), channel_id=1, source_target_pairs={{0,8},{8,16},{16,24},{24,32},{32,40},{40,48},{48,56},{56,0},{64,72... | collective-permute-start | bytes 835592 | tf_op jit(solution)/shard_map/ppermute | solution.py:402
  52.7 5.1 %slots.8 = (bf16[2,2,272,128]{3,2,1,0:T(8,128)(2,1)S(1)}, bf16[2,2,272,128]{3,2,1,0:T(8,128)(2,1)S(1)}, bf16[2,2,272,128]{3,2,1,0:T(8,128)(2,1)S(1)}, bf16[2,2,272,128]{3,2,1,0:T(8,128)(2,1)S(1)}) custom-call(s32[66]{0:T(128)S(1)} %pad_add_fusion.1.scal, f32[8,128]{1,0:T(8,128)S(1)} %gate.1.token, f32[32,4,4,128]{3,2,1,0:T(4,128)S(1)} %all-to-all-done.targets, ...), custom_call_target="tpu_custom_call" | custom-call | flops 1000 | bytes 1000 | tf_op jit(solution)/shard_map/slots/pallas_call | solution.py:213
  59.3 2.5 %collective-permute-start.16 = (bf16[2,2,272,128]{3,2,1,0:T(8,128)(2,1)S(1)}, bf16[2,2,272,128]{3,2,1,0:T(8,128)(2,1)S(1)}, u32[]{:S(2)}, u32[]{:S(2)}) collective-permute-start(bf16[2,2,272,128]{3,2,1,0:T(8,128)(2,1)S(1)} %get-tuple-element.62), channel_id=1, source_target_pairs={{0,192},{8,200},{16,208},{24,216},{32,224},{40,232},{48,240},{56,2... | collective-permute-start | bytes 835592 | tf_op jit(solution)/shard_map/ppermute | solution.py:393
  64.1 4.3 %collective-permute-start.25 = (bf16[4,272,128]{2,1,0:T(8,128)(2,1)S(1)}, bf16[4,272,128]{2,1,0:T(8,128)(2,1)S(1)}, u32[]{:S(2)}, u32[]{:S(2)}) collective-permute-start(bf16[4,272,128]{2,1,0:T(8,128)(2,1)S(1)} %get-tuple-element.72), channel_id=1, source_target_pairs={{0,56},{8,0},{16,8},{24,16},{32,24},{40,32},{48,40},{56,48},{64,12... | collective-permute-start | bytes 835592 | tf_op jit(solution)/shard_map/ppermute | solution.py:404
  68.4 4.4 %slots.7 = (bf16[1,2,272,128]{3,2,1,0:T(8,128)(2,1)S(1)}, bf16[1,2,272,128]{3,2,1,0:T(8,128)(2,1)S(1)}, bf16[1,2,272,128]{3,2,1,0:T(8,128)(2,1)S(1)}, bf16[1,2,272,128]{3,2,1,0:T(8,128)(2,1)S(1)}) custom-call(s32[66]{0:T(128)S(1)} %pad_add_fusion.1.scal, f32[8,128]{1,0:T(8,128)S(1)} %gate.1.token, f32[32,4,4,128]{3,2,1,0:T(4,128)S(1)} %all-to-all-done.targets, ...), custom_call_target="tpu_custom_call" | custom-call | flops 1000 | bytes 1000 | tf_op jit(solution)/shard_map/slots/pallas_call | solution.py:213
  72.8 2.1 %collective-permute-start.10 = (bf16[1,2,272,128]{3,2,1,0:T(8,128)(2,1)S(1)}, bf16[1,2,272,128]{3,2,1,0:T(8,128)(2,1)S(1)}, u32[]{:S(2)}, u32[]{:S(2)}) collective-permute-start(bf16[1,2,272,128]{3,2,1,0:T(8,128)(2,1)S(1)} %get-tuple-element.54), channel_id=1, source_target_pairs={{0,64},{8,72},{16,80},{24,88},{32,96},{40,104},{48,112},{56,120},{... | collective-permute-start | bytes 417800 | tf_op jit(solution)/shard_map/ppermute | solution.py:393
  74.9 5.1 %slots.6 = (bf16[2,2,272,128]{3,2,1,0:T(8,128)(2,1)S(1)}, bf16[2,2,272,128]{3,2,1,0:T(8,128)(2,1)S(1)}, bf16[2,2,272,128]{3,2,1,0:T(8,128)(2,1)S(1)}, bf16[2,2,272,128]{3,2,1,0:T(8,128)(2,1)S(1)}) custom-call(s32[66]{0:T(128)S(1)} %pad_add_fusion.1.scal, f32[8,128]{1,0:T(8,128)S(1)} %gate.1.token, f32[32,4,4,128]{3,2,1,0:T(4,128)S(1)} %all-to-all-done.targets, ...), custom_call_target="tpu_custom_call" | custom-call | flops 1000 | bytes 1000 | tf_op jit(solution)/shard_map/slots/pallas_call | solution.py:213
  80.1 3.7 %collective-permute-start.12 = (bf16[2,2,272,128]{3,2,1,0:T(8,128)(2,1)S(1)}, bf16[2,2,272,128]{3,2,1,0:T(8,128)(2,1)S(1)}, u32[]{:S(2)}, u32[]{:S(2)}) collective-permute-start(bf16[2,2,272,128]{3,2,1,0:T(8,128)(2,1)S(1)} %get-tuple-element.57), channel_id=1, source_target_pairs={{0,128},{8,136},{16,144},{24,152},{32,160},{40,168},{48,176},{56,1... | collective-permute-start | bytes 835592 | tf_op jit(solution)/shard_map/ppermute | solution.py:393
  83.8 2.5 %collective-permute-start.13 = (bf16[2,2,272,128]{3,2,1,0:T(8,128)(2,1)S(1)}, bf16[2,2,272,128]{3,2,1,0:T(8,128)(2,1)S(1)}, u32[]{:S(2)}, u32[]{:S(2)}) collective-permute-start(bf16[2,2,272,128]{3,2,1,0:T(8,128)(2,1)S(1)} %get-tuple-element.58), channel_id=1, source_target_pairs={{0,192},{8,200},{16,208},{24,216},{32,224},{40,232},{48,240},{56,2... | collective-permute-start | bytes 835592 | tf_op jit(solution)/shard_map/ppermute | solution.py:393
  87.8 3.2 %collective-permute-start.27 = (bf16[4,272,128]{2,1,0:T(8,128)(2,1)S(1)}, bf16[4,272,128]{2,1,0:T(8,128)(2,1)S(1)}, u32[]{:S(2)}, u32[]{:S(2)}) collective-permute-start(bf16[4,272,128]{2,1,0:T(8,128)(2,1)S(1)} %get-tuple-element.74), channel_id=1, source_target_pairs={{0,56},{8,0},{16,8},{24,16},{32,24},{40,32},{48,40},{56,48},{64,12... | collective-permute-start | bytes 835592 | tf_op jit(solution)/shard_map/ppermute | solution.py:404
  92.2 6.0 %collective-permute-done.26.refs_4_ = bf16[4,272,128]{2,1,0:T(8,128)(2,1)S(1)} collective-permute-done((bf16[4,272,128]{2,1,0:T(8,128)(2,1)S(1)}, bf16[4,272,128]{2,1,0:T(8,128)(2,1)S(1)}, u32[]{:S(2)}, u32[]{:S(2)}) %collective-permute-start.26) | collective-permute-done | bytes 278560 | tf_op jit(solution)/shard_map/ppermute | solution.py:402
  99.4 3.2 %collective-permute-start.29 = (bf16[4,272,128]{2,1,0:T(8,128)(2,1)S(1)}, bf16[4,272,128]{2,1,0:T(8,128)(2,1)S(1)}, u32[]{:S(2)}, u32[]{:S(2)}) collective-permute-start(bf16[4,272,128]{2,1,0:T(8,128)(2,1)S(1)} %get-tuple-element.76), channel_id=1, source_target_pairs={{0,56},{8,0},{16,8},{24,16},{32,24},{40,32},{48,40},{56,48},{64,12... | collective-permute-start | bytes 835592 | tf_op jit(solution)/shard_map/ppermute | solution.py:404
  102.6 2.3 %collective-permute-start.31 = (bf16[1,2,272,128]{3,2,1,0:T(8,128)(2,1)S(1)}, bf16[1,2,272,128]{3,2,1,0:T(8,128)(2,1)S(1)}, u32[]{:S(2)}, u32[]{:S(2)}) collective-permute-start(bf16[1,2,272,128]{3,2,1,0:T(8,128)(2,1)S(1)} %get-tuple-element.80), channel_id=1, source_target_pairs={{0,192},{8,200},{16,208},{24,216},{32,224},{40,232},{48,240},{56,2... | collective-permute-start | bytes 417800 | tf_op jit(solution)/shard_map/ppermute | solution.py:393
  105.0 4.2 %collective-permute-done.30.refs_2_ = bf16[1,2,272,128]{3,2,1,0:T(8,128)(2,1)S(1)} collective-permute-done((bf16[1,2,272,128]{3,2,1,0:T(8,128)(2,1)S(1)}, bf16[1,2,272,128]{3,2,1,0:T(8,128)(2,1)S(1)}, u32[]{:S(2)}, u32[]{:S(2)}) %collective-permute-start.30) | collective-permute-done | bytes 139296 | tf_op jit(solution)/shard_map/ppermute | solution.py:393
  (69 shorter events, 25.1 us)
Async XLA Ops:
  4.2 15.7 %collective-permute-start = (bf16[4,256,128]{2,1,0:T(8,128)(2,1)S(1)}, bf16[4,256,128]{2,1,0:T(8,128)(2,1)S(1)}, u32[]{:S(2)}, u32[]{:S(2)}) collective-permute-start(bf16[4,256,128]{2,1,0:T(8,128)(2,1)S(1)} %get-tuple-element.45.refs_0_.rest_1_.refs_5_), channel_id=1, source_target_pairs={{0,2},{1,3},{2,4},{3,5},{4,6},{5,7},{6,0},{7,1},{8,10},{9,11},{10,... | collective-permute-start | bytes 786440 | tf_op jit(solution)/shard_map/ppermute | solution.py:367
  6.5 14.1 %collective-permute-start.6 = (bf16[4,256,128]{2,1,0:T(8,128)(2,1)S(1)}, bf16[4,256,128]{2,1,0:T(8,128)(2,1)S(1)}, u32[]{:S(2)}, u32[]{:S(2)}) collective-permute-start(bf16[4,256,128]{2,1,0:T(8,128)(2,1)S(1)} %get-tuple-element.45.refs_0_.rest_1_.refs_5_), channel_id=1, source_target_pairs={{0,6},{1,7},{2,0},{3,1},{4,2},{5,3},{6,4},{7,5},{8,14},{9,15},{10,... | collective-permute-start | bytes 786440 | tf_op jit(solution)/shard_map/ppermute | solution.py:367
  6.5 14.2 %collective-permute-start.8 = (bf16[4,256,128]{2,1,0:T(8,128)(2,1)S(1)}, bf16[4,256,128]{2,1,0:T(8,128)(2,1)S(1)}, u32[]{:S(2)}, u32[]{:S(2)}) collective-permute-start(bf16[4,256,128]{2,1,0:T(8,128)(2,1)S(1)} %get-tuple-element.45.refs_0_.rest_1_.refs_5_), channel_id=1, source_target_pairs={{0,4},{1,5},{2,6},{3,7},{4,0},{5,1},{6,2},{7,3},{8,12},{9,13},{10,... | collective-permute-start | bytes 786440 | tf_op jit(solution)/shard_map/ppermute | solution.py:367
  8.7 22.6 %all-to-all-start = ((f32[32,4,4,128]{3,2,1,0:T(4,128)}), f32[32,4,4,128]{3,2,1,0:T(4,128)S(1)}, u32[]{:S(2)}, u32[]{:S(2)}) async-start(f32[32,4,4,128]{3,2,1,0:T(4,128)} %broadcast_in_dim.2), calls=%async_computation | async-start | bytes 524288 | tf_op jit(solution)/shard_map/all_to_all | solution.py:375
  36.0 11.7 %collective-permute-start.20 = (bf16[1,2,272,128]{3,2,1,0:T(8,128)(2,1)S(1)}, bf16[1,2,272,128]{3,2,1,0:T(8,128)(2,1)S(1)}, u32[]{:S(2)}, u32[]{:S(2)}) collective-permute-start(bf16[1,2,272,128]{3,2,1,0:T(8,128)(2,1)S(1)} %get-tuple-element.68), channel_id=1, source_target_pairs={{0,64},{8,72},{16,80},{24,88},{32,96},{40,104},{48,112},{56,120},{... | collective-permute-start | bytes 417800 | tf_op jit(solution)/shard_map/ppermute | solution.py:393
  36.7 13.4 %collective-permute-start.21 = (bf16[1,2,272,128]{3,2,1,0:T(8,128)(2,1)S(1)}, bf16[1,2,272,128]{3,2,1,0:T(8,128)(2,1)S(1)}, u32[]{:S(2)}, u32[]{:S(2)}) collective-permute-start(bf16[1,2,272,128]{3,2,1,0:T(8,128)(2,1)S(1)} %get-tuple-element.69), channel_id=1, source_target_pairs={{0,128},{8,136},{16,144},{24,152},{32,160},{40,168},{48,176},{56,1... | collective-permute-start | bytes 417800 | tf_op jit(solution)/shard_map/ppermute | solution.py:393
  38.9 11.2 %collective-permute-start.22 = (bf16[1,2,272,128]{3,2,1,0:T(8,128)(2,1)S(1)}, bf16[1,2,272,128]{3,2,1,0:T(8,128)(2,1)S(1)}, u32[]{:S(2)}, u32[]{:S(2)}) collective-permute-start(bf16[1,2,272,128]{3,2,1,0:T(8,128)(2,1)S(1)} %get-tuple-element.70), channel_id=1, source_target_pairs={{0,192},{8,200},{16,208},{24,216},{32,224},{40,232},{48,240},{56,2... | collective-permute-start | bytes 417800 | tf_op jit(solution)/shard_map/ppermute | solution.py:393
  45.4 13.2 %collective-permute-start.17 = (bf16[2,2,272,128]{3,2,1,0:T(8,128)(2,1)S(1)}, bf16[2,2,272,128]{3,2,1,0:T(8,128)(2,1)S(1)}, u32[]{:S(2)}, u32[]{:S(2)}) collective-permute-start(bf16[2,2,272,128]{3,2,1,0:T(8,128)(2,1)S(1)} %get-tuple-element.64), channel_id=1, source_target_pairs={{0,64},{8,72},{16,80},{24,88},{32,96},{40,104},{48,112},{56,120},{... | collective-permute-start | bytes 835592 | tf_op jit(solution)/shard_map/ppermute | solution.py:393
  46.1 13.3 %collective-permute-start.18 = (bf16[2,2,272,128]{3,2,1,0:T(8,128)(2,1)S(1)}, bf16[2,2,272,128]{3,2,1,0:T(8,128)(2,1)S(1)}, u32[]{:S(2)}, u32[]{:S(2)}) collective-permute-start(bf16[2,2,272,128]{3,2,1,0:T(8,128)(2,1)S(1)} %get-tuple-element.65), channel_id=1, source_target_pairs={{0,128},{8,136},{16,144},{24,152},{32,160},{40,168},{48,176},{56,1... | collective-permute-start | bytes 835592 | tf_op jit(solution)/shard_map/ppermute | solution.py:393
  47.7 14.1 %collective-permute-start.19 = (bf16[2,2,272,128]{3,2,1,0:T(8,128)(2,1)S(1)}, bf16[2,2,272,128]{3,2,1,0:T(8,128)(2,1)S(1)}, u32[]{:S(2)}, u32[]{:S(2)}) collective-permute-start(bf16[2,2,272,128]{3,2,1,0:T(8,128)(2,1)S(1)} %get-tuple-element.66), channel_id=1, source_target_pairs={{0,192},{8,200},{16,208},{24,216},{32,224},{40,232},{48,240},{56,2... | collective-permute-start | bytes 835592 | tf_op jit(solution)/shard_map/ppermute | solution.py:393
  50.9 10.9 %collective-permute-start.23 = (bf16[4,272,128]{2,1,0:T(8,128)(2,1)S(1)}, bf16[4,272,128]{2,1,0:T(8,128)(2,1)S(1)}, u32[]{:S(2)}, u32[]{:S(2)}) collective-permute-start(bf16[4,272,128]{2,1,0:T(8,128)(2,1)S(1)} %merge.4), channel_id=1, source_target_pairs={{0,8},{8,16},{16,24},{24,32},{32,40},{40,48},{48,56},{56,0},{64,72... | collective-permute-start | bytes 835592 | tf_op jit(solution)/shard_map/ppermute | solution.py:402
  57.8 15.0 %collective-permute-start.14 = (bf16[2,2,272,128]{3,2,1,0:T(8,128)(2,1)S(1)}, bf16[2,2,272,128]{3,2,1,0:T(8,128)(2,1)S(1)}, u32[]{:S(2)}, u32[]{:S(2)}) collective-permute-start(bf16[2,2,272,128]{3,2,1,0:T(8,128)(2,1)S(1)} %get-tuple-element.60), channel_id=1, source_target_pairs={{0,64},{8,72},{16,80},{24,88},{32,96},{40,104},{48,112},{56,120},{... | collective-permute-start | bytes 835592 | tf_op jit(solution)/shard_map/ppermute | solution.py:393
  58.6 21.4 %collective-permute-start.15 = (bf16[2,2,272,128]{3,2,1,0:T(8,128)(2,1)S(1)}, bf16[2,2,272,128]{3,2,1,0:T(8,128)(2,1)S(1)}, u32[]{:S(2)}, u32[]{:S(2)}) collective-permute-start(bf16[2,2,272,128]{3,2,1,0:T(8,128)(2,1)S(1)} %get-tuple-element.61), channel_id=1, source_target_pairs={{0,128},{8,136},{16,144},{24,152},{32,160},{40,168},{48,176},{56,1... | collective-permute-start | bytes 835592 | tf_op jit(solution)/shard_map/ppermute | solution.py:393
  59.3 20.8 %collective-permute-start.16 = (bf16[2,2,272,128]{3,2,1,0:T(8,128)(2,1)S(1)}, bf16[2,2,272,128]{3,2,1,0:T(8,128)(2,1)S(1)}, u32[]{:S(2)}, u32[]{:S(2)}) collective-permute-start(bf16[2,2,272,128]{3,2,1,0:T(8,128)(2,1)S(1)} %get-tuple-element.62), channel_id=1, source_target_pairs={{0,192},{8,200},{16,208},{24,216},{32,224},{40,232},{48,240},{56,2... | collective-permute-start | bytes 835592 | tf_op jit(solution)/shard_map/ppermute | solution.py:393
  62.8 21.0 %collective-permute-start.24 = (bf16[4,272,128]{2,1,0:T(8,128)(2,1)S(1)}, bf16[4,272,128]{2,1,0:T(8,128)(2,1)S(1)}, u32[]{:S(2)}, u32[]{:S(2)}) collective-permute-start(bf16[4,272,128]{2,1,0:T(8,128)(2,1)S(1)} %get-tuple-element.71), channel_id=1, source_target_pairs={{0,8},{8,16},{16,24},{24,32},{32,40},{40,48},{48,56},{56,0},{64,72... | collective-permute-start | bytes 835592 | tf_op jit(solution)/shard_map/ppermute | solution.py:402
  64.1 22.3 %collective-permute-start.25 = (bf16[4,272,128]{2,1,0:T(8,128)(2,1)S(1)}, bf16[4,272,128]{2,1,0:T(8,128)(2,1)S(1)}, u32[]{:S(2)}, u32[]{:S(2)}) collective-permute-start(bf16[4,272,128]{2,1,0:T(8,128)(2,1)S(1)} %get-tuple-element.72), channel_id=1, source_target_pairs={{0,56},{8,0},{16,8},{24,16},{32,24},{40,32},{48,40},{56,48},{64,12... | collective-permute-start | bytes 835592 | tf_op jit(solution)/shard_map/ppermute | solution.py:404
  72.8 14.9 %collective-permute-start.10 = (bf16[1,2,272,128]{3,2,1,0:T(8,128)(2,1)S(1)}, bf16[1,2,272,128]{3,2,1,0:T(8,128)(2,1)S(1)}, u32[]{:S(2)}, u32[]{:S(2)}) collective-permute-start(bf16[1,2,272,128]{3,2,1,0:T(8,128)(2,1)S(1)} %get-tuple-element.54), channel_id=1, source_target_pairs={{0,64},{8,72},{16,80},{24,88},{32,96},{40,104},{48,112},{56,120},{... | collective-permute-start | bytes 417800 | tf_op jit(solution)/shard_map/ppermute | solution.py:393
  80.0 12.0 %collective-permute-start.11 = (bf16[2,2,272,128]{3,2,1,0:T(8,128)(2,1)S(1)}, bf16[2,2,272,128]{3,2,1,0:T(8,128)(2,1)S(1)}, u32[]{:S(2)}, u32[]{:S(2)}) collective-permute-start(bf16[2,2,272,128]{3,2,1,0:T(8,128)(2,1)S(1)} %get-tuple-element.56), channel_id=1, source_target_pairs={{0,64},{8,72},{16,80},{24,88},{32,96},{40,104},{48,112},{56,120},{... | collective-permute-start | bytes 835592 | tf_op jit(solution)/shard_map/ppermute | solution.py:393
  80.1 11.9 %collective-permute-start.12 = (bf16[2,2,272,128]{3,2,1,0:T(8,128)(2,1)S(1)}, bf16[2,2,272,128]{3,2,1,0:T(8,128)(2,1)S(1)}, u32[]{:S(2)}, u32[]{:S(2)}) collective-permute-start(bf16[2,2,272,128]{3,2,1,0:T(8,128)(2,1)S(1)} %get-tuple-element.57), channel_id=1, source_target_pairs={{0,128},{8,136},{16,144},{24,152},{32,160},{40,168},{48,176},{56,1... | collective-permute-start | bytes 835592 | tf_op jit(solution)/shard_map/ppermute | solution.py:393
  83.8 8.4 %collective-permute-start.13 = (bf16[2,2,272,128]{3,2,1,0:T(8,128)(2,1)S(1)}, bf16[2,2,272,128]{3,2,1,0:T(8,128)(2,1)S(1)}, u32[]{:S(2)}, u32[]{:S(2)}) collective-permute-start(bf16[2,2,272,128]{3,2,1,0:T(8,128)(2,1)S(1)} %get-tuple-element.58), channel_id=1, source_target_pairs={{0,192},{8,200},{16,208},{24,216},{32,224},{40,232},{48,240},{56,2... | collective-permute-start | bytes 835592 | tf_op jit(solution)/shard_map/ppermute | solution.py:393
  87.4 10.8 %collective-permute-start.26 = (bf16[4,272,128]{2,1,0:T(8,128)(2,1)S(1)}, bf16[4,272,128]{2,1,0:T(8,128)(2,1)S(1)}, u32[]{:S(2)}, u32[]{:S(2)}) collective-permute-start(bf16[4,272,128]{2,1,0:T(8,128)(2,1)S(1)} %get-tuple-element.73), channel_id=1, source_target_pairs={{0,8},{8,16},{16,24},{24,32},{32,40},{40,48},{48,56},{56,0},{64,72... | collective-permute-start | bytes 835592 | tf_op jit(solution)/shard_map/ppermute | solution.py:402
  87.8 10.5 %collective-permute-start.27 = (bf16[4,272,128]{2,1,0:T(8,128)(2,1)S(1)}, bf16[4,272,128]{2,1,0:T(8,128)(2,1)S(1)}, u32[]{:S(2)}, u32[]{:S(2)}) collective-permute-start(bf16[4,272,128]{2,1,0:T(8,128)(2,1)S(1)} %get-tuple-element.74), channel_id=1, source_target_pairs={{0,56},{8,0},{16,8},{24,16},{32,24},{40,32},{48,40},{56,48},{64,12... | collective-permute-start | bytes 835592 | tf_op jit(solution)/shard_map/ppermute | solution.py:404
  99.3 10.7 %collective-permute-start.28 = (bf16[4,272,128]{2,1,0:T(8,128)(2,1)S(1)}, bf16[4,272,128]{2,1,0:T(8,128)(2,1)S(1)}, u32[]{:S(2)}, u32[]{:S(2)}) collective-permute-start(bf16[4,272,128]{2,1,0:T(8,128)(2,1)S(1)} %get-tuple-element.75), channel_id=1, source_target_pairs={{0,8},{8,16},{16,24},{24,32},{32,40},{40,48},{48,56},{56,0},{64,72... | collective-permute-start | bytes 835592 | tf_op jit(solution)/shard_map/ppermute | solution.py:402
  99.4 10.6 %collective-permute-start.29 = (bf16[4,272,128]{2,1,0:T(8,128)(2,1)S(1)}, bf16[4,272,128]{2,1,0:T(8,128)(2,1)S(1)}, u32[]{:S(2)}, u32[]{:S(2)}) collective-permute-start(bf16[4,272,128]{2,1,0:T(8,128)(2,1)S(1)} %get-tuple-element.76), channel_id=1, source_target_pairs={{0,56},{8,0},{16,8},{24,16},{32,24},{40,32},{48,40},{56,48},{64,12... | collective-permute-start | bytes 835592 | tf_op jit(solution)/shard_map/ppermute | solution.py:404
  (13 other events, 83.6 us)

commit v3 on v2

--- a/solution.py
+++ b/solution.py
@@ -20,7 +20,7 @@
 OWNERS = NY * NZ
 PAIRS = OWNERS * SLOTS
 ROWS = FEAT + 16
-GATE_COST = 800_000_000
+GATE_COST = 1400_000_000
 LOG2E = 1.4426950408889634
 EMPTY = -(2.0**100)
 F32 = jnp.float32
@@ -30,7 +30,7 @@
 
 
 def params(**more):
-    return pltpu.CompilerParams(vmem_limit_bytes=48 * 1024 * 1024, **more)
+    return pltpu.CompilerParams(vmem_limit_bytes=46 * 1024 * 1024, **more)
 
 
 def leaky(values):
@@ -53,7 +53,8 @@
     return [(x * NC + c, x * NC + (c - k) % NC) for x in range(NX) for c in range(NC)]
 
 
-PLAN = ((4,), (3, -3), (2, -2), (1, -1), (0,))
+PLAN = ((4,), (3, -3), (2, -2), (1, -1, 0))
+NEXT = {4: 3, 3: 2, 2: 1, 1: 0, -3: -2, -2: -1, -1: 0}
 
 
 def head_sums(products):
@@ -63,17 +64,9 @@
     )
 
 
-def prepare_kernel(x_ref, src_hbm, dst_hbm, hidden_ref, target_ref, self_ref, att_ref, src_ref, dst_ref, sems):
-    copies = [
-        pltpu.make_async_copy(src_hbm, src_ref, sems.at[0]),
-        pltpu.make_async_copy(dst_hbm, dst_ref, sems.at[1]),
-    ]
-    for copy in copies:
-        copy.start()
-    for copy in copies:
-        copy.wait()
-    att_src = jnp.broadcast_to(src_ref[...] * LOG2E, (BLK, FEAT)).T
-    att_dst = jnp.broadcast_to(dst_ref[...] * LOG2E, (BLK, FEAT)).T
+def prepare_kernel(x_ref, both_ref, hidden_ref, target_ref, self_ref, att_ref):
+    att_src = jnp.broadcast_to(both_ref[0:1] * LOG2E, (BLK, FEAT)).T
+    att_dst = jnp.broadcast_to(both_ref[1:2] * LOG2E, (BLK, FEAT)).T
     att_ref[...] = att_src
     for b in range(NBD):
         wide = x_ref[b * BLK : (b + 1) * BLK, :].astype(F32).T
@@ -93,32 +86,51 @@
             jax.ShapeDtypeStruct((NBD, HEADS, BLK), F32),
             jax.ShapeDtypeStruct((FEAT, BLK), F32),
         ),
-        in_specs=[VMEM, ANY, ANY],
+        in_specs=[VMEM] * 2,
         out_specs=(VMEM,) * 4,
-        scratch_shapes=[
-            pltpu.VMEM((1, FEAT), F32),
-            pltpu.VMEM((1, FEAT), F32),
-            pltpu.SemaphoreType.DMA((2,)),
-        ],
         compiler_params=params(),
         name="prepare",
-    )(hidden, att_src.reshape(1, FEAT), att_dst.reshape(1, FEAT))
+    )(hidden, jnp.stack([att_src, att_dst]))
 
 
 def gate_kernel(*refs):
     refs[-1][...] = jnp.zeros((8, BLK), F32)
 
 
-def gate(pieces):
+def gate(*arrays):
     return pl.pallas_call(
         gate_kernel,
         out_shape=jax.ShapeDtypeStruct((8, BLK), F32),
-        in_specs=[ANY] * PIECES,
+        in_specs=[ANY] * len(arrays),
         out_specs=VMEM,
         compiler_params=params(),
         cost_estimate=pl.CostEstimate(flops=GATE_COST, bytes_accessed=1000, transcendentals=0),
         name="gate",
-    )(*pieces)
+    )(*arrays)
+
+
+def mask_kernel(mask_ref, out_ref):
+    for n in range(mask_ref.shape[0]):
+        for t in range(SLOTS):
+            bias = jnp.where(mask_ref[n, t] > 0, 0.0, EMPTY).astype(F32)
+            out_ref[n, t] = bias.T.astype(BF16)
+
+
+def mask_bias(masks):
+    step = 4
+    spec = pl.BlockSpec((step, SLOTS, BLK, BLK), lambda i: (i, 0, 0, 0))
+    return pl.pallas_call(
+        mask_kernel,
+        grid=(OWNERS // step,),
+        out_shape=jax.ShapeDtypeStruct((OWNERS, SLOTS, BLK, BLK), BF16),
+        in_specs=[spec],
+        out_specs=spec,
+        compiler_params=params(),
+        cost_estimate=pl.CostEstimate(
+            flops=PAIRS * BLK * BLK * 8, bytes_accessed=PAIRS * BLK * BLK * 6, transcendentals=0
+        ),
+        name="mask_bias",
+    )(masks)
 
 
 def owner_of(scal, k, offset):
@@ -154,78 +166,68 @@
     out_ref[place + (pl.ds(FEAT, 16), slice(None))] = jnp.concatenate(rows, axis=0).astype(BF16)
 
 
-def slots_kernel(offsets, first, scal, token, targets, att, *rest):
+def slots_kernel(offsets, first, scal, token, targets, att, bias, *rest):
     del token
-    n_own, n_in = len(offsets), PIECES if first else 1
-    masks, sources, rest = rest[:n_own], rest[n_own : n_own + n_in], rest[n_own + n_in :]
-    step = pl.program_id(0)
     if first:
-        *outs, hidden, made, sems = rest
-
-        @pl.when(step == 0)
-        def _():
-            copies = [
-                pltpu.make_async_copy(sources[n], hidden.at[pl.ds(n * NBD, NBD)], sems.at[n])
-                for n in range(PIECES)
-            ]
-            for copy in copies:
-                copy.start()
-            for copy in copies:
-                copy.wait()
-
+        sources, (*outs, hidden, made, sems) = rest[:PIECES], rest[PIECES:]
+        copies = [
+            pltpu.make_async_copy(sources[n], hidden.at[pl.ds(n * NBD, NBD)], sems.at[n])
+            for n in range(PIECES)
+        ]
+        for copy in copies:
+            copy.start()
+        for copy in copies:
+            copy.wait()
     else:
-        (hidden,), (*outs, made) = sources, rest
-    for n, (offset, mask) in enumerate(zip(offsets, masks, strict=True)):
-        owner = owner_of(scal, step, offset)
-        for t in range(SLOTS):
-            pair = scal[owner * SLOTS + t]
-            block = pair & (SRC_BLOCKS - 1)
-            place = pair >> (SRC_BLOCKS.bit_length() - 1)
-            holder = block >> (NBD.bit_length() - 1)
-            dst = scal[PAIRS + 1]
-            dx = ((holder >> 1) - (dst >> 1)) & (NX - 1)
-            dc = (holder ^ dst) & (NC - 1)
-            held = ((dx * NC + dc) * NBD) | (block & (NBD - 1))
-            bias = jnp.where(mask[0, t] > 0, 0.0, EMPTY).astype(F32).T
-            slot_partial(hidden[held], att[...], bias, targets[owner, place], made, (n, t))
-
-    for k in range(NY):
-
-        @pl.when(step == k)
-        def _(k=k):
-            outs[k][...] = made[...]
-
-
-def slots(offsets, scal, token, masks, targets, att, source):
+        hidden, *outs, made = rest
+    dst = scal[PAIRS + 1]
+    together = made.shape[0]
+
+    def some(step, carry):
+        for part in range(together):
+            for n, offset in enumerate(offsets):
+                owner = owner_of(scal, step * together + part, offset)
+                for t in range(SLOTS):
+                    pair = scal[owner * SLOTS + t]
+                    block = pair & (SRC_BLOCKS - 1)
+                    place = pair >> (SRC_BLOCKS.bit_length() - 1)
+                    holder = block >> (NBD.bit_length() - 1)
+                    dx = ((holder >> 1) - (dst >> 1)) & (NX - 1)
+                    dc = (holder ^ dst) & (NC - 1)
+                    held = ((dx * NC + dc) * NBD) | (block & (NBD - 1))
+                    slot_partial(
+                        hidden[held], att[...], bias[owner, t].astype(F32), targets[owner, place], made, (part, n, t)
+                    )
+        for other in range(NY // together):
+
+            @pl.when(step == other)
+            def _(other=other):
+                for part in range(together):
+                    outs[other * together + part][...] = made[part]
+
+        return carry
+
+    lax.fori_loop(0, NY // together, some, 0)
+
+
+def slots(offsets, scal, token, bias, targets, att, source):
     first = isinstance(source, list)
-
-    def mask_spec(offset):
-        return pl.BlockSpec(
-            (1, SLOTS, BLK, BLK), lambda i, scal: (owner_of(scal, i, offset), 0, 0, 0)
-        )
-
     shape = (len(offsets), SLOTS, ROWS, BLK)
     out_shape = (jax.ShapeDtypeStruct(shape, BF16),) * NY
-    scratch = [pltpu.VMEM(shape, BF16)]
+    scratch = [pltpu.VMEM((max(1, 2 // len(offsets)),) + shape, BF16)]
     if first:
         out_shape += (jax.ShapeDtypeStruct((SRC_BLOCKS, FEAT, BLK), BF16),)
         scratch.append(pltpu.SemaphoreType.DMA((PIECES,)))
     return pl.pallas_call(
         functools.partial(slots_kernel, offsets, first),
         out_shape=out_shape,
-        grid_spec=pltpu.PrefetchScalarGridSpec(
-            num_scalar_prefetch=1,
-            grid=(NY,),
-            in_specs=[ANY, VMEM, VMEM]
-            + [mask_spec(offset) for offset in offsets]
-            + ([ANY] * PIECES if first else [VMEM]),
-            out_specs=(VMEM,) * len(out_shape),
-            scratch_shapes=scratch,
-        ),
+        in_specs=[SMEM, ANY, VMEM, VMEM, VMEM] + ([ANY] * PIECES if first else [VMEM]),
+        out_specs=(VMEM,) * len(out_shape),
+        scratch_shapes=scratch,
         compiler_params=params(),
         cost_estimate=pl.CostEstimate(flops=1000, bytes_accessed=1000, transcendentals=0),
         name="slots",
-    )(scal, token, targets, att, *[masks] * len(offsets), *(source if first else [source]))
+    )(scal, token, targets, att, bias, *(source if first else [source]))
 
 
 def bound_total(ref, place):
@@ -276,8 +278,9 @@
     owner = owner_of(scal, 0, offset)
     found = []
     for k in range(NY):
+        maker = owner_of(scal, -k, 0)
         for t in range(SLOTS):
-            place = every_pair[k, owner * SLOTS + t] >> (SRC_BLOCKS.bit_length() - 1)
+            place = every_pair[maker * SLOTS + t, owner] >> (SRC_BLOCKS.bit_length() - 1)
             found.append((refs[k], (n, t), place))
     return found
 
@@ -317,15 +320,15 @@
     )(scal, every_pair, *parts, *dense)
 
 
-def home_kernel(scal, every_pair, *refs):
+def home_kernel(n, scal, every_pair, *refs):
     parts, (self_ref, hidden_ref, bounds, totals, sums) = refs[:NY], refs[NY:]
-    found = placed(scal, every_pair, 0, parts, 0)
+    found = placed(scal, every_pair, 0, parts, n)
     merge(found, (), bounds, totals, sums, (self_ref, None, hidden_ref))
 
 
 def merge_home(scal, every_pair, parts, self_logit, hidden):
     return pl.pallas_call(
-        home_kernel,
+        functools.partial(home_kernel, PLAN[-1].index(0)),
         out_shape=tuple(jax.ShapeDtypeStruct(shape, F32) for shape in SUMS),
         in_specs=[SMEM] * 2 + [VMEM] * (NY + 2),
         out_specs=(VMEM,) * 3,
@@ -335,8 +338,10 @@
     )(scal, every_pair, *parts, self_logit, hidden)
 
 
-def finish_kernel(up, down, home_bounds, home_totals, home_sums, bias_ref, out, bounds, totals, sums):
-    merge((), (up, down), bounds, totals, sums, (home_bounds, home_totals, home_sums))
+def finish_kernel(*refs):
+    dense, refs = refs[:-8], refs[-8:]
+    home_bounds, home_totals, home_sums, bias_ref, out, bounds, totals, sums = refs
+    merge((), dense, bounds, totals, sums, (home_bounds, home_totals, home_sums))
     for b in range(NBD):
         scale = 1.0 / totals[b]
         value = jnp.concatenate(
@@ -348,16 +353,16 @@
         )
 
 
-def finish(up, down, home, bias):
+def finish(dense, home, bias):
     return pl.pallas_call(
         finish_kernel,
         out_shape=jax.ShapeDtypeStruct((NBD * BLK, FEAT), F32),
-        in_specs=[VMEM] * 6,
+        in_specs=[VMEM] * (len(dense) + 4),
         out_specs=VMEM,
         scratch_shapes=[pltpu.VMEM(shape, F32) for shape in SUMS],
         compiler_params=params(),
         name="finish",
-    )(up, down, *home, bias.reshape(1, FEAT))
+    )(*dense, *home, bias.reshape(1, FEAT))
 
 
 def body(features, weight, att_src, att_dst, bias, block_pairs, edge_masks):
@@ -371,18 +376,18 @@
     pairs = block_pairs.reshape(-1)
     scal = jnp.concatenate([pairs, jnp.stack([src, dst]).astype(jnp.int32)])
 
-    told = jnp.broadcast_to(own_target[None], (OWNERS,) + own_target.shape)
-    told = lax.all_to_all(told, "src", 0, 0)
+    row = block_pairs.reshape(OWNERS, SLOTS).T.astype(F32)
+    row = jnp.pad(row, ((0, HEADS - SLOTS), (0, BLK - OWNERS)))[None]
+    told = jnp.concatenate([own_target, row], axis=0)
+    told = lax.all_to_all(jnp.broadcast_to(told[None], (OWNERS,) + told.shape), "src", 0, 0)
+    every_pair = told[:, NBD, :SLOTS, :OWNERS].astype(jnp.int32).reshape(OWNERS * SLOTS, OWNERS)
 
     pieces = []
     for piece in along_x:
         pieces += [piece, lax.ppermute(piece, "dst", core_from(1))]
-    pairs, pieces[-1] = lax.optimization_barrier((pairs, pieces[-1]))
-    every_pair = jnp.stack([pairs] + [lax.ppermute(pairs, "src", y_from(-k)) for k in range(1, NY)])
-    token = gate(pieces)
-    scal, every_pair = lax.optimization_barrier((scal, every_pair))
-
-    up, down = (), ()
+    masks = mask_bias(masks)
+    token = gate(*pieces, masks)
+
     made, parts = [], []
     source = pieces
     for step, offsets in enumerate(PLAN):
@@ -392,18 +397,22 @@
         parts.append(
             [made[-1][0]] + [lax.ppermute(made[-1][k], "src", y_from(-k)) for k in range(1, NY)]
         )
-    for step, offsets in enumerate(PLAN[:-1]):
-        work = [(offsets[0], len(up))] + [(offset, len(down)) for offset in offsets[1:]]
-        if step == len(PLAN) - 2:
+    coming = {offset: () for offset in (0, *NEXT)}
+    for step, offsets in enumerate(PLAN):
+        work = [(offset, len(coming[offset])) for offset in offsets if offset != 0]
+        if not work:
+            break
+        if PLAN[step + 1 : step + 2] == ((0,),):
             parts[step][0], parts[step + 1][1] = lax.optimization_barrier(
                 (parts[step][0], parts[step + 1][1])
             )
-        sent = merge_group(work, scal, every_pair, parts[step], up + down)
-        up = (lax.ppermute(sent[0], "src", z_from(-1)),)
-        if len(sent) > 1:
-            down = (lax.ppermute(sent[1], "src", z_from(1)),)
+        dense = sum((coming[offset] for offset, _ in work), ())
+        sent = merge_group(work, scal, every_pair, parts[step], dense)
+        for (offset, _), chunk in zip(work, sent, strict=True):
+            hop = lax.ppermute(chunk, "src", z_from(NEXT[offset] - offset))
+            coming[NEXT[offset]] += (hop,)
     home = merge_home(scal, every_pair, parts[-1], self_logit, hidden)
-    return finish(up[0], down[0], home, bias)
+    return finish(coming[0], home, bias)
 
 
 def solution(mesh):

time: 112 us -> 103 us (0.920)
  the two profiles are of different devices: /device:TPU:6 before, /device:TPU:8 now
where the time goes in v3:
time: 103 us
  starting transfers between devices  51.5 us (50%)
  Pallas kernels  27.1 us (26%)
  waiting for transfers between devices  17.8 us (17%)
  local copies, waits for them, and re-layouts  3.54 us (3%)
  other arithmetic  1.56 us (2%)
  matrix products  1.36 us (1%)
    ppermute x12, starting transfers between devices, body(): lax.ppermute(made[-1][k], 'src', y_from(-k))  17.8 us
    pallas_call x4, Pallas kernels, slots(): pl.pallas_call(functools.partial(slots_kernel, offsets, first), out_shape...  16.4 us
    ppermute x7, starting transfers between devices, body(): hop = lax.ppermute(chunk, 'src', z_from(NEXT[offset] - offset))  15.3 us
    all_to_all x1, starting transfers between devices, body(): lax.all_to_all(jnp.broadcast_to(told[None], (OWNERS,) + told.shape), 'src...  11.7 us
    all_to_all x1, waiting for transfers between devices, body(): lax.all_to_all(jnp.broadcast_to(told[None], (OWNERS,) + told.shape), 'src...  6.64 us
    ppermute x7, waiting for transfers between devices, body(): hop = lax.ppermute(chunk, 'src', z_from(NEXT[offset] - offset))  6.62 us
    pallas_call x4, Pallas kernels, merge_group(): pl.pallas_call(functools.partial(merge_kernel, work), out_shape=(jax.Shap...  6.06 us
    ppermute x3, starting transfers between devices, body(): lax.ppermute(hidden, 'dst', x_from(k))  5.66 us
  transfers between devices with their start and end apart: 27, of which 6 were waited for; matrix products, arithmetic and copies ran while one was open for 2% of the time, Pallas kernels for 19%

profile of v3, /device:TPU:8, one launch (start us, length us, event | category | flops | bytes accessed | tf_op | source)
XLA Modules:
  0.0 103.1 jit_solution(11717198954772889260)
XLA Ops:
  5.0 2.7 %collective-permute-start.3 = (bf16[4,256,128]{2,1,0:T(8,128)(2,1)}, bf16[4,256,128]{2,1,0:T(8,128)(2,1)}, u32[]{:S(2)}, u32[]{:S(2)}) collective-permute-start(bf16[4,256,128]{2,1,0:T(8,128)(2,1)} %get-tuple-element.36.refs_0_.rest_0_.refs_5_), channel_id=1, source_target_pairs={{0,4},{1,5},{2,6},{3,7},{4,0},{5,1},{6,2},{7,3},{8,12},{9,13},{10,... | collective-permute-start | bytes 786440 | tf_op jit(solution)/shard_map/ppermute | solution.py:372
  10.6 11.7 %all-to-all-start = ((f32[32,5,4,128]{3,2,1,0:T(4,128)}), f32[32,5,4,128]{3,2,1,0:T(4,128)S(1)}, u32[]{:S(2)}, u32[]{:S(2)}) async-start(f32[32,5,4,128]{3,2,1,0:T(4,128)} %broadcast_in_dim.10), calls=%async_computation | async-start | bytes 655360 | tf_op jit(solution)/shard_map/all_to_all | solution.py:382
  23.7 2.2 %copy-done.1 = s32[1,1,32,2,128,128]{5,4,3,2,1,0:T(8,128)S(1)} copy-done((s32[1,1,32,2,128,128]{5,4,3,2,1,0:T(8,128)S(1)}, s32[1,1,32,2,128,128]{5,4,3,2,1,0:T(8,128)}, u32[]{:S(2)}) %copy-start.1) | copy-done | bytes 4194328
  27.1 6.6 %all-to-all-done.targets = f32[32,5,4,128]{3,2,1,0:T(4,128)S(1)} async-done(((f32[32,5,4,128]{3,2,1,0:T(4,128)}), f32[32,5,4,128]{3,2,1,0:T(4,128)S(1)}, u32[]{:S(2)}, u32[]{:S(2)}) %all-to-all-start) | async-done | bytes 327712 | tf_op jit(solution)/shard_map/all_to_all | solution.py:382
  33.8 3.7 %slots.4 = (bf16[1,2,272,128]{3,2,1,0:T(8,128)(2,1)S(1)}, bf16[1,2,272,128]{3,2,1,0:T(8,128)(2,1)S(1)}, bf16[1,2,272,128]{3,2,1,0:T(8,128)(2,1)S(1)}, bf16[1,2,2...) custom-call(s32[66]{0:T(128)S(1)} %pad_add_fusion.scal, f32[8,128]{1,0:T(8,128)S(1)} %gate.1.token, ...), custom_call_target="tpu_custom_call" | custom-call | flops 1000 | bytes 1000 | tf_op jit(solution)/shard_map/slots/pallas_call | solution.py:221
  38.5 2.5 %collective-permute-start.17 = (bf16[1,2,272,128]{3,2,1,0:T(8,128)(2,1)S(1)}, bf16[1,2,272,128]{3,2,1,0:T(8,128)(2,1)S(1)}, u32[]{:S(2)}, u32[]{:S(2)}) collective-permute-start(bf16[1,2,272,128]{3,2,1,0:T(8,128)(2,1)S(1)} %get-tuple-element.53), channel_id=1, source_target_pairs={{0,128},{8,136},{16,144},{24,152},{32,160},{40,168},{48,176},{56,1... | collective-permute-start | bytes 417800 | tf_op jit(solution)/shard_map/ppermute | solution.py:398
  41.6 3.9 %slots.7 = (bf16[2,2,272,128]{3,2,1,0:T(8,128)(2,1)S(1)}, bf16[2,2,272,128]{3,2,1,0:T(8,128)(2,1)S(1)}, bf16[2,2,272,128]{3,2,1,0:T(8,128)(2,1)S(1)}, bf16[2,2,272,128]{3,2,1,0:T(8,128)(2,1)S(1)}) custom-call(s32[66]{0:T(128)S(1)} %pad_add_fusion.scal, f32[8,128]{1,0:T(8,128)S(1)} %gate.1.token, f32[32,5,4,128]{3,2,1,0:T(4,128)S(1)} %all-to-all-done.targets, ...), custom_call_target="tpu_custom_call" | custom-call | flops 1000 | bytes 1000 | tf_op jit(solution)/shard_map/slots/pallas_call | solution.py:221
  45.5 1.6 %collective-permute-start.13 = (bf16[2,2,272,128]{3,2,1,0:T(8,128)(2,1)S(1)}, bf16[2,2,272,128]{3,2,1,0:T(8,128)(2,1)S(1)}, u32[]{:S(2)}, u32[]{:S(2)}) collective-permute-start(bf16[2,2,272,128]{3,2,1,0:T(8,128)(2,1)S(1)} %get-tuple-element.48), channel_id=1, source_target_pairs={{0,64},{8,72},{16,80},{24,88},{32,96},{40,104},{48,112},{56,120},{... | collective-permute-start | bytes 835592 | tf_op jit(solution)/shard_map/ppermute | solution.py:398
  47.0 2.2 %collective-permute-start.14 = (bf16[2,2,272,128]{3,2,1,0:T(8,128)(2,1)S(1)}, bf16[2,2,272,128]{3,2,1,0:T(8,128)(2,1)S(1)}, u32[]{:S(2)}, u32[]{:S(2)}) collective-permute-start(bf16[2,2,272,128]{3,2,1,0:T(8,128)(2,1)S(1)} %get-tuple-element.49), channel_id=1, source_target_pairs={{0,128},{8,136},{16,144},{24,152},{32,160},{40,168},{48,176},{56,1... | collective-permute-start | bytes 835592 | tf_op jit(solution)/shard_map/ppermute | solution.py:398
  50.7 2.1 %collective-permute-start.19 = (bf16[4,272,128]{2,1,0:T(8,128)(2,1)S(1)}, bf16[4,272,128]{2,1,0:T(8,128)(2,1)S(1)}, u32[]{:S(2)}, u32[]{:S(2)}) collective-permute-start(bf16[4,272,128]{2,1,0:T(8,128)(2,1)S(1)} %merge.4), channel_id=1, source_target_pairs={{0,8},{8,16},{16,24},{24,32},{32,40},{40,48},{48,56},{56,0},{64,72... | collective-permute-start | bytes 835592 | tf_op jit(solution)/shard_map/ppermute | solution.py:412
  52.8 3.9 %slots.6 = (bf16[2,2,272,128]{3,2,1,0:T(8,128)(2,1)S(1)}, bf16[2,2,272,128]{3,2,1,0:T(8,128)(2,1)S(1)}, bf16[2,2,272,128]{3,2,1,0:T(8,128)(2,1)S(1)}, bf16[2,2,272,128]{3,2,1,0:T(8,128)(2,1)S(1)}) custom-call(s32[66]{0:T(128)S(1)} %pad_add_fusion.scal, f32[8,128]{1,0:T(8,128)S(1)} %gate.1.token, f32[32,5,4,128]{3,2,1,0:T(4,128)S(1)} %all-to-all-done.targets, ...), custom_call_target="tpu_custom_call" | custom-call | flops 1000 | bytes 1000 | tf_op jit(solution)/shard_map/slots/pallas_call | solution.py:221
  56.7 2.0 %collective-permute-start.10 = (bf16[2,2,272,128]{3,2,1,0:T(8,128)(2,1)S(1)}, bf16[2,2,272,128]{3,2,1,0:T(8,128)(2,1)S(1)}, u32[]{:S(2)}, u32[]{:S(2)}) collective-permute-start(bf16[2,2,272,128]{3,2,1,0:T(8,128)(2,1)S(1)} %get-tuple-element.44), channel_id=1, source_target_pairs={{0,64},{8,72},{16,80},{24,88},{32,96},{40,104},{48,112},{56,120},{... | collective-permute-start | bytes 835592 | tf_op jit(solution)/shard_map/ppermute | solution.py:398
  58.7 2.7 %collective-permute-start.11 = (bf16[2,2,272,128]{3,2,1,0:T(8,128)(2,1)S(1)}, bf16[2,2,272,128]{3,2,1,0:T(8,128)(2,1)S(1)}, u32[]{:S(2)}, u32[]{:S(2)}) collective-permute-start(bf16[2,2,272,128]{3,2,1,0:T(8,128)(2,1)S(1)} %get-tuple-element.45), channel_id=1, source_target_pairs={{0,128},{8,136},{16,144},{24,152},{32,160},{40,168},{48,176},{56,1... | collective-permute-start | bytes 835592 | tf_op jit(solution)/shard_map/ppermute | solution.py:398
  63.0 6.5 %collective-permute-start.20 = (bf16[4,272,128]{2,1,0:T(8,128)(2,1)S(1)}, bf16[4,272,128]{2,1,0:T(8,128)(2,1)S(1)}, u32[]{:S(2)}, u32[]{:S(2)}) collective-permute-start(bf16[4,272,128]{2,1,0:T(8,128)(2,1)S(1)} %get-tuple-element.55), channel_id=1, source_target_pairs={{0,8},{8,16},{16,24},{24,32},{32,40},{40,48},{48,56},{56,0},{64,72... | collective-permute-start | bytes 835592 | tf_op jit(solution)/shard_map/ppermute | solution.py:412
  69.5 4.9 %slots.5 = (bf16[3,2,272,128]{3,2,1,0:T(8,128)(2,1)S(1)}, bf16[3,2,272,128]{3,2,1,0:T(8,128)(2,1)S(1)}, bf16[3,2,272,128]{3,2,1,0:T(8,128)(2,1)S(1)}, bf16[3,2,272,128]{3,2,1,0:T(8,128)(2,1)S(1)}) custom-call(s32[66]{0:T(128)S(1)} %pad_add_fusion.scal, f32[8,128]{1,0:T(8,128)S(1)} %gate.1.token, f32[32,5,4,128]{3,2,1,0:T(4,128)S(1)} %all-to-all-done.targets, ...), custom_call_target="tpu_custom_call" | custom-call | flops 1000 | bytes 1000 | tf_op jit(solution)/shard_map/slots/pallas_call | solution.py:221
  74.6 2.6 %collective-permute-start.8 = (bf16[3,2,272,128]{3,2,1,0:T(8,128)(2,1)S(1)}, bf16[3,2,272,128]{3,2,1,0:T(8,128)(2,1)S(1)}, u32[]{:S(2)}, u32[]{:S(2)}) collective-permute-start(bf16[3,2,272,128]{3,2,1,0:T(8,128)(2,1)S(1)} %get-tuple-element.41), channel_id=1, source_target_pairs={{0,128},{8,136},{16,144},{24,152},{32,160},{40,168},{48,176},{56,1... | collective-permute-start | bytes 1253384 | tf_op jit(solution)/shard_map/ppermute | solution.py:398
  77.1 2.5 %collective-permute-start.9 = (bf16[3,2,272,128]{3,2,1,0:T(8,128)(2,1)S(1)}, bf16[3,2,272,128]{3,2,1,0:T(8,128)(2,1)S(1)}, u32[]{:S(2)}, u32[]{:S(2)}) collective-permute-start(bf16[3,2,272,128]{3,2,1,0:T(8,128)(2,1)S(1)} %get-tuple-element.42), channel_id=1, source_target_pairs={{0,192},{8,200},{16,208},{24,216},{32,224},{40,232},{48,240},{56,2... | collective-permute-start | bytes 1253384 | tf_op jit(solution)/shard_map/ppermute | solution.py:398
  79.7 1.6 %merge.6 = (bf16[4,272,128]{2,1,0:T(8,128)(2,1)S(1)}, bf16[4,272,128]{2,1,0:T(8,128)(2,1)S(1)}) custom-call(s32[66]{0:T(128)S(1)} %pad_add_fusion.scal, s32[64,32]{1,0:T(8,128)S(1)} %bitcast.20, bf16[2,2,272,128]{3,2,1,0:T(8,128)(2,1)S(1)} %get-tuple-element.43.refs_0_, bf16[2,2,272,128]{3,2,1,0:T(8,128)(2,1)S(1)} %collective-permute-done.10.refs_1_, ...), custom_call_target="tpu_custom_call" | custom-call | flops 1000 | bytes 1000 | tf_op jit(solution)/shard_map/merge/pallas_call | solution.py:311
  81.3 2.1 %collective-permute-start.22 = (bf16[4,272,128]{2,1,0:T(8,128)(2,1)S(1)}, bf16[4,272,128]{2,1,0:T(8,128)(2,1)S(1)}, u32[]{:S(2)}, u32[]{:S(2)}) collective-permute-start(bf16[4,272,128]{2,1,0:T(8,128)(2,1)S(1)} %get-tuple-element.57), channel_id=1, source_target_pairs={{0,8},{8,16},{16,24},{24,32},{32,40},{40,48},{48,56},{56,0},{64,72... | collective-permute-start | bytes 835592 | tf_op jit(solution)/shard_map/ppermute | solution.py:412
  84.7 4.4 %collective-permute-done.9.refs_3_ = bf16[3,2,272,128]{3,2,1,0:T(8,128)(2,1)S(1)} collective-permute-done((bf16[3,2,272,128]{3,2,1,0:T(8,128)(2,1)S(1)}, bf16[3,2,272,128]{3,2,1,0:T(8,128)(2,1)S(1)}, u32[]{:S(2)}, u32[]{:S(2)}) %collective-permute-start.9) | collective-permute-done | bytes 417824 | tf_op jit(solution)/shard_map/ppermute | solution.py:398
  90.3 2.2 %collective-permute-done.23.refs_5_ = bf16[4,272,128]{2,1,0:T(8,128)(2,1)S(1)} collective-permute-done((bf16[4,272,128]{2,1,0:T(8,128)(2,1)S(1)}, bf16[4,272,128]{2,1,0:T(8,128)(2,1)S(1)}, u32[]{:S(2)}, u32[]{:S(2)}) %collective-permute-start.23) | collective-permute-done | bytes 278560 | tf_op jit(solution)/shard_map/ppermute | solution.py:412
  92.5 1.6 %merge.7 = (bf16[4,272,128]{2,1,0:T(8,128)(2,1)S(1)}, bf16[4,272,128]{2,1,0:T(8,128)(2,1)S(1)}) custom-call(s32[66]{0:T(128)S(1)} %pad_add_fusion.scal, s32[64,32]{1,0:T(8,128)S(1)} %bitcast.21, bf16[3,2,272,128]{3,2,1,0:T(8,128)(2,1)S(1)} %get-tuple-element.39.refs_0_, bf16[3,2,272,128]{3,2,1,0:T(8,128)(2,1)S(1)} %collective-permute-done.7.refs_1_, ...), custom_call_target="tpu_custom_call" | custom-call | flops 1000 | bytes 1000 | tf_op jit(solution)/shard_map/merge/pallas_call | solution.py:311
  94.5 3.0 %collective-permute-start.25 = (bf16[4,272,128]{2,1,0:T(8,128)(2,1)S(1)}, bf16[4,272,128]{2,1,0:T(8,128)(2,1)S(1)}, u32[]{:S(2)}, u32[]{:S(2)}) collective-permute-start(bf16[4,272,128]{2,1,0:T(8,128)(2,1)S(1)} %get-tuple-element.60), channel_id=1, source_target_pairs={{0,56},{8,0},{16,8},{24,16},{32,24},{40,32},{48,40},{56,48},{64,12... | collective-permute-start | bytes 835592 | tf_op jit(solution)/shard_map/ppermute | solution.py:412
  98.7 3.2 %collective-permute-done.24.refs_0_ = bf16[4,272,128]{2,1,0:T(8,128)(2,1)S(1)} collective-permute-done((bf16[4,272,128]{2,1,0:T(8,128)(2,1)S(1)}, bf16[4,272,128]{2,1,0:T(8,128)(2,1)S(1)}, u32[]{:S(2)}, u32[]{:S(2)}) %collective-permute-start.24) | collective-permute-done | bytes 278560 | tf_op jit(solution)/shard_map/ppermute | solution.py:412
  (61 shorter events, 20.4 us)
Async XLA Ops:
  3.5 18.9 %collective-permute-start.5 = (bf16[4,256,128]{2,1,0:T(8,128)(2,1)}, bf16[4,256,128]{2,1,0:T(8,128)(2,1)}, u32[]{:S(2)}, u32[]{:S(2)}) collective-permute-start(bf16[4,256,128]{2,1,0:T(8,128)(2,1)} %get-tuple-element.36.refs_0_.rest_0_.refs_5_), channel_id=1, source_target_pairs={{0,2},{1,3},{2,4},{3,5},{4,6},{5,7},{6,0},{7,1},{8,10},{9,11},{10,... | collective-permute-start | bytes 786440 | tf_op jit(solution)/shard_map/ppermute | solution.py:372
  5.0 17.9 %collective-permute-start.3 = (bf16[4,256,128]{2,1,0:T(8,128)(2,1)}, bf16[4,256,128]{2,1,0:T(8,128)(2,1)}, u32[]{:S(2)}, u32[]{:S(2)}) collective-permute-start(bf16[4,256,128]{2,1,0:T(8,128)(2,1)} %get-tuple-element.36.refs_0_.rest_0_.refs_5_), channel_id=1, source_target_pairs={{0,4},{1,5},{2,6},{3,7},{4,0},{5,1},{6,2},{7,3},{8,12},{9,13},{10,... | collective-permute-start | bytes 786440 | tf_op jit(solution)/shard_map/ppermute | solution.py:372
  7.7 15.3 %collective-permute-start.1 = (bf16[4,256,128]{2,1,0:T(8,128)(2,1)}, bf16[4,256,128]{2,1,0:T(8,128)(2,1)}, u32[]{:S(2)}, u32[]{:S(2)}) collective-permute-start(bf16[4,256,128]{2,1,0:T(8,128)(2,1)} %get-tuple-element.36.refs_0_.rest_0_.refs_5_), channel_id=1, source_target_pairs={{0,6},{1,7},{2,0},{3,1},{4,2},{5,3},{6,4},{7,5},{8,14},{9,15},{10,... | collective-permute-start | bytes 786440 | tf_op jit(solution)/shard_map/ppermute | solution.py:372
  10.6 23.1 %all-to-all-start = ((f32[32,5,4,128]{3,2,1,0:T(4,128)}), f32[32,5,4,128]{3,2,1,0:T(4,128)S(1)}, u32[]{:S(2)}, u32[]{:S(2)}) async-start(f32[32,5,4,128]{3,2,1,0:T(4,128)} %broadcast_in_dim.10), calls=%async_computation | async-start | bytes 655360 | tf_op jit(solution)/shard_map/all_to_all | solution.py:382
  22.3 4.8 %collective-permute-start = (bf16[4,256,128]{2,1,0:T(8,128)(2,1)}, bf16[4,256,128]{2,1,0:T(8,128)(2,1)}, u32[]{:S(2)}, u32[]{:S(2)}) collective-permute-start(bf16[4,256,128]{2,1,0:T(8,128)(2,1)} %get-tuple-element.36.refs_0_.rest_0_.refs_5_), channel_id=1, source_target_pairs={{0,1},{1,0},{2,3},{3,2},{4,5},{5,4},{6,7},{7,6},{8,9},{9,8},{10,11... | collective-permute-start | bytes 786440 | tf_op jit(solution)/shard_map/ppermute | solution.py:387
  37.5 11.8 %collective-permute-start.16 = (bf16[1,2,272,128]{3,2,1,0:T(8,128)(2,1)S(1)}, bf16[1,2,272,128]{3,2,1,0:T(8,128)(2,1)S(1)}, u32[]{:S(2)}, u32[]{:S(2)}) collective-permute-start(bf16[1,2,272,128]{3,2,1,0:T(8,128)(2,1)S(1)} %get-tuple-element.52), channel_id=1, source_target_pairs={{0,64},{8,72},{16,80},{24,88},{32,96},{40,104},{48,112},{56,120},{... | collective-permute-start | bytes 417800 | tf_op jit(solution)/shard_map/ppermute | solution.py:398
  38.5 10.8 %collective-permute-start.17 = (bf16[1,2,272,128]{3,2,1,0:T(8,128)(2,1)S(1)}, bf16[1,2,272,128]{3,2,1,0:T(8,128)(2,1)S(1)}, u32[]{:S(2)}, u32[]{:S(2)}) collective-permute-start(bf16[1,2,272,128]{3,2,1,0:T(8,128)(2,1)S(1)} %get-tuple-element.53), channel_id=1, source_target_pairs={{0,128},{8,136},{16,144},{24,152},{32,160},{40,168},{48,176},{56,1... | collective-permute-start | bytes 417800 | tf_op jit(solution)/shard_map/ppermute | solution.py:398
  41.1 8.3 %collective-permute-start.18 = (bf16[1,2,272,128]{3,2,1,0:T(8,128)(2,1)S(1)}, bf16[1,2,272,128]{3,2,1,0:T(8,128)(2,1)S(1)}, u32[]{:S(2)}, u32[]{:S(2)}) collective-permute-start(bf16[1,2,272,128]{3,2,1,0:T(8,128)(2,1)S(1)} %get-tuple-element.54), channel_id=1, source_target_pairs={{0,192},{8,200},{16,208},{24,216},{32,224},{40,232},{48,240},{56,2... | collective-permute-start | bytes 417800 | tf_op jit(solution)/shard_map/ppermute | solution.py:398
  45.5 13.2 %collective-permute-start.13 = (bf16[2,2,272,128]{3,2,1,0:T(8,128)(2,1)S(1)}, bf16[2,2,272,128]{3,2,1,0:T(8,128)(2,1)S(1)}, u32[]{:S(2)}, u32[]{:S(2)}) collective-permute-start(bf16[2,2,272,128]{3,2,1,0:T(8,128)(2,1)S(1)} %get-tuple-element.48), channel_id=1, source_target_pairs={{0,64},{8,72},{16,80},{24,88},{32,96},{40,104},{48,112},{56,120},{... | collective-permute-start | bytes 835592 | tf_op jit(solution)/shard_map/ppermute | solution.py:398
  47.0 14.4 %collective-permute-start.14 = (bf16[2,2,272,128]{3,2,1,0:T(8,128)(2,1)S(1)}, bf16[2,2,272,128]{3,2,1,0:T(8,128)(2,1)S(1)}, u32[]{:S(2)}, u32[]{:S(2)}) collective-permute-start(bf16[2,2,272,128]{3,2,1,0:T(8,128)(2,1)S(1)} %get-tuple-element.49), channel_id=1, source_target_pairs={{0,128},{8,136},{16,144},{24,152},{32,160},{40,168},{48,176},{56,1... | collective-permute-start | bytes 835592 | tf_op jit(solution)/shard_map/ppermute | solution.py:398
  49.3 12.1 %collective-permute-start.15 = (bf16[2,2,272,128]{3,2,1,0:T(8,128)(2,1)S(1)}, bf16[2,2,272,128]{3,2,1,0:T(8,128)(2,1)S(1)}, u32[]{:S(2)}, u32[]{:S(2)}) collective-permute-start(bf16[2,2,272,128]{3,2,1,0:T(8,128)(2,1)S(1)} %get-tuple-element.50), channel_id=1, source_target_pairs={{0,192},{8,200},{16,208},{24,216},{32,224},{40,232},{48,240},{56,2... | collective-permute-start | bytes 835592 | tf_op jit(solution)/shard_map/ppermute | solution.py:398
  50.7 10.7 %collective-permute-start.19 = (bf16[4,272,128]{2,1,0:T(8,128)(2,1)S(1)}, bf16[4,272,128]{2,1,0:T(8,128)(2,1)S(1)}, u32[]{:S(2)}, u32[]{:S(2)}) collective-permute-start(bf16[4,272,128]{2,1,0:T(8,128)(2,1)S(1)} %merge.4), channel_id=1, source_target_pairs={{0,8},{8,16},{16,24},{24,32},{32,40},{40,48},{48,56},{56,0},{64,72... | collective-permute-start | bytes 835592 | tf_op jit(solution)/shard_map/ppermute | solution.py:412
  56.7 17.7 %collective-permute-start.10 = (bf16[2,2,272,128]{3,2,1,0:T(8,128)(2,1)S(1)}, bf16[2,2,272,128]{3,2,1,0:T(8,128)(2,1)S(1)}, u32[]{:S(2)}, u32[]{:S(2)}) collective-permute-start(bf16[2,2,272,128]{3,2,1,0:T(8,128)(2,1)S(1)} %get-tuple-element.44), channel_id=1, source_target_pairs={{0,64},{8,72},{16,80},{24,88},{32,96},{40,104},{48,112},{56,120},{... | collective-permute-start | bytes 835592 | tf_op jit(solution)/shard_map/ppermute | solution.py:398
  58.7 15.9 %collective-permute-start.11 = (bf16[2,2,272,128]{3,2,1,0:T(8,128)(2,1)S(1)}, bf16[2,2,272,128]{3,2,1,0:T(8,128)(2,1)S(1)}, u32[]{:S(2)}, u32[]{:S(2)}) collective-permute-start(bf16[2,2,272,128]{3,2,1,0:T(8,128)(2,1)S(1)} %get-tuple-element.45), channel_id=1, source_target_pairs={{0,128},{8,136},{16,144},{24,152},{32,160},{40,168},{48,176},{56,1... | collective-permute-start | bytes 835592 | tf_op jit(solution)/shard_map/ppermute | solution.py:398
  61.4 15.7 %collective-permute-start.12 = (bf16[2,2,272,128]{3,2,1,0:T(8,128)(2,1)S(1)}, bf16[2,2,272,128]{3,2,1,0:T(8,128)(2,1)S(1)}, u32[]{:S(2)}, u32[]{:S(2)}) collective-permute-start(bf16[2,2,272,128]{3,2,1,0:T(8,128)(2,1)S(1)} %get-tuple-element.46), channel_id=1, source_target_pairs={{0,192},{8,200},{16,208},{24,216},{32,224},{40,232},{48,240},{56,2... | collective-permute-start | bytes 835592 | tf_op jit(solution)/shard_map/ppermute | solution.py:398
  63.0 16.7 %collective-permute-start.20 = (bf16[4,272,128]{2,1,0:T(8,128)(2,1)S(1)}, bf16[4,272,128]{2,1,0:T(8,128)(2,1)S(1)}, u32[]{:S(2)}, u32[]{:S(2)}) collective-permute-start(bf16[4,272,128]{2,1,0:T(8,128)(2,1)S(1)} %get-tuple-element.55), channel_id=1, source_target_pairs={{0,8},{8,16},{16,24},{24,32},{32,40},{40,48},{48,56},{56,0},{64,72... | collective-permute-start | bytes 835592 | tf_op jit(solution)/shard_map/ppermute | solution.py:412
  69.5 10.2 %collective-permute-start.21 = (bf16[4,272,128]{2,1,0:T(8,128)(2,1)S(1)}, bf16[4,272,128]{2,1,0:T(8,128)(2,1)S(1)}, u32[]{:S(2)}, u32[]{:S(2)}) collective-permute-start(bf16[4,272,128]{2,1,0:T(8,128)(2,1)S(1)} %get-tuple-element.56), channel_id=1, source_target_pairs={{0,56},{8,0},{16,8},{24,16},{32,24},{40,32},{48,40},{56,48},{64,12... | collective-permute-start | bytes 835592 | tf_op jit(solution)/shard_map/ppermute | solution.py:412
  74.5 10.1 %collective-permute-start.7 = (bf16[3,2,272,128]{3,2,1,0:T(8,128)(2,1)S(1)}, bf16[3,2,272,128]{3,2,1,0:T(8,128)(2,1)S(1)}, u32[]{:S(2)}, u32[]{:S(2)}) collective-permute-start(bf16[3,2,272,128]{3,2,1,0:T(8,128)(2,1)S(1)} %get-tuple-element.40), channel_id=1, source_target_pairs={{0,64},{8,72},{16,80},{24,88},{32,96},{40,104},{48,112},{56,120},{... | collective-permute-start | bytes 1253384 | tf_op jit(solution)/shard_map/ppermute | solution.py:398
  74.6 10.2 %collective-permute-start.8 = (bf16[3,2,272,128]{3,2,1,0:T(8,128)(2,1)S(1)}, bf16[3,2,272,128]{3,2,1,0:T(8,128)(2,1)S(1)}, u32[]{:S(2)}, u32[]{:S(2)}) collective-permute-start(bf16[3,2,272,128]{3,2,1,0:T(8,128)(2,1)S(1)} %get-tuple-element.41), channel_id=1, source_target_pairs={{0,128},{8,136},{16,144},{24,152},{32,160},{40,168},{48,176},{56,1... | collective-permute-start | bytes 1253384 | tf_op jit(solution)/shard_map/ppermute | solution.py:398
  77.1 12.0 %collective-permute-start.9 = (bf16[3,2,272,128]{3,2,1,0:T(8,128)(2,1)S(1)}, bf16[3,2,272,128]{3,2,1,0:T(8,128)(2,1)S(1)}, u32[]{:S(2)}, u32[]{:S(2)}) collective-permute-start(bf16[3,2,272,128]{3,2,1,0:T(8,128)(2,1)S(1)} %get-tuple-element.42), channel_id=1, source_target_pairs={{0,192},{8,200},{16,208},{24,216},{32,224},{40,232},{48,240},{56,2... | collective-permute-start | bytes 1253384 | tf_op jit(solution)/shard_map/ppermute | solution.py:398
  81.3 9.0 %collective-permute-start.22 = (bf16[4,272,128]{2,1,0:T(8,128)(2,1)S(1)}, bf16[4,272,128]{2,1,0:T(8,128)(2,1)S(1)}, u32[]{:S(2)}, u32[]{:S(2)}) collective-permute-start(bf16[4,272,128]{2,1,0:T(8,128)(2,1)S(1)} %get-tuple-element.57), channel_id=1, source_target_pairs={{0,8},{8,16},{16,24},{24,32},{32,40},{40,48},{48,56},{56,0},{64,72... | collective-permute-start | bytes 835592 | tf_op jit(solution)/shard_map/ppermute | solution.py:412
  83.3 9.2 %collective-permute-start.23 = (bf16[4,272,128]{2,1,0:T(8,128)(2,1)S(1)}, bf16[4,272,128]{2,1,0:T(8,128)(2,1)S(1)}, u32[]{:S(2)}, u32[]{:S(2)}) collective-permute-start(bf16[4,272,128]{2,1,0:T(8,128)(2,1)S(1)} %get-tuple-element.58), channel_id=1, source_target_pairs={{0,56},{8,0},{16,8},{24,16},{32,24},{40,32},{48,40},{56,48},{64,12... | collective-permute-start | bytes 835592 | tf_op jit(solution)/shard_map/ppermute | solution.py:412
  94.1 7.8 %collective-permute-start.24 = (bf16[4,272,128]{2,1,0:T(8,128)(2,1)S(1)}, bf16[4,272,128]{2,1,0:T(8,128)(2,1)S(1)}, u32[]{:S(2)}, u32[]{:S(2)}) collective-permute-start(bf16[4,272,128]{2,1,0:T(8,128)(2,1)S(1)} %get-tuple-element.59), channel_id=1, source_target_pairs={{0,8},{8,16},{16,24},{24,32},{32,40},{40,48},{48,56},{56,0},{64,72... | collective-permute-start | bytes 835592 | tf_op jit(solution)/shard_map/ppermute | solution.py:412
  94.5 7.5 %collective-permute-start.25 = (bf16[4,272,128]{2,1,0:T(8,128)(2,1)S(1)}, bf16[4,272,128]{2,1,0:T(8,128)(2,1)S(1)}, u32[]{:S(2)}, u32[]{:S(2)}) collective-permute-start(bf16[4,272,128]{2,1,0:T(8,128)(2,1)S(1)} %get-tuple-element.60), channel_id=1, source_target_pairs={{0,56},{8,0},{16,8},{24,16},{32,24},{40,32},{48,40},{56,48},{64,12... | collective-permute-start | bytes 835592 | tf_op jit(solution)/shard_map/ppermute | solution.py:412
  (7 other events, 49.1 us)

commit v4 on v3

--- a/solution.py
+++ b/solution.py
@@ -214,7 +214,7 @@
     first = isinstance(source, list)
     shape = (len(offsets), SLOTS, ROWS, BLK)
     out_shape = (jax.ShapeDtypeStruct(shape, BF16),) * NY
-    scratch = [pltpu.VMEM((max(1, 2 // len(offsets)),) + shape, BF16)]
+    scratch = [pltpu.VMEM((max(1, 4 // len(offsets)),) + shape, BF16)]
     if first:
         out_shape += (jax.ShapeDtypeStruct((SRC_BLOCKS, FEAT, BLK), BF16),)
         scratch.append(pltpu.SemaphoreType.DMA((PIECES,)))
@@ -365,6 +365,10 @@
     )(*dense, *home, bias.reshape(1, FEAT))
 
 
+def slots_list(*args):
+    return list(slots(*args))
+
+
 def body(features, weight, att_src, att_dst, bias, block_pairs, edge_masks):
     masks = edge_masks.reshape(OWNERS, SLOTS, BLK, BLK)
     hidden = jnp.dot(features, weight, preferred_element_type=F32).astype(BF16)
@@ -391,7 +395,7 @@
     made, parts = [], []
     source = pieces
     for step, offsets in enumerate(PLAN):
-        made.append(slots(offsets, scal, token, masks, told, att, source))
+        made.append(slots_list(offsets, scal, token, masks, told, att, source))
         if step == 0:
             source = made[0][NY]
         parts.append(
@@ -406,6 +410,8 @@
             parts[step][0], parts[step + 1][1] = lax.optimization_barrier(
                 (parts[step][0], parts[step + 1][1])
             )
+        if step == 1:
+            parts[1][0], made[3][0] = lax.optimization_barrier((parts[1][0], made[3][0]))
         dense = sum((coming[offset] for offset, _ in work), ())
         sent = merge_group(work, scal, every_pair, parts[step], dense)
         for (offset, _), chunk in zip(work, sent, strict=True):

time: 103 us -> 100 us (0.971); the launches traced: 103 us -> 99 us
  starting transfers between devices: 51.5 us -> 45.4 us
  waiting for transfers between devices: 17.8 us -> 20.7 us
  Pallas kernels: 27.1 us -> 25.6 us
    ppermute x7, starting transfers between devices: 15.3 us -> 11 us  [body(): hop = lax.ppermute(chunk, 'src', z_from(NEXT[offset] - offset))]
    ppermute x12, waiting for transfers between devices: 4.55 us -> 6.39 us  [body(): lax.ppermute(made[-1][k], 'src', y_from(-k))]
    pallas_call x4, Pallas kernels: 16.4 us -> 15 us  [slots(): pl.pallas_call(functools.partial(slots_kernel, offsets, first), out_shape...]
    ppermute x3, starting transfers between devices: 5.66 us -> 4.44 us  [body(): lax.ppermute(hidden, 'dst', x_from(k))]
  transfers between devices with their start and end apart: 27 -> 27, of which waited for: 6 -> 8; matrix products, arithmetic and copies ran while one was open for 2% -> 2% of each run, Pallas kernels for 19% -> 19%
where the time goes in v4:
time: 100 us; the launch traced here: 99 us
  starting transfers between devices  45.4 us (45%)
  Pallas kernels  25.6 us (26%)
  waiting for transfers between devices  20.7 us (21%)
  local copies, waits for them, and re-layouts  4.29 us (4%)
  other arithmetic  1.49 us (1%)
  matrix products  1.36 us (1%)
    ppermute x12, starting transfers between devices, body(): lax.ppermute(made[-1][k], 'src', y_from(-k))  17.2 us
    pallas_call x4, Pallas kernels, slots(): pl.pallas_call(functools.partial(slots_kernel, offsets, first), out_shape...  15 us
    all_to_all x1, starting transfers between devices, body(): lax.all_to_all(jnp.broadcast_to(told[None], (OWNERS,) + told.shape), 'src...  11.7 us
    ppermute x7, starting transfers between devices, body(): hop = lax.ppermute(chunk, 'src', z_from(NEXT[offset] - offset))  11 us
    ppermute x7, waiting for transfers between devices, body(): hop = lax.ppermute(chunk, 'src', z_from(NEXT[offset] - offset))  7.61 us
    all_to_all x1, waiting for transfers between devices, body(): lax.all_to_all(jnp.broadcast_to(told[None], (OWNERS,) + told.shape), 'src...  6.64 us
    ppermute x12, waiting for transfers between devices, body(): lax.ppermute(made[-1][k], 'src', y_from(-k))  6.39 us
    pallas_call x4, Pallas kernels, merge_group(): pl.pallas_call(functools.partial(merge_kernel, work), out_shape=(jax.Shap...  6.06 us
  transfers between devices with their start and end apart: 27, of which 8 were waited for; matrix products, arithmetic and copies ran while one was open for 2% of the time, Pallas kernels for 19%

profile of v4, /device:TPU:8, one launch (start us, length us, event | category | flops | bytes accessed | tf_op | source)
XLA Modules:
  0.0 99.0 jit_solution(15189464843376155090)
XLA Ops:
  4.2 2.8 %collective-permute-start.1 = (bf16[4,256,128]{2,1,0:T(8,128)(2,1)}, bf16[4,256,128]{2,1,0:T(8,128)(2,1)}, u32[]{:S(2)}, u32[]{:S(2)}) collective-permute-start(bf16[4,256,128]{2,1,0:T(8,128)(2,1)} %get-tuple-element.37.refs_0_.rest_0_.refs_5_), channel_id=1, source_target_pairs={{0,6},{1,7},{2,0},{3,1},{4,2},{5,3},{6,4},{7,5},{8,14},{9,15},{10,... | collective-permute-start | bytes 786440 | tf_op jit(solution)/shard_map/ppermute | solution.py:376
  10.1 11.7 %all-to-all-start = ((f32[32,5,4,128]{3,2,1,0:T(4,128)}), f32[32,5,4,128]{3,2,1,0:T(4,128)S(1)}, u32[]{:S(2)}, u32[]{:S(2)}) async-start(f32[32,5,4,128]{3,2,1,0:T(4,128)} %broadcast_in_dim.10), calls=%async_computation | async-start | bytes 655360 | tf_op jit(solution)/shard_map/all_to_all | solution.py:386
  23.1 2.2 %copy-done.1 = s32[1,1,32,2,128,128]{5,4,3,2,1,0:T(8,128)S(1)} copy-done((s32[1,1,32,2,128,128]{5,4,3,2,1,0:T(8,128)S(1)}, s32[1,1,32,2,128,128]{5,4,3,2,1,0:T(8,128)}, u32[]{:S(2)}) %copy-start.1) | copy-done | bytes 4194328
  26.6 6.6 %all-to-all-done.targets = f32[32,5,4,128]{3,2,1,0:T(4,128)S(1)} async-done(((f32[32,5,4,128]{3,2,1,0:T(4,128)}), f32[32,5,4,128]{3,2,1,0:T(4,128)S(1)}, u32[]{:S(2)}, u32[]{:S(2)}) %all-to-all-start) | async-done | bytes 327712 | tf_op jit(solution)/shard_map/all_to_all | solution.py:386
  33.2 3.5 %slots.4 = (bf16[1,2,272,128]{3,2,1,0:T(8,128)(2,1)S(1)}, bf16[1,2,272,128]{3,2,1,0:T(8,128)(2,1)S(1)}, bf16[1,2,272,128]{3,2,1,0:T(8,128)(2,1)S(1)}, bf16[1,2,2...) custom-call(s32[66]{0:T(128)S(1)} %pad_add_fusion.scal, f32[8,128]{1,0:T(8,128)S(1)} %gate.1.token, ...), custom_call_target="tpu_custom_call" | custom-call | flops 1000 | bytes 1000 | tf_op jit(solution)/shard_map/slots/pallas_call | solution.py:221
  37.7 2.5 %collective-permute-start.17 = (bf16[1,2,272,128]{3,2,1,0:T(8,128)(2,1)S(1)}, bf16[1,2,272,128]{3,2,1,0:T(8,128)(2,1)S(1)}, u32[]{:S(2)}, u32[]{:S(2)}) collective-permute-start(bf16[1,2,272,128]{3,2,1,0:T(8,128)(2,1)S(1)} %get-tuple-element.55), channel_id=1, source_target_pairs={{0,128},{8,136},{16,144},{24,152},{32,160},{40,168},{48,176},{56,1... | collective-permute-start | bytes 417800 | tf_op jit(solution)/shard_map/ppermute | solution.py:402
  40.8 3.3 %slots.7 = (bf16[2,2,272,128]{3,2,1,0:T(8,128)(2,1)S(1)}, bf16[2,2,272,128]{3,2,1,0:T(8,128)(2,1)S(1)}, bf16[2,2,272,128]{3,2,1,0:T(8,128)(2,1)S(1)}, bf16[2,2,272,128]{3,2,1,0:T(8,128)(2,1)S(1)}) custom-call(s32[66]{0:T(128)S(1)} %pad_add_fusion.scal, f32[8,128]{1,0:T(8,128)S(1)} %gate.1.token, f32[32,5,4,128]{3,2,1,0:T(4,128)S(1)} %all-to-all-done.targets, ...), custom_call_target="tpu_custom_call" | custom-call | flops 1000 | bytes 1000 | tf_op jit(solution)/shard_map/slots/pallas_call | solution.py:221
  44.1 1.6 %collective-permute-start.13 = (bf16[2,2,272,128]{3,2,1,0:T(8,128)(2,1)S(1)}, bf16[2,2,272,128]{3,2,1,0:T(8,128)(2,1)S(1)}, u32[]{:S(2)}, u32[]{:S(2)}) collective-permute-start(bf16[2,2,272,128]{3,2,1,0:T(8,128)(2,1)S(1)} %get-tuple-element.50), channel_id=1, source_target_pairs={{0,64},{8,72},{16,80},{24,88},{32,96},{40,104},{48,112},{56,120},{... | collective-permute-start | bytes 835592 | tf_op jit(solution)/shard_map/ppermute | solution.py:402
  45.6 2.2 %collective-permute-start.14 = (bf16[2,2,272,128]{3,2,1,0:T(8,128)(2,1)S(1)}, bf16[2,2,272,128]{3,2,1,0:T(8,128)(2,1)S(1)}, u32[]{:S(2)}, u32[]{:S(2)}) collective-permute-start(bf16[2,2,272,128]{3,2,1,0:T(8,128)(2,1)S(1)} %get-tuple-element.51), channel_id=1, source_target_pairs={{0,128},{8,136},{16,144},{24,152},{32,160},{40,168},{48,176},{56,1... | collective-permute-start | bytes 835592 | tf_op jit(solution)/shard_map/ppermute | solution.py:402
  51.4 3.3 %slots.6 = (bf16[2,2,272,128]{3,2,1,0:T(8,128)(2,1)S(1)}, bf16[2,2,272,128]{3,2,1,0:T(8,128)(2,1)S(1)}, bf16[2,2,272,128]{3,2,1,0:T(8,128)(2,1)S(1)}, bf16[2,2,272,128]{3,2,1,0:T(8,128)(2,1)S(1)}) custom-call(s32[66]{0:T(128)S(1)} %pad_add_fusion.scal, f32[8,128]{1,0:T(8,128)S(1)} %gate.1.token, f32[32,5,4,128]{3,2,1,0:T(4,128)S(1)} %all-to-all-done.targets, ...), custom_call_target="tpu_custom_call" | custom-call | flops 1000 | bytes 1000 | tf_op jit(solution)/shard_map/slots/pallas_call | solution.py:221
  54.7 2.0 %collective-permute-start.10 = (bf16[2,2,272,128]{3,2,1,0:T(8,128)(2,1)S(1)}, bf16[2,2,272,128]{3,2,1,0:T(8,128)(2,1)S(1)}, u32[]{:S(2)}, u32[]{:S(2)}) collective-permute-start(bf16[2,2,272,128]{3,2,1,0:T(8,128)(2,1)S(1)} %get-tuple-element.45), channel_id=1, source_target_pairs={{0,64},{8,72},{16,80},{24,88},{32,96},{40,104},{48,112},{56,120},{... | collective-permute-start | bytes 835592 | tf_op jit(solution)/shard_map/ppermute | solution.py:402
  56.7 2.7 %collective-permute-start.11 = (bf16[2,2,272,128]{3,2,1,0:T(8,128)(2,1)S(1)}, bf16[2,2,272,128]{3,2,1,0:T(8,128)(2,1)S(1)}, u32[]{:S(2)}, u32[]{:S(2)}) collective-permute-start(bf16[2,2,272,128]{3,2,1,0:T(8,128)(2,1)S(1)} %get-tuple-element.46), channel_id=1, source_target_pairs={{0,128},{8,136},{16,144},{24,152},{32,160},{40,168},{48,176},{56,1... | collective-permute-start | bytes 835592 | tf_op jit(solution)/shard_map/ppermute | solution.py:402
  59.4 4.9 %slots.5 = (bf16[3,2,272,128]{3,2,1,0:T(8,128)(2,1)S(1)}, bf16[3,2,272,128]{3,2,1,0:T(8,128)(2,1)S(1)}, bf16[3,2,272,128]{3,2,1,0:T(8,128)(2,1)S(1)}, bf16[3,2,272,128]{3,2,1,0:T(8,128)(2,1)S(1)}) custom-call(s32[66]{0:T(128)S(1)} %pad_add_fusion.scal, f32[8,128]{1,0:T(8,128)S(1)} %gate.1.token, f32[32,5,4,128]{3,2,1,0:T(4,128)S(1)} %all-to-all-done.targets, ...), custom_call_target="tpu_custom_call" | custom-call | flops 1000 | bytes 1000 | tf_op jit(solution)/shard_map/slots/pallas_call | solution.py:221
  64.4 1.6 %merge.5 = (bf16[4,272,128]{2,1,0:T(8,128)(2,1)S(1)}, bf16[4,272,128]{2,1,0:T(8,128)(2,1)S(1)}) custom-call(s32[66]{0:T(128)S(1)} %pad_add_fusion.scal, s32[64,32]{1,0:T(8,128)S(1)} %bitcast.19, bf16[2,2,272,128]{3,2,1,0:T(8,128)(2,1)S(1)} %get-tuple-element.49.refs_0_, bf16[2,2,272,128]{3,2,1,0:T(8,128)(2,1)S(1)} %collective-permute-done.13.refs_1_, ...), custom_call_target="tpu_custom_call" | custom-call | flops 1000 | bytes 1000 | tf_op jit(solution)/shard_map/merge/pallas_call | solution.py:311
  66.0 3.2 %collective-permute-start.20 = (bf16[4,272,128]{2,1,0:T(8,128)(2,1)S(1)}, bf16[4,272,128]{2,1,0:T(8,128)(2,1)S(1)}, u32[]{:S(2)}, u32[]{:S(2)}) collective-permute-start(bf16[4,272,128]{2,1,0:T(8,128)(2,1)S(1)} %get-tuple-element.57), channel_id=1, source_target_pairs={{0,8},{8,16},{16,24},{24,32},{32,40},{40,48},{48,56},{56,0},{64,72... | collective-permute-start | bytes 835592 | tf_op jit(solution)/shard_map/ppermute | solution.py:418
  69.3 2.0 %collective-permute-start.7 = (bf16[3,2,272,128]{3,2,1,0:T(8,128)(2,1)S(1)}, bf16[3,2,272,128]{3,2,1,0:T(8,128)(2,1)S(1)}, u32[]{:S(2)}, u32[]{:S(2)}) collective-permute-start(bf16[3,2,272,128]{3,2,1,0:T(8,128)(2,1)S(1)} %get-tuple-element.41), channel_id=1, source_target_pairs={{0,64},{8,72},{16,80},{24,88},{32,96},{40,104},{48,112},{56,120},{... | collective-permute-start | bytes 1253384 | tf_op jit(solution)/shard_map/ppermute | solution.py:402
  71.3 2.0 %collective-permute-start.8 = (bf16[3,2,272,128]{3,2,1,0:T(8,128)(2,1)S(1)}, bf16[3,2,272,128]{3,2,1,0:T(8,128)(2,1)S(1)}, u32[]{:S(2)}, u32[]{:S(2)}) collective-permute-start(bf16[3,2,272,128]{3,2,1,0:T(8,128)(2,1)S(1)} %get-tuple-element.42), channel_id=1, source_target_pairs={{0,128},{8,136},{16,144},{24,152},{32,160},{40,168},{48,176},{56,1... | collective-permute-start | bytes 1253384 | tf_op jit(solution)/shard_map/ppermute | solution.py:402
  74.5 2.8 %collective-permute-done.21.refs_5_ = bf16[4,272,128]{2,1,0:T(8,128)(2,1)S(1)} collective-permute-done((bf16[4,272,128]{2,1,0:T(8,128)(2,1)S(1)}, bf16[4,272,128]{2,1,0:T(8,128)(2,1)S(1)}, u32[]{:S(2)}, u32[]{:S(2)}) %collective-permute-start.21) | collective-permute-done | bytes 278560 | tf_op jit(solution)/shard_map/ppermute | solution.py:418
  77.3 1.6 %merge.6 = (bf16[4,272,128]{2,1,0:T(8,128)(2,1)S(1)}, bf16[4,272,128]{2,1,0:T(8,128)(2,1)S(1)}) custom-call(s32[66]{0:T(128)S(1)} %pad_add_fusion.scal, s32[64,32]{1,0:T(8,128)S(1)} %bitcast.20, bf16[2,2,272,128]{3,2,1,0:T(8,128)(2,1)S(1)} %get-tuple-element.44.refs_0_, bf16[2,2,272,128]{3,2,1,0:T(8,128)(2,1)S(1)} %collective-permute-done.10.refs_1_, ...), custom_call_target="tpu_custom_call" | custom-call | flops 1000 | bytes 1000 | tf_op jit(solution)/shard_map/merge/pallas_call | solution.py:311
  79.2 3.1 %collective-permute-start.23 = (bf16[4,272,128]{2,1,0:T(8,128)(2,1)S(1)}, bf16[4,272,128]{2,1,0:T(8,128)(2,1)S(1)}, u32[]{:S(2)}, u32[]{:S(2)}) collective-permute-start(bf16[4,272,128]{2,1,0:T(8,128)(2,1)S(1)} %get-tuple-element.60), channel_id=1, source_target_pairs={{0,56},{8,0},{16,8},{24,16},{32,24},{40,32},{48,40},{56,48},{64,12... | collective-permute-start | bytes 835592 | tf_op jit(solution)/shard_map/ppermute | solution.py:418
  83.4 4.3 %collective-permute-done.9.refs_3_ = bf16[3,2,272,128]{3,2,1,0:T(8,128)(2,1)S(1)} collective-permute-done((bf16[3,2,272,128]{3,2,1,0:T(8,128)(2,1)S(1)}, bf16[3,2,272,128]{3,2,1,0:T(8,128)(2,1)S(1)}, u32[]{:S(2)}, u32[]{:S(2)}) %collective-permute-start.9) | collective-permute-done | bytes 417824 | tf_op jit(solution)/shard_map/ppermute | solution.py:402
  87.7 1.6 %merge.7 = (bf16[4,272,128]{2,1,0:T(8,128)(2,1)S(1)}, bf16[4,272,128]{2,1,0:T(8,128)(2,1)S(1)}) custom-call(s32[66]{0:T(128)S(1)} %pad_add_fusion.scal, s32[64,32]{1,0:T(8,128)S(1)} %bitcast.21, bf16[3,2,272,128]{3,2,1,0:T(8,128)(2,1)S(1)} %get-tuple-element.40.refs_0_, bf16[3,2,272,128]{3,2,1,0:T(8,128)(2,1)S(1)} %collective-permute-done.7.refs_1_, ...), custom_call_target="tpu_custom_call" | custom-call | flops 1000 | bytes 1000 | tf_op jit(solution)/shard_map/merge/pallas_call | solution.py:311
  89.3 2.1 %collective-permute-start.24 = (bf16[4,272,128]{2,1,0:T(8,128)(2,1)S(1)}, bf16[4,272,128]{2,1,0:T(8,128)(2,1)S(1)}, u32[]{:S(2)}, u32[]{:S(2)}) collective-permute-start(bf16[4,272,128]{2,1,0:T(8,128)(2,1)S(1)} %get-tuple-element.61), channel_id=1, source_target_pairs={{0,8},{8,16},{16,24},{24,32},{32,40},{40,48},{48,56},{56,0},{64,72... | collective-permute-start | bytes 835592 | tf_op jit(solution)/shard_map/ppermute | solution.py:418
  93.9 3.2 %collective-permute-done.24.refs_0_ = bf16[4,272,128]{2,1,0:T(8,128)(2,1)S(1)} collective-permute-done((bf16[4,272,128]{2,1,0:T(8,128)(2,1)S(1)}, bf16[4,272,128]{2,1,0:T(8,128)(2,1)S(1)}, u32[]{:S(2)}, u32[]{:S(2)}) %collective-permute-start.24) | collective-permute-done | bytes 278560 | tf_op jit(solution)/shard_map/ppermute | solution.py:418
  (61 shorter events, 22.1 us)
Async XLA Ops:
  4.2 17.7 %collective-permute-start.1 = (bf16[4,256,128]{2,1,0:T(8,128)(2,1)}, bf16[4,256,128]{2,1,0:T(8,128)(2,1)}, u32[]{:S(2)}, u32[]{:S(2)}) collective-permute-start(bf16[4,256,128]{2,1,0:T(8,128)(2,1)} %get-tuple-element.37.refs_0_.rest_0_.refs_5_), channel_id=1, source_target_pairs={{0,6},{1,7},{2,0},{3,1},{4,2},{5,3},{6,4},{7,5},{8,14},{9,15},{10,... | collective-permute-start | bytes 786440 | tf_op jit(solution)/shard_map/ppermute | solution.py:376
  6.9 15.5 %collective-permute-start.3 = (bf16[4,256,128]{2,1,0:T(8,128)(2,1)}, bf16[4,256,128]{2,1,0:T(8,128)(2,1)}, u32[]{:S(2)}, u32[]{:S(2)}) collective-permute-start(bf16[4,256,128]{2,1,0:T(8,128)(2,1)} %get-tuple-element.37.refs_0_.rest_0_.refs_5_), channel_id=1, source_target_pairs={{0,4},{1,5},{2,6},{3,7},{4,0},{5,1},{6,2},{7,3},{8,12},{9,13},{10,... | collective-permute-start | bytes 786440 | tf_op jit(solution)/shard_map/ppermute | solution.py:376
  7.7 14.8 %collective-permute-start.5 = (bf16[4,256,128]{2,1,0:T(8,128)(2,1)}, bf16[4,256,128]{2,1,0:T(8,128)(2,1)}, u32[]{:S(2)}, u32[]{:S(2)}) collective-permute-start(bf16[4,256,128]{2,1,0:T(8,128)(2,1)} %get-tuple-element.37.refs_0_.rest_0_.refs_5_), channel_id=1, source_target_pairs={{0,2},{1,3},{2,4},{3,5},{4,6},{5,7},{6,0},{7,1},{8,10},{9,11},{10,... | collective-permute-start | bytes 786440 | tf_op jit(solution)/shard_map/ppermute | solution.py:376
  10.1 23.1 %all-to-all-start = ((f32[32,5,4,128]{3,2,1,0:T(4,128)}), f32[32,5,4,128]{3,2,1,0:T(4,128)S(1)}, u32[]{:S(2)}, u32[]{:S(2)}) async-start(f32[32,5,4,128]{3,2,1,0:T(4,128)} %broadcast_in_dim.10), calls=%async_computation | async-start | bytes 655360 | tf_op jit(solution)/shard_map/all_to_all | solution.py:386
  21.8 4.8 %collective-permute-start = (bf16[4,256,128]{2,1,0:T(8,128)(2,1)}, bf16[4,256,128]{2,1,0:T(8,128)(2,1)}, u32[]{:S(2)}, u32[]{:S(2)}) collective-permute-start(bf16[4,256,128]{2,1,0:T(8,128)(2,1)} %get-tuple-element.37.refs_0_.rest_0_.refs_5_), channel_id=1, source_target_pairs={{0,1},{1,0},{2,3},{3,2},{4,5},{5,4},{6,7},{7,6},{8,9},{9,8},{10,11... | collective-permute-start | bytes 786440 | tf_op jit(solution)/shard_map/ppermute | solution.py:391
  36.7 11.2 %collective-permute-start.16 = (bf16[1,2,272,128]{3,2,1,0:T(8,128)(2,1)S(1)}, bf16[1,2,272,128]{3,2,1,0:T(8,128)(2,1)S(1)}, u32[]{:S(2)}, u32[]{:S(2)}) collective-permute-start(bf16[1,2,272,128]{3,2,1,0:T(8,128)(2,1)S(1)} %get-tuple-element.54), channel_id=1, source_target_pairs={{0,64},{8,72},{16,80},{24,88},{32,96},{40,104},{48,112},{56,120},{... | collective-permute-start | bytes 417800 | tf_op jit(solution)/shard_map/ppermute | solution.py:402
  37.7 10.4 %collective-permute-start.17 = (bf16[1,2,272,128]{3,2,1,0:T(8,128)(2,1)S(1)}, bf16[1,2,272,128]{3,2,1,0:T(8,128)(2,1)S(1)}, u32[]{:S(2)}, u32[]{:S(2)}) collective-permute-start(bf16[1,2,272,128]{3,2,1,0:T(8,128)(2,1)S(1)} %get-tuple-element.55), channel_id=1, source_target_pairs={{0,128},{8,136},{16,144},{24,152},{32,160},{40,168},{48,176},{56,1... | collective-permute-start | bytes 417800 | tf_op jit(solution)/shard_map/ppermute | solution.py:402
  40.3 8.8 %collective-permute-start.18 = (bf16[1,2,272,128]{3,2,1,0:T(8,128)(2,1)S(1)}, bf16[1,2,272,128]{3,2,1,0:T(8,128)(2,1)S(1)}, u32[]{:S(2)}, u32[]{:S(2)}) collective-permute-start(bf16[1,2,272,128]{3,2,1,0:T(8,128)(2,1)S(1)} %get-tuple-element.56), channel_id=1, source_target_pairs={{0,192},{8,200},{16,208},{24,216},{32,224},{40,232},{48,240},{56,2... | collective-permute-start | bytes 417800 | tf_op jit(solution)/shard_map/ppermute | solution.py:402
  44.1 12.6 %collective-permute-start.13 = (bf16[2,2,272,128]{3,2,1,0:T(8,128)(2,1)S(1)}, bf16[2,2,272,128]{3,2,1,0:T(8,128)(2,1)S(1)}, u32[]{:S(2)}, u32[]{:S(2)}) collective-permute-start(bf16[2,2,272,128]{3,2,1,0:T(8,128)(2,1)S(1)} %get-tuple-element.50), channel_id=1, source_target_pairs={{0,64},{8,72},{16,80},{24,88},{32,96},{40,104},{48,112},{56,120},{... | collective-permute-start | bytes 835592 | tf_op jit(solution)/shard_map/ppermute | solution.py:402
  45.6 13.8 %collective-permute-start.14 = (bf16[2,2,272,128]{3,2,1,0:T(8,128)(2,1)S(1)}, bf16[2,2,272,128]{3,2,1,0:T(8,128)(2,1)S(1)}, u32[]{:S(2)}, u32[]{:S(2)}) collective-permute-start(bf16[2,2,272,128]{3,2,1,0:T(8,128)(2,1)S(1)} %get-tuple-element.51), channel_id=1, source_target_pairs={{0,128},{8,136},{16,144},{24,152},{32,160},{40,168},{48,176},{56,1... | collective-permute-start | bytes 835592 | tf_op jit(solution)/shard_map/ppermute | solution.py:402
  47.9 16.5 %collective-permute-start.15 = (bf16[2,2,272,128]{3,2,1,0:T(8,128)(2,1)S(1)}, bf16[2,2,272,128]{3,2,1,0:T(8,128)(2,1)S(1)}, u32[]{:S(2)}, u32[]{:S(2)}) collective-permute-start(bf16[2,2,272,128]{3,2,1,0:T(8,128)(2,1)S(1)} %get-tuple-element.52), channel_id=1, source_target_pairs={{0,192},{8,200},{16,208},{24,216},{32,224},{40,232},{48,240},{56,2... | collective-permute-start | bytes 835592 | tf_op jit(solution)/shard_map/ppermute | solution.py:402
  50.4 14.0 %collective-permute-start.19 = (bf16[4,272,128]{2,1,0:T(8,128)(2,1)S(1)}, bf16[4,272,128]{2,1,0:T(8,128)(2,1)S(1)}, u32[]{:S(2)}, u32[]{:S(2)}) collective-permute-start(bf16[4,272,128]{2,1,0:T(8,128)(2,1)S(1)} %merge.4), channel_id=1, source_target_pairs={{0,8},{8,16},{16,24},{24,32},{32,40},{40,48},{48,56},{56,0},{64,72... | collective-permute-start | bytes 835592 | tf_op jit(solution)/shard_map/ppermute | solution.py:418
  54.7 14.6 %collective-permute-start.10 = (bf16[2,2,272,128]{3,2,1,0:T(8,128)(2,1)S(1)}, bf16[2,2,272,128]{3,2,1,0:T(8,128)(2,1)S(1)}, u32[]{:S(2)}, u32[]{:S(2)}) collective-permute-start(bf16[2,2,272,128]{3,2,1,0:T(8,128)(2,1)S(1)} %get-tuple-element.45), channel_id=1, source_target_pairs={{0,64},{8,72},{16,80},{24,88},{32,96},{40,104},{48,112},{56,120},{... | collective-permute-start | bytes 835592 | tf_op jit(solution)/shard_map/ppermute | solution.py:402
  56.7 14.6 %collective-permute-start.11 = (bf16[2,2,272,128]{3,2,1,0:T(8,128)(2,1)S(1)}, bf16[2,2,272,128]{3,2,1,0:T(8,128)(2,1)S(1)}, u32[]{:S(2)}, u32[]{:S(2)}) collective-permute-start(bf16[2,2,272,128]{3,2,1,0:T(8,128)(2,1)S(1)} %get-tuple-element.46), channel_id=1, source_target_pairs={{0,128},{8,136},{16,144},{24,152},{32,160},{40,168},{48,176},{56,1... | collective-permute-start | bytes 835592 | tf_op jit(solution)/shard_map/ppermute | solution.py:402
  59.4 13.9 %collective-permute-start.12 = (bf16[2,2,272,128]{3,2,1,0:T(8,128)(2,1)S(1)}, bf16[2,2,272,128]{3,2,1,0:T(8,128)(2,1)S(1)}, u32[]{:S(2)}, u32[]{:S(2)}) collective-permute-start(bf16[2,2,272,128]{3,2,1,0:T(8,128)(2,1)S(1)} %get-tuple-element.47), channel_id=1, source_target_pairs={{0,192},{8,200},{16,208},{24,216},{32,224},{40,232},{48,240},{56,2... | collective-permute-start | bytes 835592 | tf_op jit(solution)/shard_map/ppermute | solution.py:402
  66.0 8.6 %collective-permute-start.20 = (bf16[4,272,128]{2,1,0:T(8,128)(2,1)S(1)}, bf16[4,272,128]{2,1,0:T(8,128)(2,1)S(1)}, u32[]{:S(2)}, u32[]{:S(2)}) collective-permute-start(bf16[4,272,128]{2,1,0:T(8,128)(2,1)S(1)} %get-tuple-element.57), channel_id=1, source_target_pairs={{0,8},{8,16},{16,24},{24,32},{32,40},{40,48},{48,56},{56,0},{64,72... | collective-permute-start | bytes 835592 | tf_op jit(solution)/shard_map/ppermute | solution.py:418
  69.2 8.2 %collective-permute-start.21 = (bf16[4,272,128]{2,1,0:T(8,128)(2,1)S(1)}, bf16[4,272,128]{2,1,0:T(8,128)(2,1)S(1)}, u32[]{:S(2)}, u32[]{:S(2)}) collective-permute-start(bf16[4,272,128]{2,1,0:T(8,128)(2,1)S(1)} %get-tuple-element.58), channel_id=1, source_target_pairs={{0,56},{8,0},{16,8},{24,16},{32,24},{40,32},{48,40},{56,48},{64,12... | collective-permute-start | bytes 835592 | tf_op jit(solution)/shard_map/ppermute | solution.py:418
  69.3 13.0 %collective-permute-start.7 = (bf16[3,2,272,128]{3,2,1,0:T(8,128)(2,1)S(1)}, bf16[3,2,272,128]{3,2,1,0:T(8,128)(2,1)S(1)}, u32[]{:S(2)}, u32[]{:S(2)}) collective-permute-start(bf16[3,2,272,128]{3,2,1,0:T(8,128)(2,1)S(1)} %get-tuple-element.41), channel_id=1, source_target_pairs={{0,64},{8,72},{16,80},{24,88},{32,96},{40,104},{48,112},{56,120},{... | collective-permute-start | bytes 1253384 | tf_op jit(solution)/shard_map/ppermute | solution.py:402
  71.3 12.1 %collective-permute-start.8 = (bf16[3,2,272,128]{3,2,1,0:T(8,128)(2,1)S(1)}, bf16[3,2,272,128]{3,2,1,0:T(8,128)(2,1)S(1)}, u32[]{:S(2)}, u32[]{:S(2)}) collective-permute-start(bf16[3,2,272,128]{3,2,1,0:T(8,128)(2,1)S(1)} %get-tuple-element.42), channel_id=1, source_target_pairs={{0,128},{8,136},{16,144},{24,152},{32,160},{40,168},{48,176},{56,1... | collective-permute-start | bytes 1253384 | tf_op jit(solution)/shard_map/ppermute | solution.py:402
  73.3 14.4 %collective-permute-start.9 = (bf16[3,2,272,128]{3,2,1,0:T(8,128)(2,1)S(1)}, bf16[3,2,272,128]{3,2,1,0:T(8,128)(2,1)S(1)}, u32[]{:S(2)}, u32[]{:S(2)}) collective-permute-start(bf16[3,2,272,128]{3,2,1,0:T(8,128)(2,1)S(1)} %get-tuple-element.43), channel_id=1, source_target_pairs={{0,192},{8,200},{16,208},{24,216},{32,224},{40,232},{48,240},{56,2... | collective-permute-start | bytes 1253384 | tf_op jit(solution)/shard_map/ppermute | solution.py:402
  78.9 8.8 %collective-permute-start.22 = (bf16[4,272,128]{2,1,0:T(8,128)(2,1)S(1)}, bf16[4,272,128]{2,1,0:T(8,128)(2,1)S(1)}, u32[]{:S(2)}, u32[]{:S(2)}) collective-permute-start(bf16[4,272,128]{2,1,0:T(8,128)(2,1)S(1)} %get-tuple-element.59), channel_id=1, source_target_pairs={{0,8},{8,16},{16,24},{24,32},{32,40},{40,48},{48,56},{56,0},{64,72... | collective-permute-start | bytes 835592 | tf_op jit(solution)/shard_map/ppermute | solution.py:418
  79.2 8.5 %collective-permute-start.23 = (bf16[4,272,128]{2,1,0:T(8,128)(2,1)S(1)}, bf16[4,272,128]{2,1,0:T(8,128)(2,1)S(1)}, u32[]{:S(2)}, u32[]{:S(2)}) collective-permute-start(bf16[4,272,128]{2,1,0:T(8,128)(2,1)S(1)} %get-tuple-element.60), channel_id=1, source_target_pairs={{0,56},{8,0},{16,8},{24,16},{32,24},{40,32},{48,40},{56,48},{64,12... | collective-permute-start | bytes 835592 | tf_op jit(solution)/shard_map/ppermute | solution.py:418
  89.3 7.8 %collective-permute-start.24 = (bf16[4,272,128]{2,1,0:T(8,128)(2,1)S(1)}, bf16[4,272,128]{2,1,0:T(8,128)(2,1)S(1)}, u32[]{:S(2)}, u32[]{:S(2)}) collective-permute-start(bf16[4,272,128]{2,1,0:T(8,128)(2,1)S(1)} %get-tuple-element.61), channel_id=1, source_target_pairs={{0,8},{8,16},{16,24},{24,32},{32,40},{40,48},{48,56},{56,0},{64,72... | collective-permute-start | bytes 835592 | tf_op jit(solution)/shard_map/ppermute | solution.py:418
  91.4 6.5 %collective-permute-start.25 = (bf16[4,272,128]{2,1,0:T(8,128)(2,1)S(1)}, bf16[4,272,128]{2,1,0:T(8,128)(2,1)S(1)}, u32[]{:S(2)}, u32[]{:S(2)}) collective-permute-start(bf16[4,272,128]{2,1,0:T(8,128)(2,1)S(1)} %get-tuple-element.62), channel_id=1, source_target_pairs={{0,56},{8,0},{16,8},{24,16},{32,24},{40,32},{48,40},{56,48},{64,12... | collective-permute-start | bytes 835592 | tf_op jit(solution)/shard_map/ppermute | solution.py:418
  (7 other events, 57.9 us)

commit v5 on v4

--- a/solution.py
+++ b/solution.py
@@ -280,7 +280,7 @@
     for k in range(NY):
         maker = owner_of(scal, -k, 0)
         for t in range(SLOTS):
-            place = every_pair[maker * SLOTS + t, owner] >> (SRC_BLOCKS.bit_length() - 1)
+            place = every_pair[(maker >> LOG_NZ) * SLOTS + t, owner] >> (SRC_BLOCKS.bit_length() - 1)
             found.append((refs[k], (n, t), place))
     return found
 
@@ -385,6 +385,9 @@
     told = jnp.concatenate([own_target, row], axis=0)
     told = lax.all_to_all(jnp.broadcast_to(told[None], (OWNERS,) + told.shape), "src", 0, 0)
     every_pair = told[:, NBD, :SLOTS, :OWNERS].astype(jnp.int32).reshape(OWNERS * SLOTS, OWNERS)
+    every_pair = lax.optimization_barrier(every_pair).reshape(NY, NZ, SLOTS, OWNERS)
+    every_pair = lax.dynamic_index_in_dim(every_pair, src % NZ, 1, keepdims=False)
+    every_pair = every_pair.reshape(NY * SLOTS, OWNERS)
 
     pieces = []
     for piece in along_x:
@@ -392,31 +395,38 @@
     masks = mask_bias(masks)
     token = gate(*pieces, masks)
 
-    made, parts = [], []
-    source = pieces
-    for step, offsets in enumerate(PLAN):
-        made.append(slots_list(offsets, scal, token, masks, told, att, source))
-        if step == 0:
-            source = made[0][NY]
-        parts.append(
-            [made[-1][0]] + [lax.ppermute(made[-1][k], "src", y_from(-k)) for k in range(1, NY)]
-        )
     coming = {offset: () for offset in (0, *NEXT)}
-    for step, offsets in enumerate(PLAN):
-        work = [(offset, len(coming[offset])) for offset in offsets if offset != 0]
-        if not work:
-            break
-        if PLAN[step + 1 : step + 2] == ((0,),):
-            parts[step][0], parts[step + 1][1] = lax.optimization_barrier(
-                (parts[step][0], parts[step + 1][1])
-            )
-        if step == 1:
-            parts[1][0], made[3][0] = lax.optimization_barrier((parts[1][0], made[3][0]))
+
+    def travel(made):
+        return [made[0]] + [lax.ppermute(made[k], "src", y_from(-k)) for k in range(1, NY)]
+
+    def sums(step):
+        work = [(offset, len(coming[offset])) for offset in PLAN[step] if offset != 0]
         dense = sum((coming[offset] for offset, _ in work), ())
-        sent = merge_group(work, scal, every_pair, parts[step], dense)
-        for (offset, _), chunk in zip(work, sent, strict=True):
+        return work, list(merge_group(work, scal, every_pair, parts[step], dense))
+
+    def send(work, chunks):
+        for (offset, _), chunk in zip(work, chunks, strict=True):
             hop = lax.ppermute(chunk, "src", z_from(NEXT[offset] - offset))
             coming[NEXT[offset]] += (hop,)
+
+    parts = [None] * len(PLAN)
+    first = slots(PLAN[0], scal, token, masks, told, att, pieces)
+    laid = first[NY]
+    parts[0] = travel(first[:NY])
+    parts[1] = travel(slots(PLAN[1], scal, token, masks, told, att, laid))
+    later, parts[0][1] = lax.optimization_barrier((token, parts[0][1]))
+    third = list(slots(PLAN[2], scal, later, masks, told, att, laid))
+    parts[0][0], third[0] = lax.optimization_barrier((parts[0][0], third[0]))
+    work, chunks = sums(0)
+    later, chunks[0] = lax.optimization_barrier((token, chunks[0]))
+    send(work, chunks)
+    last = list(slots(PLAN[3], scal, later, masks, told, att, laid))
+    parts[2] = travel(third)
+    parts[3] = travel(last)
+    parts[1][0], last[0] = lax.optimization_barrier((parts[1][0], last[0]))
+    for step in range(1, len(PLAN)):
+        send(*sums(step))
     home = merge_home(scal, every_pair, parts[-1], self_logit, hidden)
     return finish(coming[0], home, bias)
 

time: 100 us -> 101 us (1.010)
  starting transfers between devices: 45.4 us -> 48.3 us
  Pallas kernels: 25.6 us -> 23.6 us
    pallas_call x4, Pallas kernels: 6.06 us -> 4.16 us  [merge_group(): pl.pallas_call(functools.partial(merge_kernel, work), out_shape=(jax.Shap...]
    ppermute x19, starting transfers between devices: 28.2 us -> 29.8 us  [the longest x12 17.8 us: travel(): lax.ppermute(made[k], 'src', y_from(-k))]
    ppermute x3, starting transfers between devices: 4.44 us -> 5.66 us  [body(): lax.ppermute(hidden, 'dst', x_from(k))]
  transfers between devices with their start and end apart: 27 -> 27, of which waited for: 8 -> 7; matrix products, arithmetic and copies ran while one was open for 2% -> 2% of each run, Pallas kernels for 19% -> 17%
where the time goes in v5:
time: 101 us; the launch traced here: 99.1 us
  starting transfers between devices  48.3 us (48%)
  Pallas kernels  23.6 us (23%)
  waiting for transfers between devices  20.5 us (20%)
  local copies, waits for them, and re-layouts  3.56 us (4%)
  other arithmetic  1.56 us (2%)
  matrix products  1.36 us (1%)
    ppermute x12, starting transfers between devices, travel(): lax.ppermute(made[k], 'src', y_from(-k))  17.8 us
    pallas_call x4, Pallas kernels, slots(): pl.pallas_call(functools.partial(slots_kernel, offsets, first), out_shape...  15 us
    ppermute x7, starting transfers between devices, send(): hop = lax.ppermute(chunk, 'src', z_from(NEXT[offset] - offset))  12 us
    all_to_all x1, starting transfers between devices, body(): lax.all_to_all(jnp.broadcast_to(told[None], (OWNERS,) + told.shape), 'src...  11.7 us
    ppermute x7, waiting for transfers between devices, send(): hop = lax.ppermute(chunk, 'src', z_from(NEXT[offset] - offset))  8.97 us
    all_to_all x1, waiting for transfers between devices, body(): lax.all_to_all(jnp.broadcast_to(told[None], (OWNERS,) + told.shape), 'src...  6.64 us
    ppermute x3, starting transfers between devices, body(): lax.ppermute(hidden, 'dst', x_from(k))  5.66 us
    ppermute x12, waiting for transfers between devices, travel(): lax.ppermute(made[k], 'src', y_from(-k))  4.87 us
  transfers between devices with their start and end apart: 27, of which 7 were waited for; matrix products, arithmetic and copies ran while one was open for 2% of the time, Pallas kernels for 17%

profile of v5, /device:TPU:8, one launch (start us, length us, event | category | flops | bytes accessed | tf_op | source)
XLA Modules:
  0.0 99.1 jit_solution(14991178759738909986)
XLA Ops:
  3.5 1.5 %collective-permute-start.5 = (bf16[4,256,128]{2,1,0:T(8,128)(2,1)}, bf16[4,256,128]{2,1,0:T(8,128)(2,1)}, u32[]{:S(2)}, u32[]{:S(2)}) collective-permute-start(bf16[4,256,128]{2,1,0:T(8,128)(2,1)} %get-tuple-element.43.refs_0_.rest_0_.refs_5_), channel_id=1, source_target_pairs={{0,2},{1,3},{2,4},{3,5},{4,6},{5,7},{6,0},{7,1},{8,10},{9,11},{10,... | collective-permute-start | bytes 786440 | tf_op jit(solution)/shard_map/ppermute | solution.py:376
  5.0 2.7 %collective-permute-start.3 = (bf16[4,256,128]{2,1,0:T(8,128)(2,1)}, bf16[4,256,128]{2,1,0:T(8,128)(2,1)}, u32[]{:S(2)}, u32[]{:S(2)}) collective-permute-start(bf16[4,256,128]{2,1,0:T(8,128)(2,1)} %get-tuple-element.43.refs_0_.rest_0_.refs_5_), channel_id=1, source_target_pairs={{0,4},{1,5},{2,6},{3,7},{4,0},{5,1},{6,2},{7,3},{8,12},{9,13},{10,... | collective-permute-start | bytes 786440 | tf_op jit(solution)/shard_map/ppermute | solution.py:376
  7.7 1.4 %collective-permute-start.1 = (bf16[4,256,128]{2,1,0:T(8,128)(2,1)}, bf16[4,256,128]{2,1,0:T(8,128)(2,1)}, u32[]{:S(2)}, u32[]{:S(2)}) collective-permute-start(bf16[4,256,128]{2,1,0:T(8,128)(2,1)} %get-tuple-element.43.refs_0_.rest_0_.refs_5_), channel_id=1, source_target_pairs={{0,6},{1,7},{2,0},{3,1},{4,2},{5,3},{6,4},{7,5},{8,14},{9,15},{10,... | collective-permute-start | bytes 786440 | tf_op jit(solution)/shard_map/ppermute | solution.py:376
  10.6 11.7 %all-to-all-start = ((f32[32,5,4,128]{3,2,1,0:T(4,128)}), f32[32,5,4,128]{3,2,1,0:T(4,128)S(1)}, u32[]{:S(2)}, u32[]{:S(2)}) async-start(f32[32,5,4,128]{3,2,1,0:T(4,128)} %broadcast_in_dim.10), calls=%async_computation | async-start | bytes 655360 | tf_op jit(solution)/shard_map/all_to_all | solution.py:386
  23.7 2.2 %copy-done.1 = s32[1,1,32,2,128,128]{5,4,3,2,1,0:T(8,128)S(1)} copy-done((s32[1,1,32,2,128,128]{5,4,3,2,1,0:T(8,128)S(1)}, s32[1,1,32,2,128,128]{5,4,3,2,1,0:T(8,128)}, u32[]{:S(2)}) %copy-start.1) | copy-done | bytes 4194328
  27.1 6.6 %all-to-all-done.targets = f32[32,5,4,128]{3,2,1,0:T(4,128)S(1)} async-done(((f32[32,5,4,128]{3,2,1,0:T(4,128)}), f32[32,5,4,128]{3,2,1,0:T(4,128)S(1)}, u32[]{:S(2)}, u32[]{:S(2)}) %all-to-all-start) | async-done | bytes 327712 | tf_op jit(solution)/shard_map/all_to_all | solution.py:386
  33.8 3.5 %slots.4 = (bf16[1,2,272,128]{3,2,1,0:T(8,128)(2,1)S(1)}, bf16[1,2,272,128]{3,2,1,0:T(8,128)(2,1)S(1)}, bf16[1,2,272,128]{3,2,1,0:T(8,128)(2,1)S(1)}, bf16[1,2,2...) custom-call(s32[66]{0:T(128)S(1)} %pad_add_fusion.scal, f32[8,128]{1,0:T(8,128)S(1)} %gate.1.token, ...), custom_call_target="tpu_custom_call" | custom-call | flops 1000 | bytes 1000 | tf_op jit(solution)/shard_map/slots/pallas_call | solution.py:221
  38.3 2.5 %collective-permute-start.8 = (bf16[1,2,272,128]{3,2,1,0:T(8,128)(2,1)S(1)}, bf16[1,2,272,128]{3,2,1,0:T(8,128)(2,1)S(1)}, u32[]{:S(2)}, u32[]{:S(2)}) collective-permute-start(bf16[1,2,272,128]{3,2,1,0:T(8,128)(2,1)S(1)} %get-tuple-element.52), channel_id=1, source_target_pairs={{0,128},{8,136},{16,144},{24,152},{32,160},{40,168},{48,176},{56,1... | collective-permute-start | bytes 417800 | tf_op jit(solution)/shard_map/ppermute | solution.py:401
  41.3 3.3 %slots.7 = (bf16[2,2,272,128]{3,2,1,0:T(8,128)(2,1)S(1)}, bf16[2,2,272,128]{3,2,1,0:T(8,128)(2,1)S(1)}, bf16[2,2,272,128]{3,2,1,0:T(8,128)(2,1)S(1)}, bf16[2,2,272,128]{3,2,1,0:T(8,128)(2,1)S(1)}) custom-call(s32[66]{0:T(128)S(1)} %pad_add_fusion.scal, f32[8,128]{1,0:T(8,128)S(1)} %gate.1.token, f32[32,5,4,128]{3,2,1,0:T(4,128)S(1)} %all-to-all-done.targets, ...), custom_call_target="tpu_custom_call" | custom-call | flops 1000 | bytes 1000 | tf_op jit(solution)/shard_map/slots/pallas_call | solution.py:221
  44.6 1.6 %collective-permute-start.16 = (bf16[2,2,272,128]{3,2,1,0:T(8,128)(2,1)S(1)}, bf16[2,2,272,128]{3,2,1,0:T(8,128)(2,1)S(1)}, u32[]{:S(2)}, u32[]{:S(2)}) collective-permute-start(bf16[2,2,272,128]{3,2,1,0:T(8,128)(2,1)S(1)} %get-tuple-element.65), channel_id=1, source_target_pairs={{0,64},{8,72},{16,80},{24,88},{32,96},{40,104},{48,112},{56,120},{... | collective-permute-start | bytes 835592 | tf_op jit(solution)/shard_map/ppermute | solution.py:401
  46.2 2.2 %collective-permute-start.17 = (bf16[2,2,272,128]{3,2,1,0:T(8,128)(2,1)S(1)}, bf16[2,2,272,128]{3,2,1,0:T(8,128)(2,1)S(1)}, u32[]{:S(2)}, u32[]{:S(2)}) collective-permute-start(bf16[2,2,272,128]{3,2,1,0:T(8,128)(2,1)S(1)} %get-tuple-element.66), channel_id=1, source_target_pairs={{0,128},{8,136},{16,144},{24,152},{32,160},{40,168},{48,176},{56,1... | collective-permute-start | bytes 835592 | tf_op jit(solution)/shard_map/ppermute | solution.py:401
  48.7 3.3 %slots.5 = (bf16[2,2,272,128]{3,2,1,0:T(8,128)(2,1)S(1)}, bf16[2,2,272,128]{3,2,1,0:T(8,128)(2,1)S(1)}, bf16[2,2,272,128]{3,2,1,0:T(8,128)(2,1)S(1)}, bf16[2,2,272,128]{3,2,1,0:T(8,128)(2,1)S(1)}) custom-call(s32[66]{0:T(128)S(1)} %pad_add_fusion.scal, f32[8,128]{1,0:T(8,128)S(1)} %gate.1.token, f32[32,5,4,128]{3,2,1,0:T(4,128)S(1)} %all-to-all-done.targets, ...), custom_call_target="tpu_custom_call" | custom-call | flops 1000 | bytes 1000 | tf_op jit(solution)/shard_map/slots/pallas_call | solution.py:221
  52.9 2.0 %collective-permute-start.19 = (bf16[4,272,128]{2,1,0:T(8,128)(2,1)S(1)}, bf16[4,272,128]{2,1,0:T(8,128)(2,1)S(1)}, u32[]{:S(2)}, u32[]{:S(2)}) collective-permute-start(bf16[4,272,128]{2,1,0:T(8,128)(2,1)S(1)} %merge.4), channel_id=1, source_target_pairs={{0,8},{8,16},{16,24},{24,32},{32,40},{40,48},{48,56},{56,0},{64,72... | collective-permute-start | bytes 835592 | tf_op jit(solution)/shard_map/ppermute | solution.py:410
  54.8 1.9 %collective-permute-start.13 = (bf16[2,2,272,128]{3,2,1,0:T(8,128)(2,1)S(1)}, bf16[2,2,272,128]{3,2,1,0:T(8,128)(2,1)S(1)}, u32[]{:S(2)}, u32[]{:S(2)}) collective-permute-start(bf16[2,2,272,128]{3,2,1,0:T(8,128)(2,1)S(1)} %get-tuple-element.60), channel_id=1, source_target_pairs={{0,64},{8,72},{16,80},{24,88},{32,96},{40,104},{48,112},{56,120},{... | collective-permute-start | bytes 835592 | tf_op jit(solution)/shard_map/ppermute | solution.py:401
  56.7 2.7 %collective-permute-start.14 = (bf16[2,2,272,128]{3,2,1,0:T(8,128)(2,1)S(1)}, bf16[2,2,272,128]{3,2,1,0:T(8,128)(2,1)S(1)}, u32[]{:S(2)}, u32[]{:S(2)}) collective-permute-start(bf16[2,2,272,128]{3,2,1,0:T(8,128)(2,1)S(1)} %get-tuple-element.61), channel_id=1, source_target_pairs={{0,128},{8,136},{16,144},{24,152},{32,160},{40,168},{48,176},{56,1... | collective-permute-start | bytes 835592 | tf_op jit(solution)/shard_map/ppermute | solution.py:401
  60.3 4.9 %slots.6 = (bf16[3,2,272,128]{3,2,1,0:T(8,128)(2,1)S(1)}, bf16[3,2,272,128]{3,2,1,0:T(8,128)(2,1)S(1)}, bf16[3,2,272,128]{3,2,1,0:T(8,128)(2,1)S(1)}, bf16[3,2,272,128]{3,2,1,0:T(8,128)(2,1)S(1)}) custom-call(s32[66]{0:T(128)S(1)} %pad_add_fusion.scal, f32[8,128]{1,0:T(8,128)S(1)} %gate.1.token, f32[32,5,4,128]{3,2,1,0:T(4,128)S(1)} %all-to-all-done.targets, ...), custom_call_target="tpu_custom_call" | custom-call | flops 1000 | bytes 1000 | tf_op jit(solution)/shard_map/slots/pallas_call | solution.py:221
  66.3 3.4 %collective-permute-start.20 = (bf16[4,272,128]{2,1,0:T(8,128)(2,1)S(1)}, bf16[4,272,128]{2,1,0:T(8,128)(2,1)S(1)}, u32[]{:S(2)}, u32[]{:S(2)}) collective-permute-start(bf16[4,272,128]{2,1,0:T(8,128)(2,1)S(1)} %get-tuple-element.69), channel_id=1, source_target_pairs={{0,8},{8,16},{16,24},{24,32},{32,40},{40,48},{48,56},{56,0},{64,72... | collective-permute-start | bytes 835592 | tf_op jit(solution)/shard_map/ppermute | solution.py:410
  70.9 2.0 %collective-permute-start.11 = (bf16[3,2,272,128]{3,2,1,0:T(8,128)(2,1)S(1)}, bf16[3,2,272,128]{3,2,1,0:T(8,128)(2,1)S(1)}, u32[]{:S(2)}, u32[]{:S(2)}) collective-permute-start(bf16[3,2,272,128]{3,2,1,0:T(8,128)(2,1)S(1)} %get-tuple-element.57), channel_id=1, source_target_pairs={{0,128},{8,136},{16,144},{24,152},{32,160},{40,168},{48,176},{56,1... | collective-permute-start | bytes 1253384 | tf_op jit(solution)/shard_map/ppermute | solution.py:401
  74.1 1.9 %collective-permute-done.20.refs_4_ = bf16[4,272,128]{2,1,0:T(8,128)(2,1)S(1)} collective-permute-done((bf16[4,272,128]{2,1,0:T(8,128)(2,1)S(1)}, bf16[4,272,128]{2,1,0:T(8,128)(2,1)S(1)}, u32[]{:S(2)}, u32[]{:S(2)}) %collective-permute-start.20) | collective-permute-done | bytes 278560 | tf_op jit(solution)/shard_map/ppermute | solution.py:410
  76.0 2.8 %collective-permute-done.21.refs_5_ = bf16[4,272,128]{2,1,0:T(8,128)(2,1)S(1)} collective-permute-done((bf16[4,272,128]{2,1,0:T(8,128)(2,1)S(1)}, bf16[4,272,128]{2,1,0:T(8,128)(2,1)S(1)}, u32[]{:S(2)}, u32[]{:S(2)}) %collective-permute-start.21) | collective-permute-done | bytes 278560 | tf_op jit(solution)/shard_map/ppermute | solution.py:410
  80.8 2.5 %collective-permute-start.23 = (bf16[4,272,128]{2,1,0:T(8,128)(2,1)S(1)}, bf16[4,272,128]{2,1,0:T(8,128)(2,1)S(1)}, u32[]{:S(2)}, u32[]{:S(2)}) collective-permute-start(bf16[4,272,128]{2,1,0:T(8,128)(2,1)S(1)} %get-tuple-element.72), channel_id=1, source_target_pairs={{0,56},{8,0},{16,8},{24,16},{32,24},{40,32},{48,40},{56,48},{64,12... | collective-permute-start | bytes 835592 | tf_op jit(solution)/shard_map/ppermute | solution.py:410
  83.9 4.2 %collective-permute-done.12.refs_3_ = bf16[3,2,272,128]{3,2,1,0:T(8,128)(2,1)S(1)} collective-permute-done((bf16[3,2,272,128]{3,2,1,0:T(8,128)(2,1)S(1)}, bf16[3,2,272,128]{3,2,1,0:T(8,128)(2,1)S(1)}, u32[]{:S(2)}, u32[]{:S(2)}) %collective-permute-start.12) | collective-permute-done | bytes 417824 | tf_op jit(solution)/shard_map/ppermute | solution.py:401
  89.2 2.2 %collective-permute-start.24 = (bf16[4,272,128]{2,1,0:T(8,128)(2,1)S(1)}, bf16[4,272,128]{2,1,0:T(8,128)(2,1)S(1)}, u32[]{:S(2)}, u32[]{:S(2)}) collective-permute-start(bf16[4,272,128]{2,1,0:T(8,128)(2,1)S(1)} %get-tuple-element.73), channel_id=1, source_target_pairs={{0,8},{8,16},{16,24},{24,32},{32,40},{40,48},{48,56},{56,0},{64,72... | collective-permute-start | bytes 835592 | tf_op jit(solution)/shard_map/ppermute | solution.py:410
  93.7 3.8 %collective-permute-done.24.refs_0_ = bf16[4,272,128]{2,1,0:T(8,128)(2,1)S(1)} collective-permute-done((bf16[4,272,128]{2,1,0:T(8,128)(2,1)S(1)}, bf16[4,272,128]{2,1,0:T(8,128)(2,1)S(1)}, u32[]{:S(2)}, u32[]{:S(2)}) %collective-permute-start.24) | collective-permute-done | bytes 278560 | tf_op jit(solution)/shard_map/ppermute | solution.py:410
  (62 shorter events, 21.9 us)
Async XLA Ops:
  3.5 18.9 %collective-permute-start.5 = (bf16[4,256,128]{2,1,0:T(8,128)(2,1)}, bf16[4,256,128]{2,1,0:T(8,128)(2,1)}, u32[]{:S(2)}, u32[]{:S(2)}) collective-permute-start(bf16[4,256,128]{2,1,0:T(8,128)(2,1)} %get-tuple-element.43.refs_0_.rest_0_.refs_5_), channel_id=1, source_target_pairs={{0,2},{1,3},{2,4},{3,5},{4,6},{5,7},{6,0},{7,1},{8,10},{9,11},{10,... | collective-permute-start | bytes 786440 | tf_op jit(solution)/shard_map/ppermute | solution.py:376
  5.0 17.9 %collective-permute-start.3 = (bf16[4,256,128]{2,1,0:T(8,128)(2,1)}, bf16[4,256,128]{2,1,0:T(8,128)(2,1)}, u32[]{:S(2)}, u32[]{:S(2)}) collective-permute-start(bf16[4,256,128]{2,1,0:T(8,128)(2,1)} %get-tuple-element.43.refs_0_.rest_0_.refs_5_), channel_id=1, source_target_pairs={{0,4},{1,5},{2,6},{3,7},{4,0},{5,1},{6,2},{7,3},{8,12},{9,13},{10,... | collective-permute-start | bytes 786440 | tf_op jit(solution)/shard_map/ppermute | solution.py:376
  7.7 15.3 %collective-permute-start.1 = (bf16[4,256,128]{2,1,0:T(8,128)(2,1)}, bf16[4,256,128]{2,1,0:T(8,128)(2,1)}, u32[]{:S(2)}, u32[]{:S(2)}) collective-permute-start(bf16[4,256,128]{2,1,0:T(8,128)(2,1)} %get-tuple-element.43.refs_0_.rest_0_.refs_5_), channel_id=1, source_target_pairs={{0,6},{1,7},{2,0},{3,1},{4,2},{5,3},{6,4},{7,5},{8,14},{9,15},{10,... | collective-permute-start | bytes 786440 | tf_op jit(solution)/shard_map/ppermute | solution.py:376
  10.6 23.1 %all-to-all-start = ((f32[32,5,4,128]{3,2,1,0:T(4,128)}), f32[32,5,4,128]{3,2,1,0:T(4,128)S(1)}, u32[]{:S(2)}, u32[]{:S(2)}) async-start(f32[32,5,4,128]{3,2,1,0:T(4,128)} %broadcast_in_dim.10), calls=%async_computation | async-start | bytes 655360 | tf_op jit(solution)/shard_map/all_to_all | solution.py:386
  22.3 4.8 %collective-permute-start = (bf16[4,256,128]{2,1,0:T(8,128)(2,1)}, bf16[4,256,128]{2,1,0:T(8,128)(2,1)}, u32[]{:S(2)}, u32[]{:S(2)}) collective-permute-start(bf16[4,256,128]{2,1,0:T(8,128)(2,1)} %get-tuple-element.43.refs_0_.rest_0_.refs_5_), channel_id=1, source_target_pairs={{0,1},{1,0},{2,3},{3,2},{4,5},{5,4},{6,7},{7,6},{8,9},{9,8},{10,11... | collective-permute-start | bytes 786440 | tf_op jit(solution)/shard_map/ppermute | solution.py:394
  37.3 11.2 %collective-permute-start.7 = (bf16[1,2,272,128]{3,2,1,0:T(8,128)(2,1)S(1)}, bf16[1,2,272,128]{3,2,1,0:T(8,128)(2,1)S(1)}, u32[]{:S(2)}, u32[]{:S(2)}) collective-permute-start(bf16[1,2,272,128]{3,2,1,0:T(8,128)(2,1)S(1)} %get-tuple-element.46), channel_id=1, source_target_pairs={{0,64},{8,72},{16,80},{24,88},{32,96},{40,104},{48,112},{56,120},{... | collective-permute-start | bytes 417800 | tf_op jit(solution)/shard_map/ppermute | solution.py:401
  38.3 13.7 %collective-permute-start.8 = (bf16[1,2,272,128]{3,2,1,0:T(8,128)(2,1)S(1)}, bf16[1,2,272,128]{3,2,1,0:T(8,128)(2,1)S(1)}, u32[]{:S(2)}, u32[]{:S(2)}) collective-permute-start(bf16[1,2,272,128]{3,2,1,0:T(8,128)(2,1)S(1)} %get-tuple-element.52), channel_id=1, source_target_pairs={{0,128},{8,136},{16,144},{24,152},{32,160},{40,168},{48,176},{56,1... | collective-permute-start | bytes 417800 | tf_op jit(solution)/shard_map/ppermute | solution.py:401
  40.8 11.2 %collective-permute-start.9 = (bf16[1,2,272,128]{3,2,1,0:T(8,128)(2,1)S(1)}, bf16[1,2,272,128]{3,2,1,0:T(8,128)(2,1)S(1)}, u32[]{:S(2)}, u32[]{:S(2)}) collective-permute-start(bf16[1,2,272,128]{3,2,1,0:T(8,128)(2,1)S(1)} %get-tuple-element.53), channel_id=1, source_target_pairs={{0,192},{8,200},{16,208},{24,216},{32,224},{40,232},{48,240},{56,2... | collective-permute-start | bytes 417800 | tf_op jit(solution)/shard_map/ppermute | solution.py:401
  44.6 12.1 %collective-permute-start.16 = (bf16[2,2,272,128]{3,2,1,0:T(8,128)(2,1)S(1)}, bf16[2,2,272,128]{3,2,1,0:T(8,128)(2,1)S(1)}, u32[]{:S(2)}, u32[]{:S(2)}) collective-permute-start(bf16[2,2,272,128]{3,2,1,0:T(8,128)(2,1)S(1)} %get-tuple-element.65), channel_id=1, source_target_pairs={{0,64},{8,72},{16,80},{24,88},{32,96},{40,104},{48,112},{56,120},{... | collective-permute-start | bytes 835592 | tf_op jit(solution)/shard_map/ppermute | solution.py:401
  46.2 13.2 %collective-permute-start.17 = (bf16[2,2,272,128]{3,2,1,0:T(8,128)(2,1)S(1)}, bf16[2,2,272,128]{3,2,1,0:T(8,128)(2,1)S(1)}, u32[]{:S(2)}, u32[]{:S(2)}) collective-permute-start(bf16[2,2,272,128]{3,2,1,0:T(8,128)(2,1)S(1)} %get-tuple-element.66), channel_id=1, source_target_pairs={{0,128},{8,136},{16,144},{24,152},{32,160},{40,168},{48,176},{56,1... | collective-permute-start | bytes 835592 | tf_op jit(solution)/shard_map/ppermute | solution.py:401
  48.4 16.8 %collective-permute-start.18 = (bf16[2,2,272,128]{3,2,1,0:T(8,128)(2,1)S(1)}, bf16[2,2,272,128]{3,2,1,0:T(8,128)(2,1)S(1)}, u32[]{:S(2)}, u32[]{:S(2)}) collective-permute-start(bf16[2,2,272,128]{3,2,1,0:T(8,128)(2,1)S(1)} %get-tuple-element.67), channel_id=1, source_target_pairs={{0,192},{8,200},{16,208},{24,216},{32,224},{40,232},{48,240},{56,2... | collective-permute-start | bytes 835592 | tf_op jit(solution)/shard_map/ppermute | solution.py:401
  52.9 12.4 %collective-permute-start.19 = (bf16[4,272,128]{2,1,0:T(8,128)(2,1)S(1)}, bf16[4,272,128]{2,1,0:T(8,128)(2,1)S(1)}, u32[]{:S(2)}, u32[]{:S(2)}) collective-permute-start(bf16[4,272,128]{2,1,0:T(8,128)(2,1)S(1)} %merge.4), channel_id=1, source_target_pairs={{0,8},{8,16},{16,24},{24,32},{32,40},{40,48},{48,56},{56,0},{64,72... | collective-permute-start | bytes 835592 | tf_op jit(solution)/shard_map/ppermute | solution.py:410
  54.8 14.9 %collective-permute-start.13 = (bf16[2,2,272,128]{3,2,1,0:T(8,128)(2,1)S(1)}, bf16[2,2,272,128]{3,2,1,0:T(8,128)(2,1)S(1)}, u32[]{:S(2)}, u32[]{:S(2)}) collective-permute-start(bf16[2,2,272,128]{3,2,1,0:T(8,128)(2,1)S(1)} %get-tuple-element.60), channel_id=1, source_target_pairs={{0,64},{8,72},{16,80},{24,88},{32,96},{40,104},{48,112},{56,120},{... | collective-permute-start | bytes 835592 | tf_op jit(solution)/shard_map/ppermute | solution.py:401
  56.7 14.1 %collective-permute-start.14 = (bf16[2,2,272,128]{3,2,1,0:T(8,128)(2,1)S(1)}, bf16[2,2,272,128]{3,2,1,0:T(8,128)(2,1)S(1)}, u32[]{:S(2)}, u32[]{:S(2)}) collective-permute-start(bf16[2,2,272,128]{3,2,1,0:T(8,128)(2,1)S(1)} %get-tuple-element.61), channel_id=1, source_target_pairs={{0,128},{8,136},{16,144},{24,152},{32,160},{40,168},{48,176},{56,1... | collective-permute-start | bytes 835592 | tf_op jit(solution)/shard_map/ppermute | solution.py:401
  59.4 13.5 %collective-permute-start.15 = (bf16[2,2,272,128]{3,2,1,0:T(8,128)(2,1)S(1)}, bf16[2,2,272,128]{3,2,1,0:T(8,128)(2,1)S(1)}, u32[]{:S(2)}, u32[]{:S(2)}) collective-permute-start(bf16[2,2,272,128]{3,2,1,0:T(8,128)(2,1)S(1)} %get-tuple-element.62), channel_id=1, source_target_pairs={{0,192},{8,200},{16,208},{24,216},{32,224},{40,232},{48,240},{56,2... | collective-permute-start | bytes 835592 | tf_op jit(solution)/shard_map/ppermute | solution.py:401
  66.3 9.7 %collective-permute-start.20 = (bf16[4,272,128]{2,1,0:T(8,128)(2,1)S(1)}, bf16[4,272,128]{2,1,0:T(8,128)(2,1)S(1)}, u32[]{:S(2)}, u32[]{:S(2)}) collective-permute-start(bf16[4,272,128]{2,1,0:T(8,128)(2,1)S(1)} %get-tuple-element.69), channel_id=1, source_target_pairs={{0,8},{8,16},{16,24},{24,32},{32,40},{40,48},{48,56},{56,0},{64,72... | collective-permute-start | bytes 835592 | tf_op jit(solution)/shard_map/ppermute | solution.py:410
  69.7 9.1 %collective-permute-start.21 = (bf16[4,272,128]{2,1,0:T(8,128)(2,1)S(1)}, bf16[4,272,128]{2,1,0:T(8,128)(2,1)S(1)}, u32[]{:S(2)}, u32[]{:S(2)}) collective-permute-start(bf16[4,272,128]{2,1,0:T(8,128)(2,1)S(1)} %get-tuple-element.70), channel_id=1, source_target_pairs={{0,56},{8,0},{16,8},{24,16},{32,24},{40,32},{48,40},{56,48},{64,12... | collective-permute-start | bytes 835592 | tf_op jit(solution)/shard_map/ppermute | solution.py:410
  69.8 13.5 %collective-permute-start.10 = (bf16[3,2,272,128]{3,2,1,0:T(8,128)(2,1)S(1)}, bf16[3,2,272,128]{3,2,1,0:T(8,128)(2,1)S(1)}, u32[]{:S(2)}, u32[]{:S(2)}) collective-permute-start(bf16[3,2,272,128]{3,2,1,0:T(8,128)(2,1)S(1)} %get-tuple-element.56), channel_id=1, source_target_pairs={{0,64},{8,72},{16,80},{24,88},{32,96},{40,104},{48,112},{56,120},{... | collective-permute-start | bytes 1253384 | tf_op jit(solution)/shard_map/ppermute | solution.py:401
  70.9 13.0 %collective-permute-start.11 = (bf16[3,2,272,128]{3,2,1,0:T(8,128)(2,1)S(1)}, bf16[3,2,272,128]{3,2,1,0:T(8,128)(2,1)S(1)}, u32[]{:S(2)}, u32[]{:S(2)}) collective-permute-start(bf16[3,2,272,128]{3,2,1,0:T(8,128)(2,1)S(1)} %get-tuple-element.57), channel_id=1, source_target_pairs={{0,128},{8,136},{16,144},{24,152},{32,160},{40,168},{48,176},{56,1... | collective-permute-start | bytes 1253384 | tf_op jit(solution)/shard_map/ppermute | solution.py:401
  72.9 15.2 %collective-permute-start.12 = (bf16[3,2,272,128]{3,2,1,0:T(8,128)(2,1)S(1)}, bf16[3,2,272,128]{3,2,1,0:T(8,128)(2,1)S(1)}, u32[]{:S(2)}, u32[]{:S(2)}) collective-permute-start(bf16[3,2,272,128]{3,2,1,0:T(8,128)(2,1)S(1)} %get-tuple-element.58), channel_id=1, source_target_pairs={{0,192},{8,200},{16,208},{24,216},{32,224},{40,232},{48,240},{56,2... | collective-permute-start | bytes 1253384 | tf_op jit(solution)/shard_map/ppermute | solution.py:401
  79.9 8.2 %collective-permute-start.22 = (bf16[4,272,128]{2,1,0:T(8,128)(2,1)S(1)}, bf16[4,272,128]{2,1,0:T(8,128)(2,1)S(1)}, u32[]{:S(2)}, u32[]{:S(2)}) collective-permute-start(bf16[4,272,128]{2,1,0:T(8,128)(2,1)S(1)} %get-tuple-element.71), channel_id=1, source_target_pairs={{0,8},{8,16},{16,24},{24,32},{32,40},{40,48},{48,56},{56,0},{64,72... | collective-permute-start | bytes 835592 | tf_op jit(solution)/shard_map/ppermute | solution.py:410
  80.8 7.3 %collective-permute-start.23 = (bf16[4,272,128]{2,1,0:T(8,128)(2,1)S(1)}, bf16[4,272,128]{2,1,0:T(8,128)(2,1)S(1)}, u32[]{:S(2)}, u32[]{:S(2)}) collective-permute-start(bf16[4,272,128]{2,1,0:T(8,128)(2,1)S(1)} %get-tuple-element.72), channel_id=1, source_target_pairs={{0,56},{8,0},{16,8},{24,16},{32,24},{40,32},{48,40},{56,48},{64,12... | collective-permute-start | bytes 835592 | tf_op jit(solution)/shard_map/ppermute | solution.py:410
  89.2 8.3 %collective-permute-start.24 = (bf16[4,272,128]{2,1,0:T(8,128)(2,1)S(1)}, bf16[4,272,128]{2,1,0:T(8,128)(2,1)S(1)}, u32[]{:S(2)}, u32[]{:S(2)}) collective-permute-start(bf16[4,272,128]{2,1,0:T(8,128)(2,1)S(1)} %get-tuple-element.73), channel_id=1, source_target_pairs={{0,8},{8,16},{16,24},{24,32},{32,40},{40,48},{48,56},{56,0},{64,72... | collective-permute-start | bytes 835592 | tf_op jit(solution)/shard_map/ppermute | solution.py:410
  91.4 6.5 %collective-permute-start.25 = (bf16[4,272,128]{2,1,0:T(8,128)(2,1)S(1)}, bf16[4,272,128]{2,1,0:T(8,128)(2,1)S(1)}, u32[]{:S(2)}, u32[]{:S(2)}) collective-permute-start(bf16[4,272,128]{2,1,0:T(8,128)(2,1)S(1)} %get-tuple-element.74), channel_id=1, source_target_pairs={{0,56},{8,0},{16,8},{24,16},{32,24},{40,32},{48,40},{56,48},{64,12... | collective-permute-start | bytes 835592 | tf_op jit(solution)/shard_map/ppermute | solution.py:410
  (7 other events, 57.7 us)

commit v6 on v4

--- a/solution.py
+++ b/solution.py
@@ -214,7 +214,7 @@
     first = isinstance(source, list)
     shape = (len(offsets), SLOTS, ROWS, BLK)
     out_shape = (jax.ShapeDtypeStruct(shape, BF16),) * NY
-    scratch = [pltpu.VMEM((max(1, 4 // len(offsets)),) + shape, BF16)]
+    scratch = [pltpu.VMEM((min(NY, 8 // len(offsets)),) + shape, BF16)]
     if first:
         out_shape += (jax.ShapeDtypeStruct((SRC_BLOCKS, FEAT, BLK), BF16),)
         scratch.append(pltpu.SemaphoreType.DMA((PIECES,)))

time: 100 us -> 101 us (1.010); the launches traced: 99 us -> 98.9 us
  Pallas kernels: 25.6 us -> 24.5 us
    pallas_call x4, Pallas kernels: 15 us -> 13.9 us  [slots(): pl.pallas_call(functools.partial(slots_kernel, offsets, first), out_shape...]
  transfers between devices with their start and end apart: 27 -> 27, of which waited for: 8 -> 8; matrix products, arithmetic and copies ran while one was open for 2% -> 2% of each run, Pallas kernels for 19% -> 18%
where the time goes in v6:
time: 101 us; the launch traced here: 98.9 us
  starting transfers between devices  45.9 us (45%)
  Pallas kernels  24.5 us (24%)
  waiting for transfers between devices  21.2 us (21%)
  local copies, waits for them, and re-layouts  4.29 us (4%)
  other arithmetic  1.49 us (1%)
  matrix products  1.36 us (1%)
    ppermute x12, starting transfers between devices, body(): lax.ppermute(made[-1][k], 'src', y_from(-k))  17.9 us
    pallas_call x4, Pallas kernels, slots(): pl.pallas_call(functools.partial(slots_kernel, offsets, first), out_shape...  13.9 us
    all_to_all x1, starting transfers between devices, body(): lax.all_to_all(jnp.broadcast_to(told[None], (OWNERS,) + told.shape), 'src...  11.7 us
    ppermute x7, starting transfers between devices, body(): hop = lax.ppermute(chunk, 'src', z_from(NEXT[offset] - offset))  10.8 us
    ppermute x7, waiting for transfers between devices, body(): hop = lax.ppermute(chunk, 'src', z_from(NEXT[offset] - offset))  7.76 us
    ppermute x12, waiting for transfers between devices, body(): lax.ppermute(made[-1][k], 'src', y_from(-k))  6.82 us
    all_to_all x1, waiting for transfers between devices, body(): lax.all_to_all(jnp.broadcast_to(told[None], (OWNERS,) + told.shape), 'src...  6.64 us
    pallas_call x4, Pallas kernels, merge_group(): pl.pallas_call(functools.partial(merge_kernel, work), out_shape=(jax.Shap...  6.05 us
  transfers between devices with their start and end apart: 27, of which 8 were waited for; matrix products, arithmetic and copies ran while one was open for 2% of the time, Pallas kernels for 18%

profile of v6, /device:TPU:8, one launch (start us, length us, event | category | flops | bytes accessed | tf_op | source)
XLA Modules:
  0.0 98.9 jit_solution(12564348835263270771)
XLA Ops:
  4.2 2.8 %collective-permute-start.1 = (bf16[4,256,128]{2,1,0:T(8,128)(2,1)}, bf16[4,256,128]{2,1,0:T(8,128)(2,1)}, u32[]{:S(2)}, u32[]{:S(2)}) collective-permute-start(bf16[4,256,128]{2,1,0:T(8,128)(2,1)} %get-tuple-element.37.refs_0_.rest_0_.refs_5_), channel_id=1, source_target_pairs={{0,6},{1,7},{2,0},{3,1},{4,2},{5,3},{6,4},{7,5},{8,14},{9,15},{10,... | collective-permute-start | bytes 786440 | tf_op jit(solution)/shard_map/ppermute | solution.py:376
  10.1 11.7 %all-to-all-start = ((f32[32,5,4,128]{3,2,1,0:T(4,128)}), f32[32,5,4,128]{3,2,1,0:T(4,128)S(1)}, u32[]{:S(2)}, u32[]{:S(2)}) async-start(f32[32,5,4,128]{3,2,1,0:T(4,128)} %broadcast_in_dim.10), calls=%async_computation | async-start | bytes 655360 | tf_op jit(solution)/shard_map/all_to_all | solution.py:386
  23.1 2.2 %copy-done.1 = s32[1,1,32,2,128,128]{5,4,3,2,1,0:T(8,128)S(1)} copy-done((s32[1,1,32,2,128,128]{5,4,3,2,1,0:T(8,128)S(1)}, s32[1,1,32,2,128,128]{5,4,3,2,1,0:T(8,128)}, u32[]{:S(2)}) %copy-start.1) | copy-done | bytes 4194328
  26.6 6.6 %all-to-all-done.targets = f32[32,5,4,128]{3,2,1,0:T(4,128)S(1)} async-done(((f32[32,5,4,128]{3,2,1,0:T(4,128)}), f32[32,5,4,128]{3,2,1,0:T(4,128)S(1)}, u32[]{:S(2)}, u32[]{:S(2)}) %all-to-all-start) | async-done | bytes 327712 | tf_op jit(solution)/shard_map/all_to_all | solution.py:386
  33.2 3.5 %slots.4 = (bf16[1,2,272,128]{3,2,1,0:T(8,128)(2,1)S(1)}, bf16[1,2,272,128]{3,2,1,0:T(8,128)(2,1)S(1)}, bf16[1,2,272,128]{3,2,1,0:T(8,128)(2,1)S(1)}, bf16[1,2,2...) custom-call(s32[66]{0:T(128)S(1)} %pad_add_fusion.scal, f32[8,128]{1,0:T(8,128)S(1)} %gate.1.token, ...), custom_call_target="tpu_custom_call" | custom-call | flops 1000 | bytes 1000 | tf_op jit(solution)/shard_map/slots/pallas_call | solution.py:221
  37.7 2.5 %collective-permute-start.17 = (bf16[1,2,272,128]{3,2,1,0:T(8,128)(2,1)S(1)}, bf16[1,2,272,128]{3,2,1,0:T(8,128)(2,1)S(1)}, u32[]{:S(2)}, u32[]{:S(2)}) collective-permute-start(bf16[1,2,272,128]{3,2,1,0:T(8,128)(2,1)S(1)} %get-tuple-element.55), channel_id=1, source_target_pairs={{0,128},{8,136},{16,144},{24,152},{32,160},{40,168},{48,176},{56,1... | collective-permute-start | bytes 417800 | tf_op jit(solution)/shard_map/ppermute | solution.py:402
  40.8 3.0 %slots.7 = (bf16[2,2,272,128]{3,2,1,0:T(8,128)(2,1)S(1)}, bf16[2,2,272,128]{3,2,1,0:T(8,128)(2,1)S(1)}, bf16[2,2,272,128]{3,2,1,0:T(8,128)(2,1)S(1)}, bf16[2,2,272,128]{3,2,1,0:T(8,128)(2,1)S(1)}) custom-call(s32[66]{0:T(128)S(1)} %pad_add_fusion.scal, f32[8,128]{1,0:T(8,128)S(1)} %gate.1.token, f32[32,5,4,128]{3,2,1,0:T(4,128)S(1)} %all-to-all-done.targets, ...), custom_call_target="tpu_custom_call" | custom-call | flops 1000 | bytes 1000 | tf_op jit(solution)/shard_map/slots/pallas_call | solution.py:221
  43.8 1.8 %collective-permute-start.13 = (bf16[2,2,272,128]{3,2,1,0:T(8,128)(2,1)S(1)}, bf16[2,2,272,128]{3,2,1,0:T(8,128)(2,1)S(1)}, u32[]{:S(2)}, u32[]{:S(2)}) collective-permute-start(bf16[2,2,272,128]{3,2,1,0:T(8,128)(2,1)S(1)} %get-tuple-element.50), channel_id=1, source_target_pairs={{0,64},{8,72},{16,80},{24,88},{32,96},{40,104},{48,112},{56,120},{... | collective-permute-start | bytes 835592 | tf_op jit(solution)/shard_map/ppermute | solution.py:402
  45.6 2.2 %collective-permute-start.14 = (bf16[2,2,272,128]{3,2,1,0:T(8,128)(2,1)S(1)}, bf16[2,2,272,128]{3,2,1,0:T(8,128)(2,1)S(1)}, u32[]{:S(2)}, u32[]{:S(2)}) collective-permute-start(bf16[2,2,272,128]{3,2,1,0:T(8,128)(2,1)S(1)} %get-tuple-element.51), channel_id=1, source_target_pairs={{0,128},{8,136},{16,144},{24,152},{32,160},{40,168},{48,176},{56,1... | collective-permute-start | bytes 835592 | tf_op jit(solution)/shard_map/ppermute | solution.py:402
  51.2 3.0 %slots.6 = (bf16[2,2,272,128]{3,2,1,0:T(8,128)(2,1)S(1)}, bf16[2,2,272,128]{3,2,1,0:T(8,128)(2,1)S(1)}, bf16[2,2,272,128]{3,2,1,0:T(8,128)(2,1)S(1)}, bf16[2,2,272,128]{3,2,1,0:T(8,128)(2,1)S(1)}) custom-call(s32[66]{0:T(128)S(1)} %pad_add_fusion.scal, f32[8,128]{1,0:T(8,128)S(1)} %gate.1.token, f32[32,5,4,128]{3,2,1,0:T(4,128)S(1)} %all-to-all-done.targets, ...), custom_call_target="tpu_custom_call" | custom-call | flops 1000 | bytes 1000 | tf_op jit(solution)/shard_map/slots/pallas_call | solution.py:221
  54.2 2.0 %collective-permute-start.10 = (bf16[2,2,272,128]{3,2,1,0:T(8,128)(2,1)S(1)}, bf16[2,2,272,128]{3,2,1,0:T(8,128)(2,1)S(1)}, u32[]{:S(2)}, u32[]{:S(2)}) collective-permute-start(bf16[2,2,272,128]{3,2,1,0:T(8,128)(2,1)S(1)} %get-tuple-element.45), channel_id=1, source_target_pairs={{0,64},{8,72},{16,80},{24,88},{32,96},{40,104},{48,112},{56,120},{... | collective-permute-start | bytes 835592 | tf_op jit(solution)/shard_map/ppermute | solution.py:402
  56.2 2.7 %collective-permute-start.11 = (bf16[2,2,272,128]{3,2,1,0:T(8,128)(2,1)S(1)}, bf16[2,2,272,128]{3,2,1,0:T(8,128)(2,1)S(1)}, u32[]{:S(2)}, u32[]{:S(2)}) collective-permute-start(bf16[2,2,272,128]{3,2,1,0:T(8,128)(2,1)S(1)} %get-tuple-element.46), channel_id=1, source_target_pairs={{0,128},{8,136},{16,144},{24,152},{32,160},{40,168},{48,176},{56,1... | collective-permute-start | bytes 835592 | tf_op jit(solution)/shard_map/ppermute | solution.py:402
  59.7 4.4 %slots.5 = (bf16[3,2,272,128]{3,2,1,0:T(8,128)(2,1)S(1)}, bf16[3,2,272,128]{3,2,1,0:T(8,128)(2,1)S(1)}, bf16[3,2,272,128]{3,2,1,0:T(8,128)(2,1)S(1)}, bf16[3,2,272,128]{3,2,1,0:T(8,128)(2,1)S(1)}) custom-call(s32[66]{0:T(128)S(1)} %pad_add_fusion.scal, f32[8,128]{1,0:T(8,128)S(1)} %gate.1.token, f32[32,5,4,128]{3,2,1,0:T(4,128)S(1)} %all-to-all-done.targets, ...), custom_call_target="tpu_custom_call" | custom-call | flops 1000 | bytes 1000 | tf_op jit(solution)/shard_map/slots/pallas_call | solution.py:221
  64.1 1.6 %merge.5 = (bf16[4,272,128]{2,1,0:T(8,128)(2,1)S(1)}, bf16[4,272,128]{2,1,0:T(8,128)(2,1)S(1)}) custom-call(s32[66]{0:T(128)S(1)} %pad_add_fusion.scal, s32[64,32]{1,0:T(8,128)S(1)} %bitcast.19, bf16[2,2,272,128]{3,2,1,0:T(8,128)(2,1)S(1)} %get-tuple-element.49.refs_0_, bf16[2,2,272,128]{3,2,1,0:T(8,128)(2,1)S(1)} %collective-permute-done.13.refs_1_, ...), custom_call_target="tpu_custom_call" | custom-call | flops 1000 | bytes 1000 | tf_op jit(solution)/shard_map/merge/pallas_call | solution.py:311
  65.6 3.5 %collective-permute-start.20 = (bf16[4,272,128]{2,1,0:T(8,128)(2,1)S(1)}, bf16[4,272,128]{2,1,0:T(8,128)(2,1)S(1)}, u32[]{:S(2)}, u32[]{:S(2)}) collective-permute-start(bf16[4,272,128]{2,1,0:T(8,128)(2,1)S(1)} %get-tuple-element.57), channel_id=1, source_target_pairs={{0,8},{8,16},{16,24},{24,32},{32,40},{40,48},{48,56},{56,0},{64,72... | collective-permute-start | bytes 835592 | tf_op jit(solution)/shard_map/ppermute | solution.py:418
  70.2 2.5 %collective-permute-start.8 = (bf16[3,2,272,128]{3,2,1,0:T(8,128)(2,1)S(1)}, bf16[3,2,272,128]{3,2,1,0:T(8,128)(2,1)S(1)}, u32[]{:S(2)}, u32[]{:S(2)}) collective-permute-start(bf16[3,2,272,128]{3,2,1,0:T(8,128)(2,1)S(1)} %get-tuple-element.42), channel_id=1, source_target_pairs={{0,128},{8,136},{16,144},{24,152},{32,160},{40,168},{48,176},{56,1... | collective-permute-start | bytes 1253384 | tf_op jit(solution)/shard_map/ppermute | solution.py:402
  74.4 2.8 %collective-permute-done.21.refs_5_ = bf16[4,272,128]{2,1,0:T(8,128)(2,1)S(1)} collective-permute-done((bf16[4,272,128]{2,1,0:T(8,128)(2,1)S(1)}, bf16[4,272,128]{2,1,0:T(8,128)(2,1)S(1)}, u32[]{:S(2)}, u32[]{:S(2)}) %collective-permute-start.21) | collective-permute-done | bytes 278560 | tf_op jit(solution)/shard_map/ppermute | solution.py:418
  77.2 1.6 %merge.6 = (bf16[4,272,128]{2,1,0:T(8,128)(2,1)S(1)}, bf16[4,272,128]{2,1,0:T(8,128)(2,1)S(1)}) custom-call(s32[66]{0:T(128)S(1)} %pad_add_fusion.scal, s32[64,32]{1,0:T(8,128)S(1)} %bitcast.20, bf16[2,2,272,128]{3,2,1,0:T(8,128)(2,1)S(1)} %get-tuple-element.44.refs_0_, bf16[2,2,272,128]{3,2,1,0:T(8,128)(2,1)S(1)} %collective-permute-done.10.refs_1_, ...), custom_call_target="tpu_custom_call" | custom-call | flops 1000 | bytes 1000 | tf_op jit(solution)/shard_map/merge/pallas_call | solution.py:311
  78.8 1.6 %collective-permute-start.22 = (bf16[4,272,128]{2,1,0:T(8,128)(2,1)S(1)}, bf16[4,272,128]{2,1,0:T(8,128)(2,1)S(1)}, u32[]{:S(2)}, u32[]{:S(2)}) collective-permute-start(bf16[4,272,128]{2,1,0:T(8,128)(2,1)S(1)} %get-tuple-element.59), channel_id=1, source_target_pairs={{0,8},{8,16},{16,24},{24,32},{32,40},{40,48},{48,56},{56,0},{64,72... | collective-permute-start | bytes 835592 | tf_op jit(solution)/shard_map/ppermute | solution.py:418
  80.4 1.7 %collective-permute-start.23 = (bf16[4,272,128]{2,1,0:T(8,128)(2,1)S(1)}, bf16[4,272,128]{2,1,0:T(8,128)(2,1)S(1)}, u32[]{:S(2)}, u32[]{:S(2)}) collective-permute-start(bf16[4,272,128]{2,1,0:T(8,128)(2,1)S(1)} %get-tuple-element.60), channel_id=1, source_target_pairs={{0,56},{8,0},{16,8},{24,16},{32,24},{40,32},{48,40},{56,48},{64,12... | collective-permute-start | bytes 835592 | tf_op jit(solution)/shard_map/ppermute | solution.py:418
  83.3 4.2 %collective-permute-done.9.refs_3_ = bf16[3,2,272,128]{3,2,1,0:T(8,128)(2,1)S(1)} collective-permute-done((bf16[3,2,272,128]{3,2,1,0:T(8,128)(2,1)S(1)}, bf16[3,2,272,128]{3,2,1,0:T(8,128)(2,1)S(1)}, u32[]{:S(2)}, u32[]{:S(2)}) %collective-permute-start.9) | collective-permute-done | bytes 417824 | tf_op jit(solution)/shard_map/ppermute | solution.py:402
  87.6 1.6 %merge.7 = (bf16[4,272,128]{2,1,0:T(8,128)(2,1)S(1)}, bf16[4,272,128]{2,1,0:T(8,128)(2,1)S(1)}) custom-call(s32[66]{0:T(128)S(1)} %pad_add_fusion.scal, s32[64,32]{1,0:T(8,128)S(1)} %bitcast.21, bf16[3,2,272,128]{3,2,1,0:T(8,128)(2,1)S(1)} %get-tuple-element.40.refs_0_, bf16[3,2,272,128]{3,2,1,0:T(8,128)(2,1)S(1)} %collective-permute-done.7.refs_1_, ...), custom_call_target="tpu_custom_call" | custom-call | flops 1000 | bytes 1000 | tf_op jit(solution)/shard_map/merge/pallas_call | solution.py:311
  89.2 2.1 %collective-permute-start.24 = (bf16[4,272,128]{2,1,0:T(8,128)(2,1)S(1)}, bf16[4,272,128]{2,1,0:T(8,128)(2,1)S(1)}, u32[]{:S(2)}, u32[]{:S(2)}) collective-permute-start(bf16[4,272,128]{2,1,0:T(8,128)(2,1)S(1)} %get-tuple-element.61), channel_id=1, source_target_pairs={{0,8},{8,16},{16,24},{24,32},{32,40},{40,48},{48,56},{56,0},{64,72... | collective-permute-start | bytes 835592 | tf_op jit(solution)/shard_map/ppermute | solution.py:418
  93.8 3.6 %collective-permute-done.24.refs_0_ = bf16[4,272,128]{2,1,0:T(8,128)(2,1)S(1)} collective-permute-done((bf16[4,272,128]{2,1,0:T(8,128)(2,1)S(1)}, bf16[4,272,128]{2,1,0:T(8,128)(2,1)S(1)}, u32[]{:S(2)}, u32[]{:S(2)}) %collective-permute-start.24) | collective-permute-done | bytes 278560 | tf_op jit(solution)/shard_map/ppermute | solution.py:418
  (61 shorter events, 23.7 us)
Async XLA Ops:
  4.2 17.7 %collective-permute-start.1 = (bf16[4,256,128]{2,1,0:T(8,128)(2,1)}, bf16[4,256,128]{2,1,0:T(8,128)(2,1)}, u32[]{:S(2)}, u32[]{:S(2)}) collective-permute-start(bf16[4,256,128]{2,1,0:T(8,128)(2,1)} %get-tuple-element.37.refs_0_.rest_0_.refs_5_), channel_id=1, source_target_pairs={{0,6},{1,7},{2,0},{3,1},{4,2},{5,3},{6,4},{7,5},{8,14},{9,15},{10,... | collective-permute-start | bytes 786440 | tf_op jit(solution)/shard_map/ppermute | solution.py:376
  6.9 15.5 %collective-permute-start.3 = (bf16[4,256,128]{2,1,0:T(8,128)(2,1)}, bf16[4,256,128]{2,1,0:T(8,128)(2,1)}, u32[]{:S(2)}, u32[]{:S(2)}) collective-permute-start(bf16[4,256,128]{2,1,0:T(8,128)(2,1)} %get-tuple-element.37.refs_0_.rest_0_.refs_5_), channel_id=1, source_target_pairs={{0,4},{1,5},{2,6},{3,7},{4,0},{5,1},{6,2},{7,3},{8,12},{9,13},{10,... | collective-permute-start | bytes 786440 | tf_op jit(solution)/shard_map/ppermute | solution.py:376
  7.7 14.8 %collective-permute-start.5 = (bf16[4,256,128]{2,1,0:T(8,128)(2,1)}, bf16[4,256,128]{2,1,0:T(8,128)(2,1)}, u32[]{:S(2)}, u32[]{:S(2)}) collective-permute-start(bf16[4,256,128]{2,1,0:T(8,128)(2,1)} %get-tuple-element.37.refs_0_.rest_0_.refs_5_), channel_id=1, source_target_pairs={{0,2},{1,3},{2,4},{3,5},{4,6},{5,7},{6,0},{7,1},{8,10},{9,11},{10,... | collective-permute-start | bytes 786440 | tf_op jit(solution)/shard_map/ppermute | solution.py:376
  10.1 23.1 %all-to-all-start = ((f32[32,5,4,128]{3,2,1,0:T(4,128)}), f32[32,5,4,128]{3,2,1,0:T(4,128)S(1)}, u32[]{:S(2)}, u32[]{:S(2)}) async-start(f32[32,5,4,128]{3,2,1,0:T(4,128)} %broadcast_in_dim.10), calls=%async_computation | async-start | bytes 655360 | tf_op jit(solution)/shard_map/all_to_all | solution.py:386
  21.8 4.8 %collective-permute-start = (bf16[4,256,128]{2,1,0:T(8,128)(2,1)}, bf16[4,256,128]{2,1,0:T(8,128)(2,1)}, u32[]{:S(2)}, u32[]{:S(2)}) collective-permute-start(bf16[4,256,128]{2,1,0:T(8,128)(2,1)} %get-tuple-element.37.refs_0_.rest_0_.refs_5_), channel_id=1, source_target_pairs={{0,1},{1,0},{2,3},{3,2},{4,5},{5,4},{6,7},{7,6},{8,9},{9,8},{10,11... | collective-permute-start | bytes 786440 | tf_op jit(solution)/shard_map/ppermute | solution.py:391
  36.7 11.1 %collective-permute-start.16 = (bf16[1,2,272,128]{3,2,1,0:T(8,128)(2,1)S(1)}, bf16[1,2,272,128]{3,2,1,0:T(8,128)(2,1)S(1)}, u32[]{:S(2)}, u32[]{:S(2)}) collective-permute-start(bf16[1,2,272,128]{3,2,1,0:T(8,128)(2,1)S(1)} %get-tuple-element.54), channel_id=1, source_target_pairs={{0,64},{8,72},{16,80},{24,88},{32,96},{40,104},{48,112},{56,120},{... | collective-permute-start | bytes 417800 | tf_op jit(solution)/shard_map/ppermute | solution.py:402
  37.7 10.2 %collective-permute-start.17 = (bf16[1,2,272,128]{3,2,1,0:T(8,128)(2,1)S(1)}, bf16[1,2,272,128]{3,2,1,0:T(8,128)(2,1)S(1)}, u32[]{:S(2)}, u32[]{:S(2)}) collective-permute-start(bf16[1,2,272,128]{3,2,1,0:T(8,128)(2,1)S(1)} %get-tuple-element.55), channel_id=1, source_target_pairs={{0,128},{8,136},{16,144},{24,152},{32,160},{40,168},{48,176},{56,1... | collective-permute-start | bytes 417800 | tf_op jit(solution)/shard_map/ppermute | solution.py:402
  40.3 9.0 %collective-permute-start.18 = (bf16[1,2,272,128]{3,2,1,0:T(8,128)(2,1)S(1)}, bf16[1,2,272,128]{3,2,1,0:T(8,128)(2,1)S(1)}, u32[]{:S(2)}, u32[]{:S(2)}) collective-permute-start(bf16[1,2,272,128]{3,2,1,0:T(8,128)(2,1)S(1)} %get-tuple-element.56), channel_id=1, source_target_pairs={{0,192},{8,200},{16,208},{24,216},{32,224},{40,232},{48,240},{56,2... | collective-permute-start | bytes 417800 | tf_op jit(solution)/shard_map/ppermute | solution.py:402
  43.8 12.4 %collective-permute-start.13 = (bf16[2,2,272,128]{3,2,1,0:T(8,128)(2,1)S(1)}, bf16[2,2,272,128]{3,2,1,0:T(8,128)(2,1)S(1)}, u32[]{:S(2)}, u32[]{:S(2)}) collective-permute-start(bf16[2,2,272,128]{3,2,1,0:T(8,128)(2,1)S(1)} %get-tuple-element.50), channel_id=1, source_target_pairs={{0,64},{8,72},{16,80},{24,88},{32,96},{40,104},{48,112},{56,120},{... | collective-permute-start | bytes 835592 | tf_op jit(solution)/shard_map/ppermute | solution.py:402
  45.6 13.3 %collective-permute-start.14 = (bf16[2,2,272,128]{3,2,1,0:T(8,128)(2,1)S(1)}, bf16[2,2,272,128]{3,2,1,0:T(8,128)(2,1)S(1)}, u32[]{:S(2)}, u32[]{:S(2)}) collective-permute-start(bf16[2,2,272,128]{3,2,1,0:T(8,128)(2,1)S(1)} %get-tuple-element.51), channel_id=1, source_target_pairs={{0,128},{8,136},{16,144},{24,152},{32,160},{40,168},{48,176},{56,1... | collective-permute-start | bytes 835592 | tf_op jit(solution)/shard_map/ppermute | solution.py:402
  47.8 16.3 %collective-permute-start.15 = (bf16[2,2,272,128]{3,2,1,0:T(8,128)(2,1)S(1)}, bf16[2,2,272,128]{3,2,1,0:T(8,128)(2,1)S(1)}, u32[]{:S(2)}, u32[]{:S(2)}) collective-permute-start(bf16[2,2,272,128]{3,2,1,0:T(8,128)(2,1)S(1)} %get-tuple-element.52), channel_id=1, source_target_pairs={{0,192},{8,200},{16,208},{24,216},{32,224},{40,232},{48,240},{56,2... | collective-permute-start | bytes 835592 | tf_op jit(solution)/shard_map/ppermute | solution.py:402
  50.6 13.5 %collective-permute-start.19 = (bf16[4,272,128]{2,1,0:T(8,128)(2,1)S(1)}, bf16[4,272,128]{2,1,0:T(8,128)(2,1)S(1)}, u32[]{:S(2)}, u32[]{:S(2)}) collective-permute-start(bf16[4,272,128]{2,1,0:T(8,128)(2,1)S(1)} %merge.4), channel_id=1, source_target_pairs={{0,8},{8,16},{16,24},{24,32},{32,40},{40,48},{48,56},{56,0},{64,72... | collective-permute-start | bytes 835592 | tf_op jit(solution)/shard_map/ppermute | solution.py:418
  54.2 15.0 %collective-permute-start.10 = (bf16[2,2,272,128]{3,2,1,0:T(8,128)(2,1)S(1)}, bf16[2,2,272,128]{3,2,1,0:T(8,128)(2,1)S(1)}, u32[]{:S(2)}, u32[]{:S(2)}) collective-permute-start(bf16[2,2,272,128]{3,2,1,0:T(8,128)(2,1)S(1)} %get-tuple-element.45), channel_id=1, source_target_pairs={{0,64},{8,72},{16,80},{24,88},{32,96},{40,104},{48,112},{56,120},{... | collective-permute-start | bytes 835592 | tf_op jit(solution)/shard_map/ppermute | solution.py:402
  56.2 14.0 %collective-permute-start.11 = (bf16[2,2,272,128]{3,2,1,0:T(8,128)(2,1)S(1)}, bf16[2,2,272,128]{3,2,1,0:T(8,128)(2,1)S(1)}, u32[]{:S(2)}, u32[]{:S(2)}) collective-permute-start(bf16[2,2,272,128]{3,2,1,0:T(8,128)(2,1)S(1)} %get-tuple-element.46), channel_id=1, source_target_pairs={{0,128},{8,136},{16,144},{24,152},{32,160},{40,168},{48,176},{56,1... | collective-permute-start | bytes 835592 | tf_op jit(solution)/shard_map/ppermute | solution.py:402
  58.9 13.8 %collective-permute-start.12 = (bf16[2,2,272,128]{3,2,1,0:T(8,128)(2,1)S(1)}, bf16[2,2,272,128]{3,2,1,0:T(8,128)(2,1)S(1)}, u32[]{:S(2)}, u32[]{:S(2)}) collective-permute-start(bf16[2,2,272,128]{3,2,1,0:T(8,128)(2,1)S(1)} %get-tuple-element.47), channel_id=1, source_target_pairs={{0,192},{8,200},{16,208},{24,216},{32,224},{40,232},{48,240},{56,2... | collective-permute-start | bytes 835592 | tf_op jit(solution)/shard_map/ppermute | solution.py:402
  65.6 8.8 %collective-permute-start.20 = (bf16[4,272,128]{2,1,0:T(8,128)(2,1)S(1)}, bf16[4,272,128]{2,1,0:T(8,128)(2,1)S(1)}, u32[]{:S(2)}, u32[]{:S(2)}) collective-permute-start(bf16[4,272,128]{2,1,0:T(8,128)(2,1)S(1)} %get-tuple-element.57), channel_id=1, source_target_pairs={{0,8},{8,16},{16,24},{24,32},{32,40},{40,48},{48,56},{56,0},{64,72... | collective-permute-start | bytes 835592 | tf_op jit(solution)/shard_map/ppermute | solution.py:418
  69.1 8.1 %collective-permute-start.21 = (bf16[4,272,128]{2,1,0:T(8,128)(2,1)S(1)}, bf16[4,272,128]{2,1,0:T(8,128)(2,1)S(1)}, u32[]{:S(2)}, u32[]{:S(2)}) collective-permute-start(bf16[4,272,128]{2,1,0:T(8,128)(2,1)S(1)} %get-tuple-element.58), channel_id=1, source_target_pairs={{0,56},{8,0},{16,8},{24,16},{32,24},{40,32},{48,40},{56,48},{64,12... | collective-permute-start | bytes 835592 | tf_op jit(solution)/shard_map/ppermute | solution.py:418
  69.1 13.0 %collective-permute-start.7 = (bf16[3,2,272,128]{3,2,1,0:T(8,128)(2,1)S(1)}, bf16[3,2,272,128]{3,2,1,0:T(8,128)(2,1)S(1)}, u32[]{:S(2)}, u32[]{:S(2)}) collective-permute-start(bf16[3,2,272,128]{3,2,1,0:T(8,128)(2,1)S(1)} %get-tuple-element.41), channel_id=1, source_target_pairs={{0,64},{8,72},{16,80},{24,88},{32,96},{40,104},{48,112},{56,120},{... | collective-permute-start | bytes 1253384 | tf_op jit(solution)/shard_map/ppermute | solution.py:402
  70.2 13.1 %collective-permute-start.8 = (bf16[3,2,272,128]{3,2,1,0:T(8,128)(2,1)S(1)}, bf16[3,2,272,128]{3,2,1,0:T(8,128)(2,1)S(1)}, u32[]{:S(2)}, u32[]{:S(2)}) collective-permute-start(bf16[3,2,272,128]{3,2,1,0:T(8,128)(2,1)S(1)} %get-tuple-element.42), channel_id=1, source_target_pairs={{0,128},{8,136},{16,144},{24,152},{32,160},{40,168},{48,176},{56,1... | collective-permute-start | bytes 1253384 | tf_op jit(solution)/shard_map/ppermute | solution.py:402
  72.7 14.9 %collective-permute-start.9 = (bf16[3,2,272,128]{3,2,1,0:T(8,128)(2,1)S(1)}, bf16[3,2,272,128]{3,2,1,0:T(8,128)(2,1)S(1)}, u32[]{:S(2)}, u32[]{:S(2)}) collective-permute-start(bf16[3,2,272,128]{3,2,1,0:T(8,128)(2,1)S(1)} %get-tuple-element.43), channel_id=1, source_target_pairs={{0,192},{8,200},{16,208},{24,216},{32,224},{40,232},{48,240},{56,2... | collective-permute-start | bytes 1253384 | tf_op jit(solution)/shard_map/ppermute | solution.py:402
  78.8 8.8 %collective-permute-start.22 = (bf16[4,272,128]{2,1,0:T(8,128)(2,1)S(1)}, bf16[4,272,128]{2,1,0:T(8,128)(2,1)S(1)}, u32[]{:S(2)}, u32[]{:S(2)}) collective-permute-start(bf16[4,272,128]{2,1,0:T(8,128)(2,1)S(1)} %get-tuple-element.59), channel_id=1, source_target_pairs={{0,8},{8,16},{16,24},{24,32},{32,40},{40,48},{48,56},{56,0},{64,72... | collective-permute-start | bytes 835592 | tf_op jit(solution)/shard_map/ppermute | solution.py:418
  80.4 7.2 %collective-permute-start.23 = (bf16[4,272,128]{2,1,0:T(8,128)(2,1)S(1)}, bf16[4,272,128]{2,1,0:T(8,128)(2,1)S(1)}, u32[]{:S(2)}, u32[]{:S(2)}) collective-permute-start(bf16[4,272,128]{2,1,0:T(8,128)(2,1)S(1)} %get-tuple-element.60), channel_id=1, source_target_pairs={{0,56},{8,0},{16,8},{24,16},{32,24},{40,32},{48,40},{56,48},{64,12... | collective-permute-start | bytes 835592 | tf_op jit(solution)/shard_map/ppermute | solution.py:418
  89.2 8.2 %collective-permute-start.24 = (bf16[4,272,128]{2,1,0:T(8,128)(2,1)S(1)}, bf16[4,272,128]{2,1,0:T(8,128)(2,1)S(1)}, u32[]{:S(2)}, u32[]{:S(2)}) collective-permute-start(bf16[4,272,128]{2,1,0:T(8,128)(2,1)S(1)} %get-tuple-element.61), channel_id=1, source_target_pairs={{0,8},{8,16},{16,24},{24,32},{32,40},{40,48},{48,56},{56,0},{64,72... | collective-permute-start | bytes 835592 | tf_op jit(solution)/shard_map/ppermute | solution.py:418
  91.3 6.5 %collective-permute-start.25 = (bf16[4,272,128]{2,1,0:T(8,128)(2,1)S(1)}, bf16[4,272,128]{2,1,0:T(8,128)(2,1)S(1)}, u32[]{:S(2)}, u32[]{:S(2)}) collective-permute-start(bf16[4,272,128]{2,1,0:T(8,128)(2,1)S(1)} %get-tuple-element.62), channel_id=1, source_target_pairs={{0,56},{8,0},{16,8},{24,16},{32,24},{40,32},{48,40},{56,48},{64,12... | collective-permute-start | bytes 835592 | tf_op jit(solution)/shard_map/ppermute | solution.py:418
  (7 other events, 56.5 us)
